TPU v7x, 512 devices: a whole 4x8x8 slice. The times are simulated.
512 devices in a mesh: ctx: 64 (over x, z_lo, y), dp: 8 (over z_hi, core).
Axes of the slice: x: 4, y: 8, z: 8 (z_hi: 4, z_lo: 2; z = z_hi * 2 + z_lo), core: 2. Of those that a mesh axis runs over, the one named last changes fastest.
Arguments:
- queries: bfloat16 [8, 8192, 4096], P('dp', 'ctx'), may hold values from -9 to 9
- keys: bfloat16 [8, 8192, 512], P('dp', 'ctx'), may hold values from -6 to 6
- values: bfloat16 [8, 8192, 512], P('dp', 'ctx'), may hold values from -6 to 6
- output_gradient: bfloat16 [8, 8192, 4096], P('dp', 'ctx'), may hold values from -6 to 6
- adapter_query_down: bfloat16 [8, 8192, 16], P('dp', 'ctx'), may hold values from -0.29882812 to 0.29882812
- adapter_value_down: bfloat16 [8, 8192, 16], P('dp', 'ctx'), may hold values from -0.029907227 to 0.029907227
Outputs:
- query_gradient: bfloat16 [8, 8192, 4096], P('dp', 'ctx')
- key_gradient: bfloat16 [8, 8192, 512], P('dp', 'ctx')
- value_gradient: bfloat16 [8, 8192, 512], P('dp', 'ctx')
- adapter_query_up_gradient: float32 [16, 4096], replicated
- adapter_value_up_gradient: float32 [16, 512], replicated
All inputs are finite; a program needn't handle non-finite values.
Results may differ from a plain program's by a relative error of at most 0.009.
Values may be sent and summed in bfloat16 or wider, within the bound.
No kernel may reach another device: no remote copies, remote signals or barrier semaphores. Data moves between devices by JAX's collectives and lax.ppermute only.
A program may use at most 64 MiB of HBM per device.

v0:
```python
import jax
import jax.numpy as jnp
from jax import lax
from jax.sharding import PartitionSpec as P

QUERY_HEAD_COUNT = 32
KEY_VALUE_HEADS = 4
HEAD_WIDTH = 128
GROUP_DEVS = 4


ADAPTER_SCALE = 2.0


def passed_along(block, axis, distance):
    devices = range(lax.axis_size(axis))
    route = [((i - distance) % len(devices), i) for i in devices]
    return lax.ppermute(block, axis, route)


def head_backward(head_queries, head_grad, head_keys, head_values, allowed):
    softmax_scale = head_queries.shape[-1] ** (-0.5)
    score_matrix = (
        jnp.einsum("rtd,sd->rts", head_queries, head_keys, preferred_element_type=jnp.float32)
        * softmax_scale
    )
    score_matrix = jnp.where(allowed[None], score_matrix, -1e30)
    top = jnp.max(score_matrix, axis=-1, keepdims=True)
    raised = jnp.exp(score_matrix - top)
    probs = raised / jnp.sum(raised, axis=-1, keepdims=True)
    attention_weights = probs.astype(jnp.bfloat16)
    attended_output = jnp.einsum(
        "rts,sd->rtd", attention_weights, head_values, preferred_element_type=jnp.float32
    )
    delta = jnp.sum(head_grad.astype(jnp.float32) * attended_output, axis=-1, keepdims=True)
    score_gradient = jnp.einsum(
        "rtd,sd->rts", head_grad, head_values, preferred_element_type=jnp.float32
    )
    logit_gradient = (probs * (score_gradient - delta)).astype(jnp.bfloat16)
    query_part = (
        jnp.einsum("rts,sd->rtd", logit_gradient, head_keys, preferred_element_type=jnp.float32)
        * softmax_scale
    )
    key_part = (
        jnp.einsum("rts,rtd->sd", logit_gradient, head_queries, preferred_element_type=jnp.float32)
        * softmax_scale
    )
    value_part = jnp.einsum(
        "rts,rtd->sd", attention_weights, head_grad, preferred_element_type=jnp.float32
    )
    return (query_part.astype(jnp.bfloat16), key_part, value_part)


def attend_block(query_heads, grad_heads, key_all, value_all, places):
    rows = query_heads.shape[0]
    column = jnp.arange(key_all.shape[0])
    distance = GROUP_DEVS - 1 - column // rows
    within = column % rows
    query_row = jnp.arange(rows)

    def per_head(inputs):
        head_queries, head_grad, head_keys, head_values, place = inputs
        allowed = (distance[None, :] <= place) & (
            (distance[None, :] > 0) | (within[None, :] <= query_row[:, None])
        )
        return head_backward(head_queries, head_grad, head_keys, head_values, allowed)

    query_part, key_part, value_part = lax.map(
        per_head,
        (
            query_heads.transpose(1, 2, 0, 3),
            grad_heads.transpose(1, 2, 0, 3),
            key_all.transpose(1, 0, 2),
            value_all.transpose(1, 0, 2),
            places,
        ),
    )
    return (
        query_part.transpose(2, 0, 1, 3),
        key_part.transpose(1, 0, 2),
        value_part.transpose(1, 0, 2),
    )


def gather_keys(key_heads, value_heads):
    earlier = [
        passed_along((key_heads, value_heads), "ctx", distance) for distance in range(1, GROUP_DEVS)
    ]
    ordered = earlier[::-1] + [(key_heads, value_heads)]
    key_all = jnp.concatenate([piece[0] for piece in ordered], axis=0)
    value_all = jnp.concatenate([piece[1] for piece in ordered], axis=0)
    return (key_all, value_all)


def return_grads(terms):
    rounded = terms.astype(jnp.bfloat16)
    total = rounded[GROUP_DEVS - 1].astype(jnp.float32)
    for distance in range(1, GROUP_DEVS):
        arrived = passed_along(rounded[GROUP_DEVS - 1 - distance], "ctx", -distance)
        total = total + arrived.astype(jnp.float32)
    return total


def body(queries, keys, values, output_gradient, adapter_query_down, adapter_value_down):
    rows = queries.shape[1]
    per_head = QUERY_HEAD_COUNT // KEY_VALUE_HEADS
    half = KEY_VALUE_HEADS // 2
    query_heads = queries[0].reshape(rows, KEY_VALUE_HEADS, per_head, HEAD_WIDTH)
    grad_heads = output_gradient[0].reshape(rows, KEY_VALUE_HEADS, per_head, HEAD_WIDTH)
    key_heads = keys[0].reshape(rows, KEY_VALUE_HEADS, HEAD_WIDTH)
    value_heads = values[0].reshape(rows, KEY_VALUE_HEADS, HEAD_WIDTH)
    position = lax.axis_index("ctx")
    mine = position % GROUP_DEVS
    rolled_place = (position - GROUP_DEVS // 2) % GROUP_DEVS
    places = jnp.where(jnp.arange(KEY_VALUE_HEADS) < half, mine, rolled_place)
    key_all, value_all = gather_keys(key_heads, value_heads)
    query_part, key_part, value_part = attend_block(
        query_heads, grad_heads, key_all, value_all, places
    )
    terms = jnp.stack(
        [
            key_part.reshape(GROUP_DEVS, rows, KEY_VALUE_HEADS * HEAD_WIDTH),
            value_part.reshape(GROUP_DEVS, rows, KEY_VALUE_HEADS * HEAD_WIDTH),
        ],
        axis=1,
    )
    total = return_grads(terms).astype(jnp.bfloat16)
    query_flattened = query_part.reshape(rows, QUERY_HEAD_COUNT * HEAD_WIDTH)
    key_flattened = total[0]
    value_flattened = total[1]
    query_adapter_term = ADAPTER_SCALE * jnp.dot(
        adapter_query_down[0].T, query_flattened, preferred_element_type=jnp.float32
    )
    value_adapter_term = ADAPTER_SCALE * jnp.dot(
        adapter_value_down[0].T, value_flattened, preferred_element_type=jnp.float32
    )
    adapter_query_up_gradient, adapter_value_up_gradient = lax.psum(
        (query_adapter_term, value_adapter_term), ("ctx", "dp")
    )
    return (
        query_flattened[None],
        key_flattened[None],
        value_flattened[None],
        adapter_query_up_gradient,
        adapter_value_up_gradient,
    )


def solution(mesh):
    in_specs = (
        P("dp", "ctx", None),
        P("dp", "ctx", None),
        P("dp", "ctx", None),
        P("dp", "ctx", None),
        P("dp", "ctx", None),
        P("dp", "ctx", None),
    )
    out_specs = (P("dp", "ctx", None), P("dp", "ctx", None), P("dp", "ctx", None), P(), P())
    return jax.shard_map(body, mesh=mesh, in_specs=in_specs, out_specs=out_specs, check_vma=False)
```

profile of v0, /device:TPU:1, one launch (start us, length us, event | category | flops | bytes accessed | tf_op | source)
XLA Modules:
  0.0 417.2 jit_solution(1145865493346359280)
XLA Ops:
  8.3 6.1 %collective-permute-start = (bf16[128,4,128]{0,2,1:T(8,128)(2,1)S(1)}, bf16[128,4,128]{0,2,1:T(8,128)(2,1)S(1)}, u32[]{:S(2)}, u32[]{:S(2)}) collective-permute-start(bf16[128,4,128]{0,2,1:T(8,128)(2,1)S(1)} %bitcast.184), channel_id=1, source_target_pairs={{488,0},{496,8},{504,16},{0,24},{8,32},{16,40},{24,48},{32,56},{40... | collective-permute-start | bytes 393224 | tf_op jit(solution)/shard_map/ppermute | solution.py:18
  14.4 4.5 %collective-permute-start.1 = (bf16[128,4,128]{0,2,1:T(8,128)(2,1)S(1)}, bf16[128,4,128]{0,2,1:T(8,128)(2,1)}, u32[]{:S(2)}, u32[]{:S(2)}) collective-permute-start(bf16[128,4,128]{0,2,1:T(8,128)(2,1)S(1)} %bitcast.185), channel_id=1, source_target_pairs={{496,0},{504,8},{0,16},{8,24},{16,32},{24,40},{32,48},{40,56},{48,... | collective-permute-start | bytes 393224 | tf_op jit(solution)/shard_map/ppermute | solution.py:18
  18.9 2.3 collective-permute-start.2
  22.3 4.3 %collective-permute-start.3 = (bf16[128,4,128]{0,2,1:T(8,128)(2,1)S(1)}, bf16[128,4,128]{0,2,1:T(8,128)(2,1)S(1)}, u32[]{:S(2)}, u32[]{:S(2)}) collective-permute-start(bf16[128,4,128]{0,2,1:T(8,128)(2,1)S(1)} %bitcast.180), channel_id=1, source_target_pairs={{488,0},{496,8},{504,16},{0,24},{8,32},{16,40},{24,48},{32,56},{40... | collective-permute-start | bytes 393224 | tf_op jit(solution)/shard_map/ppermute | solution.py:18
  26.6 4.2 %collective-permute-start.4 = (bf16[128,4,128]{0,2,1:T(8,128)(2,1)S(1)}, bf16[128,4,128]{0,2,1:T(8,128)(2,1)}, u32[]{:S(2)}, u32[]{:S(2)}) collective-permute-start(bf16[128,4,128]{0,2,1:T(8,128)(2,1)S(1)} %bitcast.181), channel_id=1, source_target_pairs={{496,0},{504,8},{0,16},{8,24},{16,32},{24,40},{32,48},{40,56},{48,... | collective-permute-start | bytes 393224 | tf_op jit(solution)/shard_map/ppermute | solution.py:18
  30.9 4.4 %collective-permute-start.5 = (bf16[128,4,128]{0,2,1:T(8,128)(2,1)S(1)}, bf16[128,4,128]{0,2,1:T(8,128)(2,1)}, u32[]{:S(2)}, u32[]{:S(2)}) collective-permute-start(bf16[128,4,128]{0,2,1:T(8,128)(2,1)S(1)} %bitcast.182), channel_id=1, source_target_pairs={{504,0},{0,8},{8,16},{16,24},{24,32},{32,40},{40,48},{48,56},{56,6... | collective-permute-start | bytes 393224 | tf_op jit(solution)/shard_map/ppermute | solution.py:18
  39.1 9.5 %collective-permute-done.4 = bf16[128,4,128]{0,2,1:T(8,128)(2,1)} collective-permute-done((bf16[128,4,128]{0,2,1:T(8,128)(2,1)S(1)}, bf16[128,4,128]{0,2,1:T(8,128)(2,1)}, u32[]{:S(2)}, u32[]{:S(2)}) %collective-permute-start.4) | collective-permute-done | bytes 131104 | tf_op jit(solution)/shard_map/ppermute | solution.py:18
  48.6 4.9 %collective-permute-done.5 = bf16[128,4,128]{0,2,1:T(8,128)(2,1)} collective-permute-done((bf16[128,4,128]{0,2,1:T(8,128)(2,1)S(1)}, bf16[128,4,128]{0,2,1:T(8,128)(2,1)}, u32[]{:S(2)}, u32[]{:S(2)}) %collective-permute-start.5) | collective-permute-done | bytes 131104 | tf_op jit(solution)/shard_map/ppermute | solution.py:18
  55.5 67.0 %while.16 = (s32[]{:T(128)}, bf16[4,8,128,128]{2,3,1,0:T(8,128)(2,1)}, bf16[4,512,128]{2,1,0:T(8,128)(2,1)}, bf16[4,512,128]{2,1,0:T(8,128)(2,1)}, s32[4]{0:T(12...) while((s32[]{:T(128)}, ...), condition=%wide.region_4.5_spmd.clone.clone, body=%wide.region_0.4_spmd.clone.clone.sunk | while | flops 1084107776 | bytes 25728236 | solution.py:68
  56.9 2.2 fusion.142
  59.3 3.0 fusion.143
  62.4 2.2 multiply_convert_fusion.2
  68.0 3.4 fusion.146
  73.6 2.2 fusion.142
  76.0 3.0 fusion.143
  79.1 2.2 multiply_convert_fusion.2
  84.7 3.4 fusion.146
  90.3 2.2 fusion.142
  92.8 3.0 fusion.143
  95.8 2.2 multiply_convert_fusion.2
  99.3 2.1 fusion.145
  101.5 3.4 fusion.146
  107.1 2.2 fusion.142
  109.5 3.0 fusion.143
  112.6 2.2 multiply_convert_fusion.2
  118.2 3.4 fusion.146
  127.6 3.7 collective-permute-start.7
  131.3 6.5 %collective-permute-start.8 = (bf16[2,128,512]{2,1,0:T(8,128)(2,1)S(1)}, bf16[2,128,512]{2,1,0:T(8,128)(2,1)S(1)}, u32[]{:S(2)}, u32[]{:S(2)}) collective-permute-start(bf16[2,128,512]{2,1,0:T(8,128)(2,1)S(1)} %get-tuple-element.162), channel_id=1, source_target_pairs={{24,0},{32,8},{40,16},{48,24},{56,32},{64,40},{72,48},{80,56},{88,... | collective-permute-start | bytes 786440 | tf_op jit(solution)/shard_map/ppermute | solution.py:18
  140.2 4.3 %collective-permute-done.7 = bf16[2,128,512]{2,1,0:T(8,128)(2,1)S(1)} collective-permute-done((bf16[2,128,512]{2,1,0:T(8,128)(2,1)S(1)}, bf16[2,128,512]{2,1,0:T(8,128)(2,1)S(1)}, u32[]{:S(2)}, u32[]{:S(2)}) %collective-permute-start.7) | collective-permute-done | bytes 262176 | tf_op jit(solution)/shard_map/ppermute | solution.py:18
  144.5 14.1 %collective-permute-done.8 = bf16[2,128,512]{2,1,0:T(8,128)(2,1)S(1)} collective-permute-done((bf16[2,128,512]{2,1,0:T(8,128)(2,1)S(1)}, bf16[2,128,512]{2,1,0:T(8,128)(2,1)S(1)}, u32[]{:S(2)}, u32[]{:S(2)}) %collective-permute-start.8) | collective-permute-done | bytes 262176 | tf_op jit(solution)/shard_map/ppermute | solution.py:18
  159.6 108.8 %psum.15 = f32[16,512]{1,0:T(8,128)} all-reduce(f32[16,512]{1,0:T(8,128)S(1)} %fusion.85), channel_id=1, replica_groups=mesh['ctx'=64,'dp'=8] {'ctx','dp'}, use_global_device_ids=true, to_apply=%region_6.7 | all-reduce | flops 8192 | bytes 65536 | tf_op jit(solution)/shard_map/psum | solution.py:137
  268.4 140.3 %all-reduce.2.cloned.1.call-done = f32[16,4096]{1,0:T(8,128)} async-done(((f32[16,4096]{1,0:T(8,128)}), f32[16,4096]{1,0:T(8,128)}) %all-reduce.2.cloned.1.call-update) | async-done | bytes 262160 | tf_op jit(solution)/shard_map/psum | solution.py:137
  (116 shorter events, 39.1 us)
Async XLA Ops:
  7.2 131.9 %copy-start = (bf16[1,128,16]{1,2,0:T(8,128)(2,1)S(1)}, bf16[1,128,16]{1,2,0:T(8,128)(2,1)}, u32[]{:S(2)}) copy-start(bf16[1,128,16]{1,2,0:T(8,128)(2,1)} %param.12) | copy-start | bytes 12292
  7.2 29.8 %copy-start.4 = (bf16[1,128,4096]{2,1,0:T(8,128)(2,1)S(1)}, bf16[1,128,4096]{2,1,0:T(8,128)(2,1)}, u32[]{:S(2)}) copy-start(bf16[1,128,4096]{2,1,0:T(8,128)(2,1)} %param.11) | copy-start | bytes 3145732
  7.2 401.5 %all-reduce.2.cloned.1.call-start = ((), (), s32[]{:S(2)}) async-start(), calls=%async_computation | async-start | bytes 524288 | tf_op jit(solution)/shard_map/psum | solution.py:137
  8.3 22.5 %collective-permute-start = (bf16[128,4,128]{0,2,1:T(8,128)(2,1)S(1)}, bf16[128,4,128]{0,2,1:T(8,128)(2,1)S(1)}, u32[]{:S(2)}, u32[]{:S(2)}) collective-permute-start(bf16[128,4,128]{0,2,1:T(8,128)(2,1)S(1)} %bitcast.184), channel_id=1, source_target_pairs={{488,0},{496,8},{504,16},{0,24},{8,32},{16,40},{24,48},{32,56},{40... | collective-permute-start | bytes 393224 | tf_op jit(solution)/shard_map/ppermute | solution.py:18
  14.4 23.3 %collective-permute-start.1 = (bf16[128,4,128]{0,2,1:T(8,128)(2,1)S(1)}, bf16[128,4,128]{0,2,1:T(8,128)(2,1)}, u32[]{:S(2)}, u32[]{:S(2)}) collective-permute-start(bf16[128,4,128]{0,2,1:T(8,128)(2,1)S(1)} %bitcast.185), channel_id=1, source_target_pairs={{496,0},{504,8},{0,16},{8,24},{16,32},{24,40},{32,48},{40,56},{48,... | collective-permute-start | bytes 393224 | tf_op jit(solution)/shard_map/ppermute | solution.py:18
  18.9 19.0 %collective-permute-start.2 = (bf16[128,4,128]{0,2,1:T(8,128)(2,1)S(1)}, bf16[128,4,128]{0,2,1:T(8,128)(2,1)}, u32[]{:S(2)}, u32[]{:S(2)}) collective-permute-start(bf16[128,4,128]{0,2,1:T(8,128)(2,1)S(1)} %bitcast.186), channel_id=1, source_target_pairs={{504,0},{0,8},{8,16},{16,24},{24,32},{32,40},{40,48},{48,56},{56,6... | collective-permute-start | bytes 393224 | tf_op jit(solution)/shard_map/ppermute | solution.py:18
  22.3 16.8 %collective-permute-start.3 = (bf16[128,4,128]{0,2,1:T(8,128)(2,1)S(1)}, bf16[128,4,128]{0,2,1:T(8,128)(2,1)S(1)}, u32[]{:S(2)}, u32[]{:S(2)}) collective-permute-start(bf16[128,4,128]{0,2,1:T(8,128)(2,1)S(1)} %bitcast.180), channel_id=1, source_target_pairs={{488,0},{496,8},{504,16},{0,24},{8,32},{16,40},{24,48},{32,56},{40... | collective-permute-start | bytes 393224 | tf_op jit(solution)/shard_map/ppermute | solution.py:18
  26.6 22.0 %collective-permute-start.4 = (bf16[128,4,128]{0,2,1:T(8,128)(2,1)S(1)}, bf16[128,4,128]{0,2,1:T(8,128)(2,1)}, u32[]{:S(2)}, u32[]{:S(2)}) collective-permute-start(bf16[128,4,128]{0,2,1:T(8,128)(2,1)S(1)} %bitcast.181), channel_id=1, source_target_pairs={{496,0},{504,8},{0,16},{8,24},{16,32},{24,40},{32,48},{40,56},{48,... | collective-permute-start | bytes 393224 | tf_op jit(solution)/shard_map/ppermute | solution.py:18
  30.9 4.5 %copy-start.9 = (bf16[128,4,128]{0,2,1:T(8,128)(2,1)}, bf16[128,4,128]{0,2,1:T(8,128)(2,1)S(1)}, u32[]{:S(2)}) copy-start(bf16[128,4,128]{0,2,1:T(8,128)(2,1)S(1)} %collective-permute-done) | copy-start | bytes 393220
  30.9 22.7 %collective-permute-start.5 = (bf16[128,4,128]{0,2,1:T(8,128)(2,1)S(1)}, bf16[128,4,128]{0,2,1:T(8,128)(2,1)}, u32[]{:S(2)}, u32[]{:S(2)}) collective-permute-start(bf16[128,4,128]{0,2,1:T(8,128)(2,1)S(1)} %bitcast.182), channel_id=1, source_target_pairs={{504,0},{0,8},{8,16},{16,24},{24,32},{32,40},{40,48},{48,56},{56,6... | collective-permute-start | bytes 393224 | tf_op jit(solution)/shard_map/ppermute | solution.py:18
  55.5 3.9 copy-start.1
  65.1 2.8 copy-start.5
  68.0 4.2 %copy-start.2 = (bf16[4,8,128,128]{2,3,1,0:T(8,128)(2,1)S(1)}, bf16[4,8,128,128]{2,3,1,0:T(8,128)(2,1)}, u32[]{:S(2)}) copy-start(bf16[4,8,128,128]{2,3,1,0:T(8,128)(2,1)} %copy-done.1) | copy-start | bytes 3145732 | tf_op jit(solution)/shard_map/while
  71.4 0.8 copy-start.6
  72.2 3.8 copy-start.1
  81.9 2.8 copy-start.5
  84.7 4.2 %copy-start.2 = (bf16[4,8,128,128]{2,3,1,0:T(8,128)(2,1)S(1)}, bf16[4,8,128,128]{2,3,1,0:T(8,128)(2,1)}, u32[]{:S(2)}) copy-start(bf16[4,8,128,128]{2,3,1,0:T(8,128)(2,1)} %copy-done.1) | copy-start | bytes 3145732 | tf_op jit(solution)/shard_map/while
  88.1 0.8 copy-start.6
  88.9 3.8 copy-start.1
  98.6 2.9 copy-start.5
  101.5 4.2 %copy-start.2 = (bf16[4,8,128,128]{2,3,1,0:T(8,128)(2,1)S(1)}, bf16[4,8,128,128]{2,3,1,0:T(8,128)(2,1)}, u32[]{:S(2)}) copy-start(bf16[4,8,128,128]{2,3,1,0:T(8,128)(2,1)} %copy-done.1) | copy-start | bytes 3145732 | tf_op jit(solution)/shard_map/while
  104.9 0.8 copy-start.6
  105.7 3.8 copy-start.1
  115.4 2.8 copy-start.5
  118.2 4.2 %copy-start.2 = (bf16[4,8,128,128]{2,3,1,0:T(8,128)(2,1)S(1)}, bf16[4,8,128,128]{2,3,1,0:T(8,128)(2,1)}, u32[]{:S(2)}) copy-start(bf16[4,8,128,128]{2,3,1,0:T(8,128)(2,1)} %copy-done.1) | copy-start | bytes 3145732 | tf_op jit(solution)/shard_map/while
  122.4 1.8 copy-start.7
  124.6 13.2 %copy-start.3 = (bf16[4,8,128,128]{2,3,1,0:T(8,128)(2,1)S(1)}, bf16[4,8,128,128]{2,3,1,0:T(8,128)(2,1)}, u32[]{:S(2)}) copy-start(bf16[4,8,128,128]{2,3,1,0:T(8,128)(2,1)} %get-tuple-element.72) | copy-start | bytes 3145732
  125.6 14.6 %collective-permute-start.6 = (bf16[2,128,512]{2,1,0:T(8,128)(2,1)}, bf16[2,128,512]{2,1,0:T(8,128)(2,1)S(1)}, u32[]{:S(2)}, u32[]{:S(2)}) collective-permute-start(bf16[2,128,512]{2,1,0:T(8,128)(2,1)} %get-tuple-element.161), channel_id=1, source_target_pairs={{8,0},{16,8},{24,16},{32,24},{40,32},{48,40},{56,48},{64,56},{72,6... | collective-permute-start | bytes 786440 | tf_op jit(solution)/shard_map/ppermute | solution.py:18
  127.6 17.0 %collective-permute-start.7 = (bf16[2,128,512]{2,1,0:T(8,128)(2,1)S(1)}, bf16[2,128,512]{2,1,0:T(8,128)(2,1)S(1)}, u32[]{:S(2)}, u32[]{:S(2)}) collective-permute-start(bf16[2,128,512]{2,1,0:T(8,128)(2,1)S(1)} %get-tuple-element.163), channel_id=1, source_target_pairs={{16,0},{24,8},{32,16},{40,24},{48,32},{56,40},{64,48},{72,56},{80,... | collective-permute-start | bytes 786440 | tf_op jit(solution)/shard_map/ppermute | solution.py:18
  131.3 27.4 %collective-permute-start.8 = (bf16[2,128,512]{2,1,0:T(8,128)(2,1)S(1)}, bf16[2,128,512]{2,1,0:T(8,128)(2,1)S(1)}, u32[]{:S(2)}, u32[]{:S(2)}) collective-permute-start(bf16[2,128,512]{2,1,0:T(8,128)(2,1)S(1)} %get-tuple-element.162), channel_id=1, source_target_pairs={{24,0},{32,8},{40,16},{48,24},{56,32},{64,40},{72,48},{80,56},{88,... | collective-permute-start | bytes 786440 | tf_op jit(solution)/shard_map/ppermute | solution.py:18
  139.1 20.4 %copy-start.10 = (bf16[1,128,16]{1,2,0:T(8,128)(2,1)S(1)}, bf16[1,128,16]{1,2,0:T(8,128)(2,1)}, u32[]{:S(2)}) copy-start(bf16[1,128,16]{1,2,0:T(8,128)(2,1)} %param.13) | copy-start | bytes 12292
  159.5 250.9 %copy-start.8 = (bf16[1,128,512]{2,1,0:T(8,128)(2,1)}, bf16[1,128,512]{2,1,0:T(8,128)(2,1)S(1)}, u32[]{:S(2)}) copy-start(bf16[1,128,512]{2,1,0:T(8,128)(2,1)S(1)} %get-tuple-element.261) | copy-start | bytes 393220
  (1 other events, 0.8 us)
Sparse Core Ops, SparseCore 0:
  140.3 268.2 all-reduce.1
where the time goes:
time: 418 us; the launch traced here: 417 us
  waiting for transfers between devices  173 us (41%)
  blocking collectives  109 us (26%)
  matrix products  54.6 us (13%)
  starting transfers between devices  38 us (9%)
  local copies, waits for them, and re-layouts  21.6 us (5%)
  between operations  14.3 us (3%)
  other arithmetic  6.01 us (1%)
    psum x1, waiting for transfers between devices, body(): lax.psum((query_adapter_term, value_adapter_term), ('ctx', 'dp'))  140 us
    psum x1, blocking collectives, body(): lax.psum((query_adapter_term, value_adapter_term), ('ctx', 'dp'))  109 us
    ppermute x9, starting transfers between devices, passed_along(): return lax.ppermute(block, axis, route)  38 us
    ppermute x9, waiting for transfers between devices, passed_along(): return lax.ppermute(block, axis, route)  33.2 us
    dot_general x4, matrix products, head_backward(): jnp.einsum('rts,rtd->sd', attention_weights, head_grad, preferred_element...  13.6 us
    dot_general x4, matrix products, head_backward(): jnp.einsum('rts,sd->rtd', attention_weights, head_values, preferred_eleme...  12.2 us
    sub x4, matrix products, head_backward(): raised = jnp.exp(score_matrix - top)  8.91 us
    dot_general x4, matrix products, head_backward(): jnp.einsum('rtd,sd->rts', head_grad, head_values, preferred_element_type=...  8.63 us
  transfers between devices with their start and end apart: 10, of which 6 were waited for; matrix products, arithmetic and copies ran while one was open for 2% of the time, Pallas kernels for 0%

commit v1 on v0

v1 whole, which is shorter than its diff:
```python
import jax
import jax.numpy as jnp
from jax import lax
from jax.experimental import pallas as pl
from jax.experimental.pallas import tpu as pltpu
from jax.sharding import Mesh, PartitionSpec as P

QUERY_HEAD_COUNT = 32
KEY_VALUE_HEADS = 4
WIDTH = 128
ROWS = 128
RANK = 16
GROUP_DEVS = 4
ADAPTER_SCALE = 2.0
SOFTMAX_SCALE = WIDTH ** (-0.5)
LOG2E = 1.4426950408889634
PER_HEAD = QUERY_HEAD_COUNT // KEY_VALUE_HEADS
HALF_HEADS = QUERY_HEAD_COUNT // 2
UNIT = 4 * ROWS
SEL_ROWS = UNIT + RANK
FULL_ROWS = SEL_ROWS + UNIT
ADAPTER_ROWS = 640
HALF_ADAPTER_ROWS = (HALF_HEADS + 2) * RANK

AXES = ("x", "zl", "yh", "yl", "zh", "core")
SIZES = (4, 2, 4, 2, 4, 2)
CTX = ("x", "zl", "yh", "yl")
DP = ("zh", "core")
NEAR = ("x", "zl", "yl", "core")
FAR = ("yh", "zh")
CTX_SIZE = 64

NT = (((1,), (1,)), ((), ()))
NN = (((1,), (0,)), ((), ()))
bf16 = jnp.bfloat16
f32 = jnp.float32


def dot(a, b, dims):
    return lax.dot_general(a, b, dims, preferred_element_type=f32)


def eye(n):
    return (
        lax.broadcasted_iota(jnp.int32, (n, n), 0) == lax.broadcasted_iota(jnp.int32, (n, n), 1)
    ).astype(bf16)


def transposed_narrow(narrow):
    return dot(eye(RANK), narrow, NT).astype(bf16)


def head_columns(head):
    return pl.ds(pl.multiple_of(head * WIDTH, WIDTH), WIDTH)


def pack_kernel(place_ref, k_ref, v_ref, av_ref, full_ref, sel_ref):
    short = place_ref[0]
    av_t = transposed_narrow(av_ref[...])
    for which, half in ((0, short), (1, 1 - short)):
        base = which * SEL_ROWS
        for part, ref in ((0, k_ref), (1, v_ref)):
            for h in range(2):
                block = ref[:, head_columns(half * 2 + h)]
                rows = pl.ds(base + (part * 2 + h) * ROWS, ROWS)
                full_ref[rows, :] = block
                if which == 0:
                    sel_ref[rows, :] = block
    full_ref[UNIT:SEL_ROWS, :] = av_t
    sel_ref[UNIT:SEL_ROWS, :] = av_t


def attend_head(q_ref, g_ref, keys, values, av_t, aq_t, dq_ref, ad_ref):
    count = len(keys)
    key_all = jnp.concatenate(keys, axis=0) if count > 1 else keys[0]
    value_all = jnp.concatenate(values, axis=0) if count > 1 else values[0]
    key_t = key_all.T
    step = 2
    q_list, g_list, w_list, s_list = [], [], [], []
    allowed = lax.broadcasted_iota(jnp.int32, (ROWS, ROWS), 0) <= lax.broadcasted_iota(
        jnp.int32, (ROWS, ROWS), 1
    )
    allowed = jnp.concatenate([allowed.astype(f32)] * step, axis=1) > 0.5
    for c in range(PER_HEAD // step):
        heads = range(c * step, (c + 1) * step)
        q = jnp.concatenate([q_ref[:, h * WIDTH : (h + 1) * WIDTH] for h in heads], axis=0)
        g = jnp.concatenate([g_ref[:, h * WIDTH : (h + 1) * WIDTH] for h in heads], axis=0)
        scores = dot(key_all, q, NT)
        diagonal = jnp.where(allowed, scores[:ROWS], -1e30)
        scores = jnp.concatenate([diagonal, scores[ROWS:]], axis=0) if count > 1 else diagonal
        top = jnp.max(scores, axis=0, keepdims=True)
        raised = jnp.exp2((scores - top) * (SOFTMAX_SCALE * LOG2E))
        probs = raised * (1.0 / jnp.sum(raised, axis=0, keepdims=True))
        weights = probs.astype(bf16)
        score_grad = dot(value_all, g, NT)
        delta = jnp.sum(probs * score_grad, axis=0, keepdims=True)
        logit_grad = (probs * (score_grad - delta)).astype(bf16)
        dq_t = (dot(key_t, logit_grad, NN) * SOFTMAX_SCALE).astype(bf16)
        for i, h in enumerate(heads):
            part = dq_t[:, i * ROWS : (i + 1) * ROWS]
            dq_ref[:, h * WIDTH : (h + 1) * WIDTH] = part.T
            ad_ref[h * RANK : (h + 1) * RANK, :] = dot(aq_t, part, NT).astype(bf16)
        q_list.append(q)
        g_list.append(g)
        w_list.append(weights)
        s_list.append(logit_grad)
    q_all = jnp.concatenate(q_list, axis=0)
    g_all = jnp.concatenate(g_list, axis=0)
    dk = (dot(jnp.concatenate(s_list, axis=1), q_all, NN) * SOFTMAX_SCALE).astype(bf16)
    dv = dot(jnp.concatenate(w_list, axis=1), g_all, NN).astype(bf16)
    av_all = jnp.concatenate(av_t, axis=1) if count > 1 else av_t[0]
    ad_v = dot(av_all, dv, NN).astype(bf16)
    return dk, dv, ad_v


def block_of(ref, base, g):
    k = ref[pl.ds(pl.multiple_of(base + g * ROWS, 16), ROWS), :]
    v = ref[pl.ds(pl.multiple_of(base + (2 + g) * ROWS, 16), ROWS), :]
    return k, v


def put(ref, base, g, dk, dv):
    ref[pl.ds(pl.multiple_of(base + g * ROWS, 16), ROWS), :] = dk
    ref[pl.ds(pl.multiple_of(base + (2 + g) * ROWS, 16), ROWS), :] = dv


def run_head(blocks, outs, q_ref, g_ref, aq_ref, dq_ref, ad_ref):
    g = pl.program_id(0)
    aq_t = transposed_narrow(aq_ref[...])
    pairs = [block_of(ref, base, g) for ref, base in blocks]
    av_t = [ref[UNIT:SEL_ROWS, :] for ref, _ in blocks]
    dk, dv, ad_v = attend_head(
        q_ref, g_ref, [p[0] for p in pairs], [p[1] for p in pairs], av_t, aq_t, dq_ref, ad_ref
    )
    for n, (ref, base) in enumerate(outs):
        rows = slice(n * ROWS, (n + 1) * ROWS)
        put(ref, base, g, dk[rows], dv[rows])
    return ad_v


def short_kernel(place_ref, q_ref, g_ref, aq_ref, full_ref, one_ref, dq_ref, ad_ref, own_ref, back_ref, adq):
    g = pl.program_id(0)
    odd = place_ref[1]

    def go(blocks, outs):
        ad_v = run_head(blocks, outs, q_ref, g_ref, aq_ref, dq_ref, adq)
        ad_ref[pl.ds(pl.multiple_of(g * PER_HEAD * RANK, 16), PER_HEAD * RANK), :] = adq[...]
        ad_ref[pl.ds(pl.multiple_of(HALF_HEADS * RANK + g * RANK, 16), RANK), :] = ad_v

    @pl.when(odd == 0)
    def _():
        go([(full_ref, 0)], [(own_ref, 0)])

    @pl.when(odd == 1)
    def _():
        go([(full_ref, 0), (one_ref, 0)], [(own_ref, 0), (back_ref, 0)])


def long_kernel(
    place_ref, q_ref, g_ref, aq_ref, full_ref, one_ref, two_ref, three_ref, ads_ref, backs_ref, dq_in,
    dq_ref, ad_ref, own_ref, r1_ref, r2_ref, r3_ref, adq,
):
    g = pl.program_id(0)
    short = place_ref[0]
    odd = place_ref[1]
    long = 1 - short

    @pl.when(g == 0)
    def _():
        ad_ref[QUERY_HEAD_COUNT * RANK + 4 * RANK :, :] = jnp.zeros(
            (ADAPTER_ROWS - (QUERY_HEAD_COUNT + 4) * RANK, WIDTH), bf16
        )
        n = HALF_HEADS * RANK
        ad_ref[pl.ds(pl.multiple_of(short * n, 16), n), :] = ads_ref[:n, :]
        ad_ref[pl.ds(pl.multiple_of(2 * n + short * 2 * RANK, 16), 2 * RANK), :] = ads_ref[n:, :]

    def go(blocks, outs):
        ad_v = run_head(blocks, outs, q_ref, g_ref, aq_ref, dq_ref, adq)
        n = PER_HEAD * RANK
        ad_ref[pl.ds(pl.multiple_of((long * 2 + g) * n, 16), n), :] = adq[...]
        ad_ref[pl.ds(pl.multiple_of(QUERY_HEAD_COUNT * RANK + (long * 2 + g) * RANK, 16), RANK), :] = ad_v

    @pl.when(odd == 0)
    def _():
        go(
            [(full_ref, SEL_ROWS), (one_ref, 0), (two_ref, 0)],
            [(own_ref, 0), (r1_ref, 0), (r2_ref, 0)],
        )

    @pl.when(odd == 1)
    def _():
        go(
            [(full_ref, SEL_ROWS), (one_ref, SEL_ROWS), (two_ref, 0), (three_ref, 0)],
            [(own_ref, 0), (r1_ref, UNIT), (r2_ref, 0), (r3_ref, 0)],
        )

    @pl.when((g == 0) & (odd == 0))
    def _():
        r1_ref[UNIT:, :] = jnp.zeros((UNIT, WIDTH), bf16)

    @pl.when((g == 0) & (odd == 1))
    def _():
        r1_ref[:UNIT, :] = backs_ref[...]


def finish_kernel(place_ref, sum_ref, short_ref, long_ref, r1_ref, r2_ref, r3_ref, dk_ref, dv_ref, aq_ref, av_ref):
    short = place_ref[0]
    even = place_ref[1] == 0
    for part, ref in ((0, dk_ref), (1, dv_ref)):
        for h in range(2):
            base = (part * 2 + h) * ROWS
            rows = slice(base, base + ROWS)
            total = short_ref[rows, :].astype(f32) + r1_ref[rows, :].astype(f32)
            total = total + r2_ref[rows, :].astype(f32)
            total = total + jnp.where(even, r3_ref[rows, :].astype(f32), 0.0)
            ref[:, head_columns(short * 2 + h)] = total.astype(bf16)
            other = r1_ref[UNIT + base : UNIT + base + ROWS, :].astype(f32)
            total = long_ref[rows, :].astype(f32) + jnp.where(even, other, 0.0)
            ref[:, head_columns((1 - short) * 2 + h)] = total.astype(bf16)
    for h in range(QUERY_HEAD_COUNT):
        aq_ref[:, h * WIDTH : (h + 1) * WIDTH] = (
            sum_ref[h * RANK : (h + 1) * RANK, :].astype(f32) * ADAPTER_SCALE
        )
    for h in range(KEY_VALUE_HEADS):
        base = (QUERY_HEAD_COUNT + h) * RANK
        av_ref[:, h * WIDTH : (h + 1) * WIDTH] = sum_ref[base : base + RANK, :].astype(f32) * ADAPTER_SCALE


def shape(dims, kind=bf16):
    return jax.ShapeDtypeStruct(dims, kind)


def whole(dims):
    return pl.BlockSpec(dims, lambda *_: (0,) * len(dims))


def passed_along(block, distance, senders=range(CTX_SIZE)):
    return lax.ppermute(block, CTX, [(i, (i + distance) % CTX_SIZE) for i in senders])


PARAMS = pltpu.CompilerParams(vmem_limit_bytes=48 * 1024 * 1024)


def pack(place, k, v, av):
    return pl.pallas_call(
        pack_kernel,
        grid_spec=pltpu.PrefetchScalarGridSpec(
            num_scalar_prefetch=1,
            grid=(1,),
            in_specs=[whole(k.shape), whole(v.shape), whole(av.shape)],
            out_specs=[whole((FULL_ROWS, WIDTH)), whole((SEL_ROWS, WIDTH))],
        ),
        out_shape=[shape((FULL_ROWS, WIDTH)), shape((SEL_ROWS, WIDTH))],
        compiler_params=PARAMS,
        name="pack",
    )(place, k, v, av)


HEAD_COLUMNS = PER_HEAD * WIDTH


def attend_short(place, q, grad, aq, full, one):
    half = pl.BlockSpec((ROWS, HEAD_COLUMNS), lambda g, place: (0, place[0] * 2 + g))
    return pl.pallas_call(
        short_kernel,
        grid_spec=pltpu.PrefetchScalarGridSpec(
            num_scalar_prefetch=1,
            grid=(2,),
            in_specs=[half, half, whole(aq.shape), whole(full.shape), whole(one.shape)],
            out_specs=[half, whole((HALF_ADAPTER_ROWS, WIDTH)), whole((UNIT, WIDTH)), whole((UNIT, WIDTH))],
            scratch_shapes=[pltpu.VMEM((PER_HEAD * RANK, WIDTH), bf16)],
        ),
        out_shape=[
            shape(q.shape),
            shape((HALF_ADAPTER_ROWS, WIDTH)),
            shape((UNIT, WIDTH)),
            shape((UNIT, WIDTH)),
        ],
        compiler_params=PARAMS,
        cost_estimate=pl.CostEstimate(flops=700_000_000, bytes_accessed=3_000_000, transcendentals=0),
        name="short",
    )(place, q, grad, aq, full, one)


def attend_long(place, q, grad, aq, full, one, two, three, ads, backs, dq):
    half = pl.BlockSpec((ROWS, HEAD_COLUMNS), lambda g, place: (0, (1 - place[0]) * 2 + g))
    return pl.pallas_call(
        long_kernel,
        grid_spec=pltpu.PrefetchScalarGridSpec(
            num_scalar_prefetch=1,
            grid=(2,),
            in_specs=[half, half]
            + [whole(a.shape) for a in (aq, full, one, two, three, ads, backs)]
            + [pl.BlockSpec(memory_space=pl.ANY)],
            out_specs=[
                half,
                whole((ADAPTER_ROWS, WIDTH)),
                whole((UNIT, WIDTH)),
                whole((2 * UNIT, WIDTH)),
                whole((UNIT, WIDTH)),
                whole((UNIT, WIDTH)),
            ],
            scratch_shapes=[pltpu.VMEM((PER_HEAD * RANK, WIDTH), bf16)],
        ),
        out_shape=[
            shape(q.shape),
            shape((ADAPTER_ROWS, WIDTH)),
            shape((UNIT, WIDTH)),
            shape((2 * UNIT, WIDTH)),
            shape((UNIT, WIDTH)),
            shape((UNIT, WIDTH)),
        ],
        input_output_aliases={10: 0},
        compiler_params=PARAMS,
        cost_estimate=pl.CostEstimate(flops=1_400_000_000, bytes_accessed=4_000_000, transcendentals=0),
        name="long",
    )(place, q, grad, aq, full, one, two, three, ads, backs, dq)


def finish(place, total, short, long, r1, r2, r3):
    operands = (total, short, long, r1, r2, r3)
    outs = [
        shape((ROWS, KEY_VALUE_HEADS * WIDTH)),
        shape((ROWS, KEY_VALUE_HEADS * WIDTH)),
        shape((RANK, QUERY_HEAD_COUNT * WIDTH), f32),
        shape((RANK, KEY_VALUE_HEADS * WIDTH), f32),
    ]
    return pl.pallas_call(
        finish_kernel,
        grid_spec=pltpu.PrefetchScalarGridSpec(
            num_scalar_prefetch=1,
            grid=(1,),
            in_specs=[whole(a.shape) for a in operands],
            out_specs=[whole(o.shape) for o in outs],
        ),
        out_shape=outs,
        compiler_params=PARAMS,
        name="finish",
    )(place, *operands)


def copies_to_all(block, axes):
    size = lax.axis_size(axes)
    return lax.all_to_all(jnp.broadcast_to(block[None], (size,) + block.shape), axes, 0, 0)


def summed(pieces):
    return jnp.sum(pieces.astype(f32), axis=0).astype(bf16)


def sum_over_all(part):
    size = lax.axis_size(NEAR)
    mine = summed(lax.all_to_all(part.reshape(size, part.shape[0] // size, WIDTH), NEAR, 0, 0))
    mine = summed(copies_to_all(mine, FAR))
    return copies_to_all(mine, NEAR).reshape(part.shape)


def body(queries, keys, values, output_gradient, adapter_query_down, adapter_value_down):
    position = lax.axis_index(CTX) % GROUP_DEVS
    place = jnp.stack([position // 2, position % 2]).astype(jnp.int32)
    q, grad, aq = queries[0], output_gradient[0], adapter_query_down[0]
    full, sel = pack(place, keys[0], values[0], adapter_value_down[0])
    one = passed_along(full, 1)
    two = passed_along(sel, 2)
    three = passed_along(sel, 3, range(0, CTX_SIZE, 2))
    dq, ads, own_short, backs = attend_short(place, q, grad, aq, full, one)
    dq, part, own_long, r1, r2, r3 = attend_long(
        place, q, grad, aq, full, one, two, three, ads, backs, dq
    )
    r1 = passed_along(r1, -1)
    r2 = passed_along(r2, -2)
    r3 = passed_along(r3, -3, range(1, CTX_SIZE, 2))
    total = sum_over_all(part)
    dk, dv, adapter_q, adapter_v = finish(place, total, own_short, own_long, r1, r2, r3)
    return dq[None], dk[None], dv[None], adapter_q, adapter_v


def solution(mesh):
    split = Mesh(mesh.devices.reshape(SIZES), AXES)
    tokens = P(DP, CTX, None)
    return jax.shard_map(
        body,
        mesh=split,
        in_specs=(tokens,) * 6,
        out_specs=(tokens, tokens, tokens, P(), P()),
        check_vma=False,
    )
```

time: 418 us -> 105 us (0.25)
  waiting for transfers between devices: 173 us -> 17 us
  blocking collectives: 109 us -> 37.5 us
  matrix products: 54.6 us -> 0 us
  local copies, waits for them, and re-layouts: 21.6 us -> 5.11 us
  Pallas kernels: 0 us -> 15.3 us
  between operations: 14.3 us -> 0.79 us
  starting transfers between devices: 38 us -> 27.9 us
  other arithmetic: 6.01 us -> 0.15 us
    psum x1 -> x0, waiting for transfers between devices: 140 us -> none  [body(): lax.psum((query_adapter_term, value_adapter_term), ('ctx', 'dp'))]
    psum x1 -> x0, blocking collectives: 109 us -> none  [body(): lax.psum((query_adapter_term, value_adapter_term), ('ctx', 'dp'))]
    dot_general x22 -> x0, matrix products: 45.7 us -> none  [the longest x4 13.6 us: head_backward(): jnp.einsum('rts,rtd->sd', attention_weights, head_grad, preferred_element...]
    all_to_all x0 -> x2, blocking collectives: none -> 37.5 us  [the longest x1 25.2 us: copies_to_all(): lax.all_to_all(jnp.broadcast_to(block[None], (size,) + block.shape), axes...]
    ppermute x9 -> x6, waiting for transfers between devices: 33.2 us -> 17 us  [passed_along(): lax.ppermute(block, CTX, [(i, (i + distance) % CTX_SIZE) for i in senders])]
    ppermute x9 -> x6, starting transfers between devices: 38 us -> 22.6 us  [passed_along(): lax.ppermute(block, CTX, [(i, (i + distance) % CTX_SIZE) for i in senders])]
    pallas_call x0 -> x4, Pallas kernels: none -> 15.3 us  [the longest x1 7.4 us: attend_long(): pl.pallas_call(long_kernel, grid_spec=pltpu.PrefetchScalarGridSpec(num_sc...]
    sub x4 -> x0, matrix products: 8.91 us -> none  [head_backward(): raised = jnp.exp(score_matrix - top)]
  transfers between devices with their start and end apart: 10 -> 7, of which waited for: 6 -> 4; matrix products, arithmetic and copies ran while one was open for 2% -> 0% of each run, Pallas kernels for 0% -> 6%
where the time goes in v1:
time: 105 us; the launch traced here: 104 us
  blocking collectives  37.5 us (36%)
  starting transfers between devices  27.9 us (27%)
  waiting for transfers between devices  17 us (16%)
  Pallas kernels  15.3 us (15%)
  local copies, waits for them, and re-layouts  5.11 us (5%)
    all_to_all x1, blocking collectives, copies_to_all(): lax.all_to_all(jnp.broadcast_to(block[None], (size,) + block.shape), axes...  25.2 us
    ppermute x6, starting transfers between devices, passed_along(): lax.ppermute(block, CTX, [(i, (i + distance) % CTX_SIZE) for i in senders])  22.6 us
    ppermute x6, waiting for transfers between devices, passed_along(): lax.ppermute(block, CTX, [(i, (i + distance) % CTX_SIZE) for i in senders])  17 us
    all_to_all x1, blocking collectives, sum_over_all(): lax.all_to_all(part.reshape(size, part.shape[0] // size, WIDTH), NEAR, 0, 0)  12.3 us
    pallas_call x1, Pallas kernels, attend_long(): pl.pallas_call(long_kernel, grid_spec=pltpu.PrefetchScalarGridSpec(num_sc...  7.4 us
    pallas_call x1, Pallas kernels, attend_short(): pl.pallas_call(short_kernel, grid_spec=pltpu.PrefetchScalarGridSpec(num_s...  5.72 us
    all_to_all x1, starting transfers between devices, copies_to_all(): lax.all_to_all(jnp.broadcast_to(block[None], (size,) + block.shape), axes...  5.29 us
    unnamed x12, local copies, waits for them, and re-layouts  4.32 us
  transfers between devices with their start and end apart: 7, of which 4 were waited for; matrix products, arithmetic and copies ran while one was open for 0% of the time, Pallas kernels for 6%

profile of v1, /device:TPU:1, one launch (start us, length us, event | category | flops | bytes accessed | tf_op | source)
XLA Modules:
  0.0 103.6 jit_solution(15787559021134056789)
XLA Ops:
  0.6 0.0 copy-start.2
  0.7 0.8 copy.19
  1.5 0.1 pad_add_fusion.place_ref
  1.6 0.0 copy-done.2
  1.6 0.0 copy-start.3
  1.6 0.9 copy-done.3
  2.5 0.0 copy-start.4
  2.5 0.7 pack.1
  3.2 4.0 %collective-permute-start = (bf16[1040,128]{1,0:T(8,128)(2,1)S(1)}, bf16[1040,128]{1,0:T(8,128)(2,1)S(1)}, u32[]{:S(2)}, u32[]{:S(2)}) collective-permute-start(bf16[1040,128]{1,0:T(8,128)(2,1)S(1)} %get-tuple-element.21.full_ref), channel_id=1, source_target_pairs={{0,8},{8,16},{16,24},{24,32},{32,40},{40,48},{48,56},{56,64},{64,7... | collective-permute-start | bytes 798728 | tf_op jit(solution)/shard_map/ppermute | solution.py:238
  7.2 6.4 %collective-permute-start.2 = (bf16[528,128]{1,0:T(8,128)(2,1)S(1)}, bf16[528,128]{1,0:T(8,128)(2,1)S(1)}, u32[]{:S(2)}, u32[]{:S(2)}) collective-permute-start(bf16[528,128]{1,0:T(8,128)(2,1)S(1)} %get-tuple-element.22), channel_id=1, source_target_pairs={{0,24},{16,40},{32,56},{48,72},{64,88},{80,104},{96,120},{112,136}... | collective-permute-start | bytes 405512 | tf_op jit(solution)/shard_map/ppermute | solution.py:238
  13.7 2.4 %collective-permute-start.1 = (bf16[528,128]{1,0:T(8,128)(2,1)S(1)}, bf16[528,128]{1,0:T(8,128)(2,1)S(1)}, u32[]{:S(2)}, u32[]{:S(2)}) collective-permute-start(bf16[528,128]{1,0:T(8,128)(2,1)S(1)} %get-tuple-element.22), channel_id=1, source_target_pairs={{0,16},{8,24},{16,32},{24,40},{32,48},{40,56},{48,64},{56,72},{64,... | collective-permute-start | bytes 405512 | tf_op jit(solution)/shard_map/ppermute | solution.py:238
  16.1 0.0 copy-done.4
  16.1 0.1 copy.18
  16.2 0.7 collective-permute-done.one_ref
  16.9 1.2 %copy-done = bf16[1,128,4096]{2,1,0:T(8,128)(2,1)S(1)} copy-done((bf16[1,128,4096]{2,1,0:T(8,128)(2,1)S(1)}, bf16[1,128,4096]{2,1,0:T(8,128)(2,1)}, u32[]{:S(2)}) %copy-start) | copy-done | bytes 1048600
  18.1 1.2 %copy-done.1 = bf16[1,128,4096]{2,1,0:T(8,128)(2,1)S(1)} copy-done((bf16[1,128,4096]{2,1,0:T(8,128)(2,1)S(1)}, bf16[1,128,4096]{2,1,0:T(8,128)(2,1)}, u32[]{:S(2)}) %copy-start.1) | copy-done | bytes 1048600
  19.4 5.7 %short.1 = (bf16[128,4096]{1,0:T(8,128)(2,1)}, bf16[288,128]{1,0:T(8,128)(2,1)S(1)}, bf16[512,128]{1,0:T(8,128)(2,1)S(1)}, bf16[512,128]{1,0:T(8,128)(2,1)S(1)}) custom-call(s32[2]{0:T(128)S(1)} %pad_add_fusion.place_ref, bf16[128,4096]{1,0:T(8,128)(2,1)S(1)} %bitcast.11, bf16[128,4096]{1,0:T(8,128)(2,1)S(1)} %bitcast.13, bf16[128,16]{1,0:T(8,128)(2,1)S(1)} %bitcast.15, ...), custom_call_target="tpu_custom_call" | custom-call | flops 700000000 | bytes 3000000 | tf_op jit(solution)/shard_map/short/pallas_call | solution.py:264
  25.1 0.0 collective-permute-done.2.three_ref
  25.1 6.4 %collective-permute-done.1.two_ref = bf16[528,128]{1,0:T(8,128)(2,1)S(1)} collective-permute-done((bf16[528,128]{1,0:T(8,128)(2,1)S(1)}, bf16[528,128]{1,0:T(8,128)(2,1)S(1)}, u32[]{:S(2)}, u32[]{:S(2)}) %collective-permute-start.1) | collective-permute-done | bytes 135200 | tf_op jit(solution)/shard_map/ppermute | solution.py:238
  31.5 7.4 %long.1 = (bf16[128,4096]{1,0:T(8,128)(2,1)}, bf16[640,128]{1,0:T(8,128)(2,1)S(1)}, bf16[512,128]{1,0:T(8,128)(2,1)S(1)}, bf16[1024,128]{1,0:T(8,128)(2,1)S(1)},...) custom-call(s32[2]{0:T(128)S(1)} %pad_add_fusion.place_ref, ...), custom_call_target="tpu_custom_call", output_to_operand_aliasing={{0}: (10, {})} | custom-call | flops 1400000000 | bytes 4000000 | tf_op jit(solution)/shard_map/long/pallas_call | solution.py:287
  39.0 12.3 %all_to_all.15 = bf16[32,20,128]{2,1,0:T(8,128)(2,1)S(1)} all-to-all(bf16[32,20,128]{2,1,0:T(8,128)(2,1)S(1)} %reshape.18), channel_id=1, replica_groups=mesh['x'=4,'zl'=2,'yh'=4,'yl'=2,'zh'=4,'core'=2] {'x','zl','yl','core'}, dimensions={0} | all-to-all | bytes 327680 | tf_op jit(solution)/shard_map/all_to_all | solution.py:353
  51.3 25.2 %all_to_all.16 = bf16[16,20,128]{2,1,0:T(8,128)(2,1)S(1)} all-to-all(bf16[16,20,128]{2,1,0:T(8,128)(2,1)S(1)} %broadcast_in_dim.22), channel_id=1, replica_groups=mesh['x'=4,'zl'=2,'yh'=4,'yl'=2,'zh'=4,'core'=2] {'yh','zh'}, dimensions={0} | all-to-all | bytes 163840 | tf_op jit(solution)/shard_map/all_to_all | solution.py:344
  76.5 0.7 broadcast_in_dim.23
  77.2 5.3 %all-to-all-start.2 = ((bf16[32,20,128]{2,1,0:T(8,128)(2,1)}), bf16[32,20,128]{2,1,0:T(8,128)(2,1)S(1)}, u32[]{:S(2)}, u32[]{:S(2)}) async-start(bf16[32,20,128]{2,1,0:T(8,128)(2,1)} %broadcast_in_dim.23), calls=%async_computation.2 | async-start | bytes 393216 | tf_op jit(solution)/shard_map/all_to_all | solution.py:344
  82.5 6.2 %collective-permute-start.3 = (bf16[1024,128]{1,0:T(8,128)(2,1)S(1)}, bf16[1024,128]{1,0:T(8,128)(2,1)S(1)}, u32[]{:S(2)}, u32[]{:S(2)}) collective-permute-start(bf16[1024,128]{1,0:T(8,128)(2,1)S(1)} %get-tuple-element.30), channel_id=1, source_target_pairs={{0,504},{8,0},{16,8},{24,16},{32,24},{40,32},{48,40},{56,48},{64,5... | collective-permute-start | bytes 786440 | tf_op jit(solution)/shard_map/ppermute | solution.py:238
  88.7 2.2 %collective-permute-start.4 = (bf16[512,128]{1,0:T(8,128)(2,1)S(1)}, bf16[512,128]{1,0:T(8,128)(2,1)S(1)}, u32[]{:S(2)}, u32[]{:S(2)}) collective-permute-start(bf16[512,128]{1,0:T(8,128)(2,1)S(1)} %get-tuple-element.31), channel_id=1, source_target_pairs={{0,496},{8,504},{16,0},{24,8},{32,16},{40,24},{48,32},{56,40},{64,... | collective-permute-start | bytes 393224 | tf_op jit(solution)/shard_map/ppermute | solution.py:238
  90.9 1.3 %collective-permute-start.5 = (bf16[512,128]{1,0:T(8,128)(2,1)S(1)}, bf16[512,128]{1,0:T(8,128)(2,1)S(1)}, u32[]{:S(2)}, u32[]{:S(2)}) collective-permute-start(bf16[512,128]{1,0:T(8,128)(2,1)S(1)} %get-tuple-element.32), channel_id=1, source_target_pairs={{8,496},{24,0},{40,16},{56,32},{72,48},{88,64},{104,80},{120,96},{... | collective-permute-start | bytes 393224 | tf_op jit(solution)/shard_map/ppermute | solution.py:238
  92.2 0.0 all-to-all-done.2
  92.3 7.5 %collective-permute-done.4.r2_ref = bf16[512,128]{1,0:T(8,128)(2,1)S(1)} collective-permute-done((bf16[512,128]{1,0:T(8,128)(2,1)S(1)}, bf16[512,128]{1,0:T(8,128)(2,1)S(1)}, u32[]{:S(2)}, u32[]{:S(2)}) %collective-permute-start.4) | collective-permute-done | bytes 131104 | tf_op jit(solution)/shard_map/ppermute | solution.py:238
  99.8 2.4 %collective-permute-done.5.r3_ref = bf16[512,128]{1,0:T(8,128)(2,1)S(1)} collective-permute-done((bf16[512,128]{1,0:T(8,128)(2,1)S(1)}, bf16[512,128]{1,0:T(8,128)(2,1)S(1)}, u32[]{:S(2)}, u32[]{:S(2)}) %collective-permute-start.5) | collective-permute-done | bytes 131104 | tf_op jit(solution)/shard_map/ppermute | solution.py:238
  102.2 0.0 collective-permute-done.3.r1_ref
  102.2 1.4 %finish.1 = (bf16[128,512]{1,0:T(8,128)(2,1)}, bf16[128,512]{1,0:T(8,128)(2,1)}, f32[16,4096]{1,0:T(8,128)}, f32[16,512]{1,0:T(8,128)}) custom-call(s32[2]{0:T(128)S(1)} %pad_add_fusion.place_ref, bf16[640,128]{1,0:T(8,128)(2,1)S(1)} %reshape.19.sum_ref, bf16[512,128]{1,0:T(8,128)(2,1)S(1)} %get-tuple-element.28.short_ref, ...), custom_call_target="tpu_custom_call" | custom-call | tf_op jit(solution)/shard_map/finish/pallas_call | solution.py:328
  (7 shorter events, 0.2 us)
Async XLA Ops:
  0.6 1.0 copy-start.2
  1.6 0.9 copy-start.3
  2.5 13.6 %copy-start.4 = (bf16[1,128,16]{1,2,0:T(8,128)(2,1)S(1)}, bf16[1,128,16]{1,2,0:T(8,128)(2,1)}, u32[]{:S(2)}) copy-start(bf16[1,128,16]{1,2,0:T(8,128)(2,1)} %param.10) | copy-start | bytes 12292
  3.2 13.7 %collective-permute-start = (bf16[1040,128]{1,0:T(8,128)(2,1)S(1)}, bf16[1040,128]{1,0:T(8,128)(2,1)S(1)}, u32[]{:S(2)}, u32[]{:S(2)}) collective-permute-start(bf16[1040,128]{1,0:T(8,128)(2,1)S(1)} %get-tuple-element.21.full_ref), channel_id=1, source_target_pairs={{0,8},{8,16},{16,24},{24,32},{32,40},{40,48},{48,56},{56,64},{64,7... | collective-permute-start | bytes 798728 | tf_op jit(solution)/shard_map/ppermute | solution.py:238
  7.2 17.9 %collective-permute-start.2 = (bf16[528,128]{1,0:T(8,128)(2,1)S(1)}, bf16[528,128]{1,0:T(8,128)(2,1)S(1)}, u32[]{:S(2)}, u32[]{:S(2)}) collective-permute-start(bf16[528,128]{1,0:T(8,128)(2,1)S(1)} %get-tuple-element.22), channel_id=1, source_target_pairs={{0,24},{16,40},{32,56},{48,72},{64,88},{80,104},{96,120},{112,136}... | collective-permute-start | bytes 405512 | tf_op jit(solution)/shard_map/ppermute | solution.py:238
  13.7 17.8 %collective-permute-start.1 = (bf16[528,128]{1,0:T(8,128)(2,1)S(1)}, bf16[528,128]{1,0:T(8,128)(2,1)S(1)}, u32[]{:S(2)}, u32[]{:S(2)}) collective-permute-start(bf16[528,128]{1,0:T(8,128)(2,1)S(1)} %get-tuple-element.22), channel_id=1, source_target_pairs={{0,16},{8,24},{16,32},{24,40},{32,48},{40,56},{48,64},{56,72},{64,... | collective-permute-start | bytes 405512 | tf_op jit(solution)/shard_map/ppermute | solution.py:238
  16.9 1.2 %copy-start = (bf16[1,128,4096]{2,1,0:T(8,128)(2,1)S(1)}, bf16[1,128,4096]{2,1,0:T(8,128)(2,1)}, u32[]{:S(2)}) copy-start(bf16[1,128,4096]{2,1,0:T(8,128)(2,1)} %param.6) | copy-start | bytes 3145732
  18.1 1.2 %copy-start.1 = (bf16[1,128,4096]{2,1,0:T(8,128)(2,1)S(1)}, bf16[1,128,4096]{2,1,0:T(8,128)(2,1)}, u32[]{:S(2)}) copy-start(bf16[1,128,4096]{2,1,0:T(8,128)(2,1)} %param.9) | copy-start | bytes 3145732
  77.2 15.0 %all-to-all-start.2 = ((bf16[32,20,128]{2,1,0:T(8,128)(2,1)}), bf16[32,20,128]{2,1,0:T(8,128)(2,1)S(1)}, u32[]{:S(2)}, u32[]{:S(2)}) async-start(bf16[32,20,128]{2,1,0:T(8,128)(2,1)} %broadcast_in_dim.23), calls=%async_computation.2 | async-start | bytes 393216 | tf_op jit(solution)/shard_map/all_to_all | solution.py:344
  82.5 19.7 %collective-permute-start.3 = (bf16[1024,128]{1,0:T(8,128)(2,1)S(1)}, bf16[1024,128]{1,0:T(8,128)(2,1)S(1)}, u32[]{:S(2)}, u32[]{:S(2)}) collective-permute-start(bf16[1024,128]{1,0:T(8,128)(2,1)S(1)} %get-tuple-element.30), channel_id=1, source_target_pairs={{0,504},{8,0},{16,8},{24,16},{32,24},{40,32},{48,40},{56,48},{64,5... | collective-permute-start | bytes 786440 | tf_op jit(solution)/shard_map/ppermute | solution.py:238
  88.7 11.1 %collective-permute-start.4 = (bf16[512,128]{1,0:T(8,128)(2,1)S(1)}, bf16[512,128]{1,0:T(8,128)(2,1)S(1)}, u32[]{:S(2)}, u32[]{:S(2)}) collective-permute-start(bf16[512,128]{1,0:T(8,128)(2,1)S(1)} %get-tuple-element.31), channel_id=1, source_target_pairs={{0,496},{8,504},{16,0},{24,8},{32,16},{40,24},{48,32},{56,40},{64,... | collective-permute-start | bytes 393224 | tf_op jit(solution)/shard_map/ppermute | solution.py:238
  90.9 11.3 %collective-permute-start.5 = (bf16[512,128]{1,0:T(8,128)(2,1)S(1)}, bf16[512,128]{1,0:T(8,128)(2,1)S(1)}, u32[]{:S(2)}, u32[]{:S(2)}) collective-permute-start(bf16[512,128]{1,0:T(8,128)(2,1)S(1)} %get-tuple-element.32), channel_id=1, source_target_pairs={{8,496},{24,0},{40,16},{56,32},{72,48},{88,64},{104,80},{120,96},{... | collective-permute-start | bytes 393224 | tf_op jit(solution)/shard_map/ppermute | solution.py:238

commit v2 on v1

v2 whole, which is shorter than its diff:
```python
import jax
import jax.numpy as jnp
from jax import lax
from jax.experimental import pallas as pl
from jax.experimental.pallas import tpu as pltpu
from jax.sharding import Mesh, PartitionSpec as P

QUERY_HEAD_COUNT = 32
KEY_VALUE_HEADS = 4
WIDTH = 128
ROWS = 128
RANK = 16
GROUP_DEVS = 4
ADAPTER_SCALE = 2.0
SOFTMAX_SCALE = WIDTH ** (-0.5)
LOG2E = 1.4426950408889634
STEP = 8
PER_HEAD = QUERY_HEAD_COUNT // KEY_VALUE_HEADS
HALF_HEADS = QUERY_HEAD_COUNT // 2
UNIT = 4 * ROWS
SEL_ROWS = UNIT + RANK
ADAPTER_ROWS = 640
HALF_ADAPTER_ROWS = (HALF_HEADS + 2) * RANK

AXES = ("x", "zl", "yh", "yl", "zh", "core")
SIZES = (4, 2, 4, 2, 4, 2)
CTX = ("x", "zl", "yh", "yl")
DP = ("zh", "core")
NEAR = ("x", "zl", "yl", "core")
FAR = ("yh", "zh")
CTX_SIZE = 64

NT = (((1,), (1,)), ((), ()))
NN = (((1,), (0,)), ((), ()))
bf16 = jnp.bfloat16
f32 = jnp.float32


def dot(a, b, dims):
    return lax.dot_general(a, b, dims, preferred_element_type=f32)


def head_columns(head):
    return pl.ds(pl.multiple_of(head * WIDTH, WIDTH), WIDTH)


def pack_kernel(place_ref, k_ref, v_ref, av_ref, sel_ref, oth_ref, sems):
    short = place_ref[0]
    copies = []

    def start(src, dst):
        copy = pltpu.make_async_copy(src, dst, sems.at[len(copies)])
        copy.start()
        copies.append(copy)

    for half, packed in ((short, sel_ref), (1 - short, oth_ref)):
        for part, ref in ((0, k_ref), (1, v_ref)):
            for h in range(2):
                block = ref.at[:, head_columns(half * 2 + h)]
                start(block, packed.at[pl.ds((part * 2 + h) * ROWS, ROWS)])
    start(av_ref, sel_ref.at[pl.ds(UNIT, RANK)])
    for copy in copies:
        copy.wait()


def attend_head(q_ref, g_ref, dq_ref, g, keys, values, av_t, aq_t, put_adapter):
    count = len(keys)
    key_all = jnp.concatenate(keys, axis=0) if count > 1 else keys[0]
    value_all = jnp.concatenate(values, axis=0) if count > 1 else values[0]
    key_t = key_all.T
    allowed = lax.broadcasted_iota(jnp.int32, (ROWS, STEP * ROWS), 0) <= (
        lax.broadcasted_iota(jnp.int32, (ROWS, STEP * ROWS), 1) % ROWS
    )
    q_list, g_list, w_list, s_list = [], [], [], []
    for c in range(PER_HEAD // STEP):
        heads = range(g * PER_HEAD + c * STEP, g * PER_HEAD + (c + 1) * STEP)
        q = jnp.concatenate([q_ref[:, h * WIDTH : (h + 1) * WIDTH] for h in heads], axis=0)
        grad = jnp.concatenate([g_ref[:, h * WIDTH : (h + 1) * WIDTH] for h in heads], axis=0)
        scores = dot(key_all, q, NT)
        score_grad = dot(value_all, grad, NT)
        diagonal = jnp.where(allowed, scores[:ROWS], -1e30)
        scores = jnp.concatenate([diagonal, scores[ROWS:]], axis=0) if count > 1 else diagonal
        top = jnp.max(scores, axis=0, keepdims=True)
        raised = jnp.exp2((scores - top) * (SOFTMAX_SCALE * LOG2E))
        probs = raised * (1.0 / jnp.sum(raised, axis=0, keepdims=True))
        delta = jnp.sum(probs * score_grad, axis=0, keepdims=True)
        logit_grad = (probs * (score_grad - delta)).astype(bf16)
        dq_t = (dot(key_t, logit_grad, NN) * SOFTMAX_SCALE).astype(bf16)
        dq = jnp.concatenate([dq_t[:, i * ROWS : (i + 1) * ROWS].T for i in range(STEP)], axis=1)
        dq_ref[:, heads[0] * WIDTH : (heads[-1] + 1) * WIDTH] = dq
        adapter = dot(aq_t, dq, NN).astype(bf16)
        for i, h in enumerate(heads):
            put_adapter(h, adapter[:, i * WIDTH : (i + 1) * WIDTH])
        q_list.append(q)
        g_list.append(grad)
        w_list.append(probs.astype(bf16))
        s_list.append(logit_grad)
    q_all = jnp.concatenate(q_list, axis=0)
    g_all = jnp.concatenate(g_list, axis=0)
    dk = (dot(jnp.concatenate(s_list, axis=1), q_all, NN) * SOFTMAX_SCALE).astype(bf16)
    dv = dot(jnp.concatenate(w_list, axis=1), g_all, NN).astype(bf16)
    av_all = jnp.concatenate(av_t, axis=1) if count > 1 else av_t[0]
    return dk, dv, dot(av_all, dv, NN).astype(bf16)


def attend_half(half, q_hbm, g_hbm, dq_hbm, q_ref, g_ref, dq_ref, sems, variants, aq_t, put_adapter, put_value):
    copies = []
    for g in range(2):
        here = pl.ds(g * HEAD_COLUMNS, HEAD_COLUMNS)
        there = pl.ds(pl.multiple_of(half * HALF_COLUMNS + g * HEAD_COLUMNS, WIDTH), HEAD_COLUMNS)
        copies.append(
            [
                pltpu.make_async_copy(q_hbm.at[:, there], q_ref.at[:, here], sems.at[g]),
                pltpu.make_async_copy(g_hbm.at[:, there], g_ref.at[:, here], sems.at[2 + g]),
                pltpu.make_async_copy(dq_ref.at[:, here], dq_hbm.at[:, there], sems.at[4 + g]),
            ]
        )
    for copy in copies:
        copy[0].start()
        copy[1].start()

    def go(blocks, av_refs, outs):
        for g in range(2):
            copies[g][0].wait()
            copies[g][1].wait()
            keys = [ref[g * ROWS : (g + 1) * ROWS, :] for ref in blocks]
            values = [ref[(2 + g) * ROWS : (3 + g) * ROWS, :] for ref in blocks]
            av_t = [ref[UNIT:SEL_ROWS, :] for ref in av_refs]
            dk, dv, ad_v = attend_head(q_ref, g_ref, dq_ref, g, keys, values, av_t, aq_t, put_adapter)
            copies[g][2].start()
            put_value(g, ad_v)
            for n, (ref, base) in enumerate(outs):
                rows = slice(n * ROWS, (n + 1) * ROWS)
                ref[base + g * ROWS : base + (g + 1) * ROWS, :] = dk[rows]
                ref[base + (2 + g) * ROWS : base + (3 + g) * ROWS, :] = dv[rows]

    for condition, *rest in variants:
        pl.when(condition)(lambda rest=rest: go(*rest))
    copies[0][2].wait()
    copies[1][2].wait()


def short_kernel(
    place_ref, aq_ref, sel_ref, one_ref, q_hbm, g_hbm, dq_hbm, ad_ref, own_ref, back_ref, q_ref, g_ref, dq_ref, sems
):
    odd = place_ref[1]

    def put_adapter(h, value):
        ad_ref[h * RANK : (h + 1) * RANK, :] = value

    def put_value(g, value):
        ad_ref[(HALF_HEADS + g) * RANK : (HALF_HEADS + g + 1) * RANK, :] = value

    variants = [
        (odd == 0, [sel_ref], [sel_ref], [(own_ref, 0)]),
        (odd == 1, [sel_ref, one_ref], [sel_ref, one_ref], [(own_ref, 0), (back_ref, 0)]),
    ]
    attend_half(
        place_ref[0], q_hbm, g_hbm, dq_hbm, q_ref, g_ref, dq_ref, sems, variants, aq_ref[...], put_adapter, put_value
    )


def long_kernel(
    place_ref, aq_ref, sel_ref, oth_ref, one_ref, other_ref, two_ref, three_ref, ads_ref, backs_ref, q_hbm, g_hbm, dq_in,
    dq_hbm, ad_ref, own_ref, r1_ref, r2_ref, r3_ref, q_ref, g_ref, dq_ref, sems,
):
    short = place_ref[0]
    odd = place_ref[1]
    long = 1 - short
    n = HALF_HEADS * RANK

    def put_adapter(h, value):
        ad_ref[pl.ds(pl.multiple_of(long * n + h * RANK, RANK), RANK), :] = value

    def put_value(g, value):
        ad_ref[pl.ds(pl.multiple_of(2 * n + (long * 2 + g) * RANK, RANK), RANK), :] = value

    variants = [
        (
            odd == 0,
            [oth_ref, one_ref, two_ref],
            [sel_ref, one_ref, two_ref],
            [(own_ref, 0), (r1_ref, 0), (r2_ref, 0)],
        ),
        (
            odd == 1,
            [oth_ref, other_ref, two_ref, three_ref],
            [sel_ref, one_ref, two_ref, three_ref],
            [(own_ref, 0), (r1_ref, UNIT), (r2_ref, 0), (r3_ref, 0)],
        ),
    ]
    attend_half(long, q_hbm, g_hbm, dq_hbm, q_ref, g_ref, dq_ref, sems, variants, aq_ref[...], put_adapter, put_value)
    ad_ref[2 * n + 4 * RANK :, :] = jnp.zeros((ADAPTER_ROWS - 2 * n - 4 * RANK, WIDTH), bf16)
    ad_ref[pl.ds(pl.multiple_of(short * n, RANK), n), :] = ads_ref[:n, :]
    ad_ref[pl.ds(pl.multiple_of(2 * n + short * 2 * RANK, RANK), 2 * RANK), :] = ads_ref[n:, :]

    @pl.when(odd == 0)
    def _():
        r1_ref[UNIT:, :] = jnp.zeros((UNIT, WIDTH), bf16)

    @pl.when(odd == 1)
    def _():
        r1_ref[:UNIT, :] = backs_ref[...]


def finish_kernel(place_ref, sum_ref, short_ref, long_ref, r1_ref, r2_ref, r3_ref, dk_ref, dv_ref, aq_ref, av_ref):
    short = place_ref[0]
    even = place_ref[1] == 0
    for part, ref in ((0, dk_ref), (1, dv_ref)):
        for h in range(2):
            base = (part * 2 + h) * ROWS
            rows = slice(base, base + ROWS)
            total = short_ref[rows, :].astype(f32) + r1_ref[rows, :].astype(f32)
            total = total + r2_ref[rows, :].astype(f32)
            total = total + jnp.where(even, r3_ref[rows, :].astype(f32), 0.0)
            ref[:, head_columns(short * 2 + h)] = total.astype(bf16)
            other = r1_ref[UNIT + base : UNIT + base + ROWS, :].astype(f32)
            total = long_ref[rows, :].astype(f32) + jnp.where(even, other, 0.0)
            ref[:, head_columns((1 - short) * 2 + h)] = total.astype(bf16)
    for h in range(QUERY_HEAD_COUNT):
        aq_ref[:, h * WIDTH : (h + 1) * WIDTH] = (
            sum_ref[h * RANK : (h + 1) * RANK, :].astype(f32) * ADAPTER_SCALE
        )
    for h in range(KEY_VALUE_HEADS):
        base = (QUERY_HEAD_COUNT + h) * RANK
        av_ref[:, h * WIDTH : (h + 1) * WIDTH] = sum_ref[base : base + RANK, :].astype(f32) * ADAPTER_SCALE


def shape(dims, kind=bf16):
    return jax.ShapeDtypeStruct(dims, kind)


def whole(dims):
    return pl.BlockSpec(dims, lambda *_: (0,) * len(dims))


def passed_along(block, distance, senders=range(CTX_SIZE)):
    return lax.ppermute(block, CTX, [(i, (i + distance) % CTX_SIZE) for i in senders])


PARAMS = pltpu.CompilerParams(vmem_limit_bytes=40 * 1024 * 1024)
HEAD_COLUMNS = PER_HEAD * WIDTH
HALF_COLUMNS = 2 * HEAD_COLUMNS
SMEM = pl.BlockSpec(memory_space=pltpu.SMEM)
VMEM = pl.BlockSpec(memory_space=pltpu.VMEM)
HBM = pl.BlockSpec(memory_space=pltpu.HBM)


def pack(place, k, v, av_t):
    return pl.pallas_call(
        pack_kernel,
        in_specs=[SMEM, HBM, HBM, HBM],
        out_specs=[VMEM, VMEM],
        out_shape=[shape((SEL_ROWS, WIDTH)), shape((UNIT, WIDTH))],
        scratch_shapes=[pltpu.SemaphoreType.DMA((9,))],
        compiler_params=PARAMS,
        name="pack",
    )(place, k, v, av_t)


HALF_SCRATCH = [
    pltpu.VMEM((ROWS, HALF_COLUMNS), bf16),
    pltpu.VMEM((ROWS, HALF_COLUMNS), bf16),
    pltpu.VMEM((ROWS, HALF_COLUMNS), bf16),
    pltpu.SemaphoreType.DMA((6,)),
]


def attend_short(place, aq_t, sel, one, q, grad):
    return pl.pallas_call(
        short_kernel,
        in_specs=[SMEM, VMEM, VMEM, VMEM, HBM, HBM],
        out_specs=[HBM, VMEM, VMEM, VMEM],
        out_shape=[
            shape(q.shape),
            shape((HALF_ADAPTER_ROWS, WIDTH)),
            shape((UNIT, WIDTH)),
            shape((UNIT, WIDTH)),
        ],
        scratch_shapes=HALF_SCRATCH,
        compiler_params=PARAMS,
        cost_estimate=pl.CostEstimate(flops=700_000_000, bytes_accessed=3_000_000, transcendentals=0),
        name="short",
    )(place, aq_t, sel, one, q, grad)


def attend_long(place, aq_t, sel, oth, one, other, two, three, ads, backs, q, grad, dq):
    return pl.pallas_call(
        long_kernel,
        in_specs=[SMEM] + [VMEM] * 9 + [HBM] * 3,
        out_specs=[HBM] + [VMEM] * 5,
        out_shape=[
            shape(q.shape),
            shape((ADAPTER_ROWS, WIDTH)),
            shape((UNIT, WIDTH)),
            shape((2 * UNIT, WIDTH)),
            shape((UNIT, WIDTH)),
            shape((UNIT, WIDTH)),
        ],
        scratch_shapes=HALF_SCRATCH,
        input_output_aliases={12: 0},
        compiler_params=PARAMS,
        cost_estimate=pl.CostEstimate(flops=1_400_000_000, bytes_accessed=4_000_000, transcendentals=0),
        name="long",
    )(place, aq_t, sel, oth, one, other, two, three, ads, backs, q, grad, dq)


def finish(place, total, short, long, r1, r2, r3):
    operands = (total, short, long, r1, r2, r3)
    outs = [
        shape((ROWS, KEY_VALUE_HEADS * WIDTH)),
        shape((ROWS, KEY_VALUE_HEADS * WIDTH)),
        shape((RANK, QUERY_HEAD_COUNT * WIDTH), f32),
        shape((RANK, KEY_VALUE_HEADS * WIDTH), f32),
    ]
    return pl.pallas_call(
        finish_kernel,
        grid_spec=pltpu.PrefetchScalarGridSpec(
            num_scalar_prefetch=1,
            grid=(1,),
            in_specs=[whole(a.shape) for a in operands],
            out_specs=[whole(o.shape) for o in outs],
        ),
        out_shape=outs,
        compiler_params=PARAMS,
        name="finish",
    )(place, *operands)


def copies_to_all(block, axes):
    size = lax.axis_size(axes)
    return lax.all_to_all(jnp.broadcast_to(block[None], (size,) + block.shape), axes, 0, 0)


def summed(pieces):
    return jnp.sum(pieces.astype(f32), axis=0).astype(bf16)


def sum_over_all(part, beside):
    size = lax.axis_size(NEAR)
    mine = summed(lax.all_to_all(part.reshape(size, part.shape[0] // size, WIDTH), NEAR, 0, 0))
    mine = summed(copies_to_all(mine, FAR))
    mine, beside = lax.optimization_barrier((mine, beside))
    return copies_to_all(mine, NEAR).reshape(part.shape), beside


def body(queries, keys, values, output_gradient, adapter_query_down, adapter_value_down):
    position = lax.axis_index(CTX) % GROUP_DEVS
    place = jnp.stack([position // 2, position % 2]).astype(jnp.int32)
    q, grad, aq_t = queries[0], output_gradient[0], adapter_query_down[0].T
    sel, oth = pack(place, keys[0], values[0], adapter_value_down[0].T)
    one = passed_along(sel, 1)
    two = passed_along(sel, 2)
    three = passed_along(sel, 3, range(0, CTX_SIZE, 2))
    other = passed_along(oth, 1, range(0, CTX_SIZE, 2))
    dq, ads, own_short, backs = attend_short(place, aq_t, sel, one, q, grad)
    dq, part, own_long, r1, r2, r3 = attend_long(
        place, aq_t, sel, oth, one, other, two, three, ads, backs, q, grad, dq
    )
    r1 = passed_along(r1, -1)
    r2 = passed_along(r2, -2)
    r3 = passed_along(r3, -3, range(1, CTX_SIZE, 2))
    total, (r1, r2, r3) = sum_over_all(part, (r1, r2, r3))
    dk, dv, adapter_q, adapter_v = finish(place, total, own_short, own_long, r1, r2, r3)
    return dq[None], dk[None], dv[None], adapter_q, adapter_v


def solution(mesh):
    split = Mesh(mesh.devices.reshape(SIZES), AXES)
    tokens = P(DP, CTX, None)
    return jax.shard_map(
        body,
        mesh=split,
        in_specs=(tokens,) * 6,
        out_specs=(tokens, tokens, tokens, P(), P()),
        check_vma=False,
    )
```

time: 105 us -> 96.1 us (0.915)
  blocking collectives: 37.5 us -> 11.1 us
  starting transfers between devices: 27.9 us -> 46.6 us
  Pallas kernels: 15.3 us -> 10.7 us
  waiting for transfers between devices: 17 us -> 19.8 us
  local copies, waits for them, and re-layouts: 5.11 us -> 6.3 us
    all_to_all x1, blocking collectives: 25.2 us -> 11.1 us  [copies_to_all(): lax.all_to_all(jnp.broadcast_to(block[None], (size,) + block.shape), axes...]
    all_to_all x1 -> x0, blocking collectives: 12.3 us -> none  [sum_over_all(): lax.all_to_all(part.reshape(size, part.shape[0] // size, WIDTH), NEAR, 0, 0)]
    all_to_all x0 -> x1, starting transfers between devices: none -> 9.04 us  [sum_over_all(): lax.all_to_all(part.reshape(size, part.shape[0] // size, WIDTH), NEAR, 0, 0)]
    all_to_all x1, starting transfers between devices: 5.29 us -> 10.6 us  [copies_to_all(): lax.all_to_all(jnp.broadcast_to(block[None], (size,) + block.shape), axes...]
    pallas_call x3, Pallas kernels: 13.8 us -> 9.24 us  [the longest x1 5.37 us: attend_long(): pl.pallas_call(long_kernel, in_specs=[SMEM] + [VMEM] * 9 + [HBM] * 3, out...]
    ppermute x6 -> x7, starting transfers between devices: 22.6 us -> 26.9 us  [passed_along(): lax.ppermute(block, CTX, [(i, (i + distance) % CTX_SIZE) for i in senders])]
    all_to_all x1, waiting for transfers between devices: 0.01 us -> 4.31 us  [copies_to_all(): lax.all_to_all(jnp.broadcast_to(block[None], (size,) + block.shape), axes...]
    ppermute x6 -> x7, waiting for transfers between devices: 17 us -> 13.2 us  [passed_along(): lax.ppermute(block, CTX, [(i, (i + distance) % CTX_SIZE) for i in senders])]
  transfers between devices with their start and end apart: 7 -> 9, of which waited for: 4 -> 6; matrix products, arithmetic and copies ran while one was open for 0% -> 1% of each run, Pallas kernels for 6% -> 3%
where the time goes in v2:
time: 96.1 us; the launch traced here: 95.5 us
  starting transfers between devices  46.6 us (48%)
  waiting for transfers between devices  19.8 us (21%)
  blocking collectives  11.1 us (12%)
  Pallas kernels  10.7 us (11%)
  local copies, waits for them, and re-layouts  6.3 us (7%)
    ppermute x7, starting transfers between devices, passed_along(): lax.ppermute(block, CTX, [(i, (i + distance) % CTX_SIZE) for i in senders])  26.9 us
    ppermute x7, waiting for transfers between devices, passed_along(): lax.ppermute(block, CTX, [(i, (i + distance) % CTX_SIZE) for i in senders])  13.2 us
    all_to_all x1, blocking collectives, copies_to_all(): lax.all_to_all(jnp.broadcast_to(block[None], (size,) + block.shape), axes...  11.1 us
    all_to_all x1, starting transfers between devices, copies_to_all(): lax.all_to_all(jnp.broadcast_to(block[None], (size,) + block.shape), axes...  10.6 us
    all_to_all x1, starting transfers between devices, sum_over_all(): lax.all_to_all(part.reshape(size, part.shape[0] // size, WIDTH), NEAR, 0, 0)  9.04 us
    pallas_call x1, Pallas kernels, attend_long(): pl.pallas_call(long_kernel, in_specs=[SMEM] + [VMEM] * 9 + [HBM] * 3, out...  5.37 us
    unnamed x14, local copies, waits for them, and re-layouts  4.87 us
    all_to_all x1, waiting for transfers between devices, copies_to_all(): lax.all_to_all(jnp.broadcast_to(block[None], (size,) + block.shape), axes...  4.31 us
  transfers between devices with their start and end apart: 9, of which 6 were waited for; matrix products, arithmetic and copies ran while one was open for 1% of the time, Pallas kernels for 3%

profile of v2, /device:TPU:1, one launch (start us, length us, event | category | flops | bytes accessed | tf_op | source)
XLA Modules:
  0.0 95.5 jit_solution(4831740216512788024)
XLA Ops:
  0.7 0.1 pad_add_fusion.place_ref
  0.8 0.6 copy-done.2
  1.4 0.9 copy-done
  2.3 0.9 copy-done.1
  3.2 0.7 pack.1
  3.9 0.0 copy-start.6
  3.9 4.0 %collective-permute-start = (bf16[528,128]{1,0:T(8,128)(2,1)S(1)}, bf16[528,128]{1,0:T(8,128)(2,1)S(1)}, u32[]{:S(2)}, u32[]{:S(2)}) collective-permute-start(bf16[528,128]{1,0:T(8,128)(2,1)S(1)} %get-tuple-element.25.sel_ref), channel_id=1, source_target_pairs={{0,8},{8,16},{16,24},{24,32},{32,40},{40,48},{48,56},{56,64},{64,7... | collective-permute-start | bytes 405512 | tf_op jit(solution)/shard_map/ppermute | solution.py:238
  7.9 6.4 %collective-permute-start.3 = (bf16[528,128]{1,0:T(8,128)(2,1)S(1)}, bf16[528,128]{1,0:T(8,128)(2,1)S(1)}, u32[]{:S(2)}, u32[]{:S(2)}) collective-permute-start(bf16[528,128]{1,0:T(8,128)(2,1)S(1)} %get-tuple-element.25.sel_ref), channel_id=1, source_target_pairs={{0,24},{16,40},{32,56},{48,72},{64,88},{80,104},{96,120},{112,136}... | collective-permute-start | bytes 405512 | tf_op jit(solution)/shard_map/ppermute | solution.py:238
  14.4 2.4 %collective-permute-start.2 = (bf16[528,128]{1,0:T(8,128)(2,1)S(1)}, bf16[528,128]{1,0:T(8,128)(2,1)S(1)}, u32[]{:S(2)}, u32[]{:S(2)}) collective-permute-start(bf16[528,128]{1,0:T(8,128)(2,1)S(1)} %get-tuple-element.25.sel_ref), channel_id=1, source_target_pairs={{0,16},{8,24},{16,32},{24,40},{32,48},{40,56},{48,64},{56,72},{64,... | collective-permute-start | bytes 405512 | tf_op jit(solution)/shard_map/ppermute | solution.py:238
  16.8 1.3 %collective-permute-start.1 = (bf16[512,128]{1,0:T(8,128)(2,1)S(1)}, bf16[512,128]{1,0:T(8,128)(2,1)S(1)}, u32[]{:S(2)}, u32[]{:S(2)}) collective-permute-start(bf16[512,128]{1,0:T(8,128)(2,1)S(1)} %get-tuple-element.26.oth_ref), channel_id=1, source_target_pairs={{0,8},{16,24},{32,40},{48,56},{64,72},{80,88},{96,104},{112,120},{... | collective-permute-start | bytes 393224 | tf_op jit(solution)/shard_map/ppermute | solution.py:238
  18.1 0.0 collective-permute-done.one_ref
  18.1 0.0 copy-start.3
  18.2 1.2 %copy-done.3 = bf16[1,128,4096]{2,1,0:T(8,128)(2,1)S(1)} copy-done((bf16[1,128,4096]{2,1,0:T(8,128)(2,1)S(1)}, bf16[1,128,4096]{2,1,0:T(8,128)(2,1)}, u32[]{:S(2)}) %copy-start.3) | copy-done | bytes 1048600
  19.4 1.2 %copy-done.5 = bf16[1,128,4096]{2,1,0:T(8,128)(2,1)S(1)} copy-done((bf16[1,128,4096]{2,1,0:T(8,128)(2,1)S(1)}, bf16[1,128,4096]{2,1,0:T(8,128)(2,1)}, u32[]{:S(2)}) %copy-start.5) | copy-done | bytes 1048600
  20.6 3.2 %short.1 = (bf16[128,4096]{1,0:T(8,128)(2,1)}, bf16[288,128]{1,0:T(8,128)(2,1)S(1)}, bf16[512,128]{1,0:T(8,128)(2,1)S(1)}, bf16[512,128]{1,0:T(8,128)(2,1)S(1)}) custom-call(s32[2]{0:T(128)S(1)} %pad_add_fusion.place_ref, bf16[16,128]{1,0:T(8,128)(2,1)S(1)} %bitcast.22, bf16[528,128]{1,0:T(8,128)(2,1)S(1)} %get-tuple-element.25.sel_ref, ...), custom_call_target="tpu_custom_call" | custom-call | flops 700000000 | bytes 3000000 | tf_op jit(solution)/shard_map/short/pallas_call | solution.py:270
  23.8 4.6 %collective-permute-done.1.other_ref = bf16[512,128]{1,0:T(8,128)(2,1)S(1)} collective-permute-done((bf16[512,128]{1,0:T(8,128)(2,1)S(1)}, bf16[512,128]{1,0:T(8,128)(2,1)S(1)}, u32[]{:S(2)}, u32[]{:S(2)}) %collective-permute-start.1) | collective-permute-done | bytes 131104 | tf_op jit(solution)/shard_map/ppermute | solution.py:238
  28.4 0.0 collective-permute-done.3.three_ref
  28.4 0.2 collective-permute-done.2.two_ref
  28.6 5.4 %long.1 = (bf16[128,4096]{1,0:T(8,128)(2,1)}, bf16[640,128]{1,0:T(8,128)(2,1)S(1)}, bf16[512,128]{1,0:T(8,128)(2,1)S(1)}, bf16[1024,128]{1,0:T(8,128)(2,1)S(1)},...) custom-call(s32[2]{0:T(128)S(1)} %pad_add_fusion.place_ref, ...), custom_call_target="tpu_custom_call", output_to_operand_aliasing={{0}: (12, {})} | custom-call | flops 1400000000 | bytes 4000000 | tf_op jit(solution)/shard_map/long/pallas_call | solution.py:288
  34.0 0.7 reshape.18
  34.7 9.0 %all-to-all-start = ((bf16[32,20,128]{2,1,0:T(8,128)(2,1)}), bf16[32,20,128]{2,1,0:T(8,128)(2,1)S(1)}, u32[]{:S(2)}, u32[]{:S(2)}) async-start(bf16[32,20,128]{2,1,0:T(8,128)(2,1)} %reshape.18), calls=%async_computation | async-start | bytes 393216 | tf_op jit(solution)/shard_map/all_to_all | solution.py:341
  43.7 5.5 %collective-permute-start.4 = (bf16[1024,128]{1,0:T(8,128)(2,1)S(1)}, bf16[1024,128]{1,0:T(8,128)(2,1)S(1)}, u32[]{:S(2)}, u32[]{:S(2)}) collective-permute-start(bf16[1024,128]{1,0:T(8,128)(2,1)S(1)} %get-tuple-element.32), channel_id=1, source_target_pairs={{0,504},{8,0},{16,8},{24,16},{32,24},{40,32},{48,40},{56,48},{64,5... | collective-permute-start | bytes 786440 | tf_op jit(solution)/shard_map/ppermute | solution.py:238
  49.3 2.3 %all-to-all-done = bf16[32,20,128]{2,1,0:T(8,128)(2,1)S(1)} async-done(((bf16[32,20,128]{2,1,0:T(8,128)(2,1)}), bf16[32,20,128]{2,1,0:T(8,128)(2,1)S(1)}, u32[]{:S(2)}, u32[]{:S(2)}) %all-to-all-start) | async-done | bytes 163872 | tf_op jit(solution)/shard_map/all_to_all | solution.py:341
  51.6 0.7 broadcast_in_dim.22
  52.3 10.6 %all-to-all-start.1 = ((bf16[16,20,128]{2,1,0:T(8,128)(2,1)}), bf16[16,20,128]{2,1,0:T(8,128)(2,1)S(1)}, u32[]{:S(2)}, u32[]{:S(2)}) async-start(bf16[16,20,128]{2,1,0:T(8,128)(2,1)} %broadcast_in_dim.22), calls=%async_computation.1 | async-start | bytes 196608 | tf_op jit(solution)/shard_map/all_to_all | solution.py:332
  62.9 5.9 %collective-permute-start.5 = (bf16[512,128]{1,0:T(8,128)(2,1)S(1)}, bf16[512,128]{1,0:T(8,128)(2,1)S(1)}, u32[]{:S(2)}, u32[]{:S(2)}) collective-permute-start(bf16[512,128]{1,0:T(8,128)(2,1)S(1)} %get-tuple-element.33), channel_id=1, source_target_pairs={{0,496},{8,504},{16,0},{24,8},{32,16},{40,24},{48,32},{56,40},{64,... | collective-permute-start | bytes 393224 | tf_op jit(solution)/shard_map/ppermute | solution.py:238
  68.8 1.3 %collective-permute-start.6 = (bf16[512,128]{1,0:T(8,128)(2,1)S(1)}, bf16[512,128]{1,0:T(8,128)(2,1)S(1)}, u32[]{:S(2)}, u32[]{:S(2)}) collective-permute-start(bf16[512,128]{1,0:T(8,128)(2,1)S(1)} %get-tuple-element.34), channel_id=1, source_target_pairs={{8,496},{24,0},{40,16},{56,32},{72,48},{88,64},{104,80},{120,96},{... | collective-permute-start | bytes 393224 | tf_op jit(solution)/shard_map/ppermute | solution.py:238
  70.1 4.3 %all-to-all-done.1 = bf16[16,20,128]{2,1,0:T(8,128)(2,1)S(1)} async-done(((bf16[16,20,128]{2,1,0:T(8,128)(2,1)}), bf16[16,20,128]{2,1,0:T(8,128)(2,1)S(1)}, u32[]{:S(2)}, u32[]{:S(2)}) %all-to-all-start.1) | async-done | bytes 81952 | tf_op jit(solution)/shard_map/all_to_all | solution.py:332
  74.5 0.1 collective-permute-done.5.r2_ref
  74.5 8.3 %collective-permute-done.6.r3_ref = bf16[512,128]{1,0:T(8,128)(2,1)S(1)} collective-permute-done((bf16[512,128]{1,0:T(8,128)(2,1)S(1)}, bf16[512,128]{1,0:T(8,128)(2,1)S(1)}, u32[]{:S(2)}, u32[]{:S(2)}) %collective-permute-start.6) | collective-permute-done | bytes 131104 | tf_op jit(solution)/shard_map/ppermute | solution.py:238
  82.9 11.1 %all_to_all.15 = bf16[32,20,128]{2,1,0:T(8,128)(2,1)S(1)} all-to-all(bf16[32,20,128]{2,1,0:T(8,128)(2,1)S(1)} %broadcast_in_dim.23), channel_id=1, replica_groups=mesh['x'=4,'zl'=2,'yh'=4,'yl'=2,'zh'=4,'core'=2] {'x','zl','yl','core'}, dimensions={0} | all-to-all | bytes 327680 | tf_op jit(solution)/shard_map/all_to_all | solution.py:332
  94.0 1.4 %finish.1 = (bf16[128,512]{1,0:T(8,128)(2,1)}, bf16[128,512]{1,0:T(8,128)(2,1)}, f32[16,4096]{1,0:T(8,128)}, f32[16,512]{1,0:T(8,128)}) custom-call(s32[2]{0:T(128)S(1)} %pad_add_fusion.place_ref, bf16[640,128]{1,0:T(8,128)(2,1)S(1)} %reshape.19.sum_ref, bf16[512,128]{1,0:T(8,128)(2,1)S(1)} %get-tuple-element.36.short_ref, ...), custom_call_target="tpu_custom_call" | custom-call | tf_op jit(solution)/shard_map/finish/pallas_call | solution.py:316
  (12 shorter events, 0.2 us)
Async XLA Ops:
  0.7 0.7 copy-start.2
  1.4 0.9 copy-start
  2.3 0.9 copy-start.1
  3.9 14.3 %copy-start.6 = (bf16[1,128,16]{1,2,0:T(8,128)(2,1)S(1)}, bf16[1,128,16]{1,2,0:T(8,128)(2,1)}, u32[]{:S(2)}) copy-start(bf16[1,128,16]{1,2,0:T(8,128)(2,1)} %param.10) | copy-start | bytes 12292
  3.9 14.2 %collective-permute-start = (bf16[528,128]{1,0:T(8,128)(2,1)S(1)}, bf16[528,128]{1,0:T(8,128)(2,1)S(1)}, u32[]{:S(2)}, u32[]{:S(2)}) collective-permute-start(bf16[528,128]{1,0:T(8,128)(2,1)S(1)} %get-tuple-element.25.sel_ref), channel_id=1, source_target_pairs={{0,8},{8,16},{16,24},{24,32},{32,40},{40,48},{48,56},{56,64},{64,7... | collective-permute-start | bytes 405512 | tf_op jit(solution)/shard_map/ppermute | solution.py:238
  7.9 20.4 %collective-permute-start.3 = (bf16[528,128]{1,0:T(8,128)(2,1)S(1)}, bf16[528,128]{1,0:T(8,128)(2,1)S(1)}, u32[]{:S(2)}, u32[]{:S(2)}) collective-permute-start(bf16[528,128]{1,0:T(8,128)(2,1)S(1)} %get-tuple-element.25.sel_ref), channel_id=1, source_target_pairs={{0,24},{16,40},{32,56},{48,72},{64,88},{80,104},{96,120},{112,136}... | collective-permute-start | bytes 405512 | tf_op jit(solution)/shard_map/ppermute | solution.py:238
  14.4 14.2 %collective-permute-start.2 = (bf16[528,128]{1,0:T(8,128)(2,1)S(1)}, bf16[528,128]{1,0:T(8,128)(2,1)S(1)}, u32[]{:S(2)}, u32[]{:S(2)}) collective-permute-start(bf16[528,128]{1,0:T(8,128)(2,1)S(1)} %get-tuple-element.25.sel_ref), channel_id=1, source_target_pairs={{0,16},{8,24},{16,32},{24,40},{32,48},{40,56},{48,64},{56,72},{64,... | collective-permute-start | bytes 405512 | tf_op jit(solution)/shard_map/ppermute | solution.py:238
  16.8 11.5 %collective-permute-start.1 = (bf16[512,128]{1,0:T(8,128)(2,1)S(1)}, bf16[512,128]{1,0:T(8,128)(2,1)S(1)}, u32[]{:S(2)}, u32[]{:S(2)}) collective-permute-start(bf16[512,128]{1,0:T(8,128)(2,1)S(1)} %get-tuple-element.26.oth_ref), channel_id=1, source_target_pairs={{0,8},{16,24},{32,40},{48,56},{64,72},{80,88},{96,104},{112,120},{... | collective-permute-start | bytes 393224 | tf_op jit(solution)/shard_map/ppermute | solution.py:238
  18.1 1.2 %copy-start.3 = (bf16[1,128,4096]{2,1,0:T(8,128)(2,1)S(1)}, bf16[1,128,4096]{2,1,0:T(8,128)(2,1)}, u32[]{:S(2)}) copy-start(bf16[1,128,4096]{2,1,0:T(8,128)(2,1)} %param.6) | copy-start | bytes 3145732
  19.4 1.2 %copy-start.5 = (bf16[1,128,4096]{2,1,0:T(8,128)(2,1)S(1)}, bf16[1,128,4096]{2,1,0:T(8,128)(2,1)}, u32[]{:S(2)}) copy-start(bf16[1,128,4096]{2,1,0:T(8,128)(2,1)} %param.9) | copy-start | bytes 3145732
  20.6 8.0 %copy-start.4 = (bf16[1,128,4096]{2,1,0:T(8,128)(2,1)S(1)}, bf16[1,128,4096]{2,1,0:T(8,128)(2,1)}, u32[]{:S(2)}) copy-start(bf16[1,128,4096]{2,1,0:T(8,128)(2,1)} %param.6) | copy-start | bytes 3145732
  34.7 16.9 %all-to-all-start = ((bf16[32,20,128]{2,1,0:T(8,128)(2,1)}), bf16[32,20,128]{2,1,0:T(8,128)(2,1)S(1)}, u32[]{:S(2)}, u32[]{:S(2)}) async-start(bf16[32,20,128]{2,1,0:T(8,128)(2,1)} %reshape.18), calls=%async_computation | async-start | bytes 393216 | tf_op jit(solution)/shard_map/all_to_all | solution.py:341
  43.7 39.1 %collective-permute-start.4 = (bf16[1024,128]{1,0:T(8,128)(2,1)S(1)}, bf16[1024,128]{1,0:T(8,128)(2,1)S(1)}, u32[]{:S(2)}, u32[]{:S(2)}) collective-permute-start(bf16[1024,128]{1,0:T(8,128)(2,1)S(1)} %get-tuple-element.32), channel_id=1, source_target_pairs={{0,504},{8,0},{16,8},{24,16},{32,24},{40,32},{48,40},{56,48},{64,5... | collective-permute-start | bytes 786440 | tf_op jit(solution)/shard_map/ppermute | solution.py:238
  52.3 22.2 %all-to-all-start.1 = ((bf16[16,20,128]{2,1,0:T(8,128)(2,1)}), bf16[16,20,128]{2,1,0:T(8,128)(2,1)S(1)}, u32[]{:S(2)}, u32[]{:S(2)}) async-start(bf16[16,20,128]{2,1,0:T(8,128)(2,1)} %broadcast_in_dim.22), calls=%async_computation.1 | async-start | bytes 196608 | tf_op jit(solution)/shard_map/all_to_all | solution.py:332
  62.9 11.6 %collective-permute-start.5 = (bf16[512,128]{1,0:T(8,128)(2,1)S(1)}, bf16[512,128]{1,0:T(8,128)(2,1)S(1)}, u32[]{:S(2)}, u32[]{:S(2)}) collective-permute-start(bf16[512,128]{1,0:T(8,128)(2,1)S(1)} %get-tuple-element.33), channel_id=1, source_target_pairs={{0,496},{8,504},{16,0},{24,8},{32,16},{40,24},{48,32},{56,40},{64,... | collective-permute-start | bytes 393224 | tf_op jit(solution)/shard_map/ppermute | solution.py:238
  68.8 14.0 %collective-permute-start.6 = (bf16[512,128]{1,0:T(8,128)(2,1)S(1)}, bf16[512,128]{1,0:T(8,128)(2,1)S(1)}, u32[]{:S(2)}, u32[]{:S(2)}) collective-permute-start(bf16[512,128]{1,0:T(8,128)(2,1)S(1)} %get-tuple-element.34), channel_id=1, source_target_pairs={{8,496},{24,0},{40,16},{56,32},{72,48},{88,64},{104,80},{120,96},{... | collective-permute-start | bytes 393224 | tf_op jit(solution)/shard_map/ppermute | solution.py:238

commit v3 on v2

v3 whole, which is shorter than its diff:
```python
import jax
import jax.numpy as jnp
from jax import lax
from jax.experimental import pallas as pl
from jax.experimental.pallas import tpu as pltpu
from jax.sharding import Mesh, PartitionSpec as P

QUERY_HEAD_COUNT = 32
KEY_VALUE_HEADS = 4
WIDTH = 128
ROWS = 128
RANK = 16
GROUP_DEVS = 4
ADAPTER_SCALE = 2.0
SOFTMAX_SCALE = WIDTH ** (-0.5)
LOG2E = 1.4426950408889634
PER_HEAD = QUERY_HEAD_COUNT // KEY_VALUE_HEADS
HALF_HEADS = QUERY_HEAD_COUNT // 2
UNIT = 4 * ROWS
SEL_ROWS = UNIT + RANK
ADAPTER_ROWS = 768
HALF_ADAPTER_ROWS = (HALF_HEADS + 2) * RANK

AXES = ("x", "zl", "yh", "yl", "zh", "core")
SIZES = (4, 2, 4, 2, 4, 2)
CTX = ("x", "zl", "yh", "yl")
DP = ("zh", "core")
NEAR = ("x", "zl", "yl", "core")
FAR = ("yh", "zh")
CTX_SIZE = 64

NT = (((1,), (1,)), ((), ()))
NN = (((1,), (0,)), ((), ()))
bf16 = jnp.bfloat16
f32 = jnp.float32


def dot(a, b, dims):
    return lax.dot_general(a, b, dims, preferred_element_type=f32)


def head_columns(head):
    return pl.ds(pl.multiple_of(head * WIDTH, WIDTH), WIDTH)


def attend_head(q_wide, g_wide, put_dq, keys, values, av_t, aq_t):
    count = len(keys)
    key_all = jnp.concatenate(keys, axis=0) if count > 1 else keys[0]
    value_all = jnp.concatenate(values, axis=0) if count > 1 else values[0]
    rows = PER_HEAD * ROWS
    allowed = lax.broadcasted_iota(jnp.int32, (ROWS, rows), 0) <= (
        lax.broadcasted_iota(jnp.int32, (ROWS, rows), 1) % ROWS
    )
    heads = [slice(h * WIDTH, (h + 1) * WIDTH) for h in range(PER_HEAD)]
    q = jnp.concatenate([q_wide[:, h] for h in heads], axis=0)
    grad = jnp.concatenate([g_wide[:, h] for h in heads], axis=0)
    scores = dot(key_all, q, NT)
    score_grad = dot(value_all, grad, NT)
    diagonal = jnp.where(allowed, scores[:ROWS], -1e30)
    scores = jnp.concatenate([diagonal, scores[ROWS:]], axis=0) if count > 1 else diagonal
    top = jnp.max(scores, axis=0, keepdims=True)
    raised = jnp.exp2((scores - top) * (SOFTMAX_SCALE * LOG2E))
    probs = raised * (1.0 / jnp.sum(raised, axis=0, keepdims=True))
    delta = jnp.sum(probs * score_grad, axis=0, keepdims=True)
    logit_grad = (probs * (score_grad - delta)).astype(bf16)
    dq_t = (dot(key_all.T, logit_grad, NN) * SOFTMAX_SCALE).astype(bf16)
    dq = jnp.concatenate([dq_t[:, h].T for h in heads], axis=1)
    put_dq(dq)
    dv = dot(probs.astype(bf16), grad, NN).astype(bf16)
    dk = (dot(logit_grad, q, NN) * SOFTMAX_SCALE).astype(bf16)
    av_all = jnp.concatenate(av_t, axis=1) if count > 1 else av_t[0]
    return dk, dv, dot(aq_t, dq, NN).astype(bf16), dot(av_all, dv, NN).astype(bf16)


def attend_half(half, q_ref, g_ref, dq_hbm, dq_ref, sems, variants, aq_t, put_adapter, put_value):
    def columns(g):
        return pl.ds(pl.multiple_of(half * HALF_COLUMNS + g * HEAD_COLUMNS, WIDTH), HEAD_COLUMNS)

    copies = [
        pltpu.make_async_copy(
            dq_ref.at[:, pl.ds(g * HEAD_COLUMNS, HEAD_COLUMNS)], dq_hbm.at[:, columns(g)], sems.at[g]
        )
        for g in range(2)
    ]

    def go(blocks, av_refs, outs):
        for g in range(2):
            keys = [ref[g * ROWS : (g + 1) * ROWS, :] for ref in blocks]
            values = [ref[(2 + g) * ROWS : (3 + g) * ROWS, :] for ref in blocks]
            av_t = [ref[UNIT:SEL_ROWS, :] for ref in av_refs]

            def put_dq(dq, g=g):
                dq_ref[:, g * HEAD_COLUMNS : (g + 1) * HEAD_COLUMNS] = dq
                copies[g].start()

            dk, dv, ad_q, ad_v = attend_head(
                q_ref[:, columns(g)], g_ref[:, columns(g)], put_dq, keys, values, av_t, aq_t
            )
            for h in range(PER_HEAD):
                put_adapter(g * PER_HEAD + h, ad_q[:, h * WIDTH : (h + 1) * WIDTH])
            put_value(g, ad_v)
            for n, (ref, base) in enumerate(outs):
                rows = slice(n * ROWS, (n + 1) * ROWS)
                ref[base + g * ROWS : base + (g + 1) * ROWS, :] = dk[rows]
                ref[base + (2 + g) * ROWS : base + (3 + g) * ROWS, :] = dv[rows]

    for condition, *rest in variants:
        pl.when(condition)(lambda rest=rest: go(*rest))
    copies[0].wait()
    copies[1].wait()


def short_kernel(
    place_ref, aq_ref, sel_ref, one_ref, q_ref, g_ref, dq_hbm, ad_ref, own_ref, back_ref, dq_ref, sems
):
    odd = place_ref[1]

    def put_adapter(h, value):
        ad_ref[h * RANK : (h + 1) * RANK, :] = value

    def put_value(g, value):
        ad_ref[(HALF_HEADS + g) * RANK : (HALF_HEADS + g + 1) * RANK, :] = value

    variants = [
        (odd == 0, [sel_ref], [sel_ref], [(own_ref, 0)]),
        (odd == 1, [sel_ref, one_ref], [sel_ref, one_ref], [(own_ref, 0), (back_ref, 0)]),
    ]
    attend_half(place_ref[0], q_ref, g_ref, dq_hbm, dq_ref, sems, variants, aq_ref[...], put_adapter, put_value)


def long_kernel(
    place_ref, aq_ref, sel_ref, oth_ref, one_ref, other_ref, two_ref, three_ref, ads_ref, backs_ref, q_ref, g_ref, dq_in,
    dq_hbm, ad_ref, own_ref, r1_ref, r2_ref, r3_ref, dq_ref, sems,
):
    short = place_ref[0]
    odd = place_ref[1]
    long = 1 - short
    n = HALF_HEADS * RANK

    def put_adapter(h, value):
        ad_ref[pl.ds(pl.multiple_of(long * n + h * RANK, RANK), RANK), :] = value

    def put_value(g, value):
        ad_ref[pl.ds(pl.multiple_of(2 * n + (long * 2 + g) * RANK, RANK), RANK), :] = value

    variants = [
        (
            odd == 0,
            [oth_ref, one_ref, two_ref],
            [sel_ref, one_ref, two_ref],
            [(own_ref, 0), (r1_ref, 0), (r2_ref, 0)],
        ),
        (
            odd == 1,
            [oth_ref, other_ref, two_ref, three_ref],
            [sel_ref, one_ref, two_ref, three_ref],
            [(own_ref, 0), (r1_ref, UNIT), (r2_ref, 0), (r3_ref, 0)],
        ),
    ]
    attend_half(long, q_ref, g_ref, dq_hbm, dq_ref, sems, variants, aq_ref[...], put_adapter, put_value)
    ad_ref[2 * n + 4 * RANK :, :] = jnp.zeros((ADAPTER_ROWS - 2 * n - 4 * RANK, WIDTH), bf16)
    ad_ref[pl.ds(pl.multiple_of(short * n, RANK), n), :] = ads_ref[:n, :]
    ad_ref[pl.ds(pl.multiple_of(2 * n + short * 2 * RANK, RANK), 2 * RANK), :] = ads_ref[n:, :]

    @pl.when(odd == 0)
    def _():
        r1_ref[UNIT:, :] = jnp.zeros((UNIT, WIDTH), bf16)

    @pl.when(odd == 1)
    def _():
        r1_ref[:UNIT, :] = backs_ref[...]


def key_sum_kernel(place_ref, short_ref, long_ref, r1_ref, r2_ref, r3_ref, dk_ref, dv_ref):
    short = place_ref[0]
    even = place_ref[1] == 0
    for part, ref in ((0, dk_ref), (1, dv_ref)):
        for h in range(2):
            base = (part * 2 + h) * ROWS
            rows = slice(base, base + ROWS)
            total = short_ref[rows, :].astype(f32) + r1_ref[rows, :].astype(f32)
            total = total + r2_ref[rows, :].astype(f32)
            total = total + jnp.where(even, r3_ref[rows, :].astype(f32), 0.0)
            ref[:, head_columns(short * 2 + h)] = total.astype(bf16)
            other = r1_ref[UNIT + base : UNIT + base + ROWS, :].astype(f32)
            total = long_ref[rows, :].astype(f32) + jnp.where(even, other, 0.0)
            ref[:, head_columns((1 - short) * 2 + h)] = total.astype(bf16)


def adapter_kernel(sum_ref, aq_ref, av_ref):
    for h in range(QUERY_HEAD_COUNT):
        aq_ref[:, h * WIDTH : (h + 1) * WIDTH] = (
            sum_ref[h * RANK : (h + 1) * RANK, :].astype(f32) * ADAPTER_SCALE
        )
    for h in range(KEY_VALUE_HEADS):
        base = (QUERY_HEAD_COUNT + h) * RANK
        av_ref[:, h * WIDTH : (h + 1) * WIDTH] = sum_ref[base : base + RANK, :].astype(f32) * ADAPTER_SCALE


def shape(dims, kind=bf16):
    return jax.ShapeDtypeStruct(dims, kind)


def whole(dims):
    return pl.BlockSpec(dims, lambda *_: (0,) * len(dims))


def passed_along(block, distance, senders=range(CTX_SIZE)):
    return lax.ppermute(block, CTX, [(i, (i + distance) % CTX_SIZE) for i in senders])


SUM_FLOPS = 20_000_000_000
PARAMS = pltpu.CompilerParams(vmem_limit_bytes=40 * 1024 * 1024)
HEAD_COLUMNS = PER_HEAD * WIDTH
HALF_COLUMNS = 2 * HEAD_COLUMNS
SMEM = pl.BlockSpec(memory_space=pltpu.SMEM)
VMEM = pl.BlockSpec(memory_space=pltpu.VMEM)
HBM = pl.BlockSpec(memory_space=pltpu.HBM)


def pack(short, k, v, av_t):
    half = 2 * WIDTH

    def chosen(array, first):
        return jnp.where(first, array[:, :half], array[:, half:])

    def stacked(first):
        pieces = [chosen(k, first), chosen(v, first)]
        return [piece[:, h * WIDTH : (h + 1) * WIDTH] for piece in pieces for h in range(2)]

    sel = jnp.concatenate(stacked(short == 0) + [av_t], axis=0)
    oth = jnp.concatenate(stacked(short == 1), axis=0)
    return sel, oth


HALF_SCRATCH = [pltpu.VMEM((ROWS, HALF_COLUMNS), bf16), pltpu.SemaphoreType.DMA((2,))]


def attend_short(place, aq_t, sel, one, q, grad):
    return pl.pallas_call(
        short_kernel,
        in_specs=[SMEM] + [VMEM] * 5,
        out_specs=[HBM, VMEM, VMEM, VMEM],
        out_shape=[
            shape(q.shape),
            shape((HALF_ADAPTER_ROWS, WIDTH)),
            shape((UNIT, WIDTH)),
            shape((UNIT, WIDTH)),
        ],
        scratch_shapes=HALF_SCRATCH,
        compiler_params=PARAMS,
        cost_estimate=pl.CostEstimate(flops=700_000_000, bytes_accessed=3_000_000, transcendentals=0),
        name="short",
    )(place, aq_t, sel, one, q, grad)


def attend_long(place, aq_t, sel, oth, one, other, two, three, ads, backs, q, grad, dq):
    return pl.pallas_call(
        long_kernel,
        in_specs=[SMEM] + [VMEM] * 11 + [HBM],
        out_specs=[HBM] + [VMEM] * 5,
        out_shape=[
            shape(q.shape),
            shape((ADAPTER_ROWS, WIDTH)),
            shape((UNIT, WIDTH)),
            shape((2 * UNIT, WIDTH)),
            shape((UNIT, WIDTH)),
            shape((UNIT, WIDTH)),
        ],
        scratch_shapes=HALF_SCRATCH,
        input_output_aliases={12: 0},
        compiler_params=PARAMS,
        cost_estimate=pl.CostEstimate(flops=1_400_000_000, bytes_accessed=4_000_000, transcendentals=0),
        name="long",
    )(place, aq_t, sel, oth, one, other, two, three, ads, backs, q, grad, dq)


def key_sums(place, short, long, r1, r2, r3):
    out = shape((ROWS, KEY_VALUE_HEADS * WIDTH))
    return pl.pallas_call(
        key_sum_kernel,
        in_specs=[SMEM] + [VMEM] * 5,
        out_specs=[VMEM, VMEM],
        out_shape=[out, out],
        compiler_params=PARAMS,
        cost_estimate=pl.CostEstimate(flops=SUM_FLOPS, bytes_accessed=2_000_000, transcendentals=0),
        name="key_sums",
    )(place, short, long, r1, r2, r3)


def adapter_out(total):
    return pl.pallas_call(
        adapter_kernel,
        in_specs=[VMEM],
        out_specs=[VMEM, VMEM],
        out_shape=[
            shape((RANK, QUERY_HEAD_COUNT * WIDTH), f32),
            shape((RANK, KEY_VALUE_HEADS * WIDTH), f32),
        ],
        compiler_params=PARAMS,
        name="adapter_out",
    )(total)


def copies_to_all(block, axes):
    size = lax.axis_size(axes)
    return lax.all_to_all(jnp.broadcast_to(block[None], (size,) + block.shape), axes, 0, 0)


def summed(pieces):
    return jnp.sum(pieces.astype(f32), axis=0).astype(bf16)


def sum_over_all(part):
    size = lax.axis_size(NEAR)
    mine = summed(lax.all_to_all(part.reshape(size, part.shape[0] // size, WIDTH), NEAR, 0, 0))
    mine = summed(copies_to_all(mine, FAR))
    return copies_to_all(mine, NEAR).reshape(part.shape)


def body(queries, keys, values, output_gradient, adapter_query_down, adapter_value_down):
    position = lax.axis_index(CTX) % GROUP_DEVS
    place = jnp.stack([position // 2, position % 2]).astype(jnp.int32)
    q, grad, aq_t = queries[0], output_gradient[0], adapter_query_down[0].T
    sel, oth = pack(position // 2, keys[0], values[0], adapter_value_down[0].T)
    one = passed_along(sel, 1)
    two = passed_along(sel, 2)
    three = passed_along(one, 2, range(1, CTX_SIZE, 2))
    other = passed_along(oth, 1, range(0, CTX_SIZE, 2))
    dq, ads, own_short, backs = attend_short(place, aq_t, sel, one, q, grad)
    dq, part, own_long, r1, r2, r3 = attend_long(
        place, aq_t, sel, oth, one, other, two, three, ads, backs, q, grad, dq
    )
    r1 = passed_along(r1, -1)
    r2 = passed_along(r2, -2)
    r3 = passed_along(r3, -3, range(1, CTX_SIZE, 2))
    dk, dv = key_sums(place, own_short, own_long, r1, r2, r3)
    total = sum_over_all(part)
    adapter_q, adapter_v = adapter_out(total)
    return dq[None], dk[None], dv[None], adapter_q, adapter_v


def solution(mesh):
    split = Mesh(mesh.devices.reshape(SIZES), AXES)
    tokens = P(DP, CTX, None)
    return jax.shard_map(
        body,
        mesh=split,
        in_specs=(tokens,) * 6,
        out_specs=(tokens, tokens, tokens, P(), P()),
        check_vma=False,
    )
```

time: 96.1 us -> 89.3 us (0.929)
  blocking collectives: 11.1 us -> 0 us
  starting transfers between devices: 46.6 us -> 56.4 us
  waiting for transfers between devices: 19.8 us -> 16.2 us
  local copies, waits for them, and re-layouts: 6.3 us -> 3.94 us
  other arithmetic: 0.15 us -> 1.19 us
    all_to_all x1 -> x0, blocking collectives: 11.1 us -> none  [copies_to_all(): lax.all_to_all(jnp.broadcast_to(block[None], (size,) + block.shape), axes...]
    ppermute x7, waiting for transfers between devices: 13.2 us -> 6.3 us  [passed_along(): lax.ppermute(block, CTX, [(i, (i + distance) % CTX_SIZE) for i in senders])]
    all_to_all x1 -> x2, starting transfers between devices: 10.6 us -> 16.3 us  [copies_to_all(): lax.all_to_all(jnp.broadcast_to(block[None], (size,) + block.shape), axes...]
    all_to_all x1 -> x2, waiting for transfers between devices: 4.31 us -> 8.51 us  [copies_to_all(): lax.all_to_all(jnp.broadcast_to(block[None], (size,) + block.shape), axes...]
    all_to_all x1, starting transfers between devices: 9.04 us -> 13.1 us  [sum_over_all(): lax.all_to_all(part.reshape(size, part.shape[0] // size, WIDTH), NEAR, 0, 0)]
    unnamed x14 -> x10, local copies, waits for them, and re-layouts: 4.87 us -> 1.87 us
    select_n x0 -> x1, other arithmetic: none -> 1.04 us  [chosen(): return jnp.where(first, array[:, :half], array[:, half:])]
  transfers between devices with their start and end apart: 9 -> 10, of which waited for: 6 -> 5; matrix products, arithmetic and copies ran while one was open for 1% -> 2% of each run, Pallas kernels for 3% -> 5%
where the time goes in v3:
time: 89.3 us; the launch traced here: 88.7 us
  starting transfers between devices  56.4 us (63%)
  waiting for transfers between devices  16.2 us (18%)
  Pallas kernels  10.1 us (11%)
  local copies, waits for them, and re-layouts  3.94 us (4%)
  other arithmetic  1.19 us (1%)
    ppermute x7, starting transfers between devices, passed_along(): lax.ppermute(block, CTX, [(i, (i + distance) % CTX_SIZE) for i in senders])  27 us
    all_to_all x2, starting transfers between devices, copies_to_all(): lax.all_to_all(jnp.broadcast_to(block[None], (size,) + block.shape), axes...  16.3 us
    all_to_all x1, starting transfers between devices, sum_over_all(): lax.all_to_all(part.reshape(size, part.shape[0] // size, WIDTH), NEAR, 0, 0)  13.1 us
    all_to_all x2, waiting for transfers between devices, copies_to_all(): lax.all_to_all(jnp.broadcast_to(block[None], (size,) + block.shape), axes...  8.51 us
    ppermute x7, waiting for transfers between devices, passed_along(): lax.ppermute(block, CTX, [(i, (i + distance) % CTX_SIZE) for i in senders])  6.3 us
    pallas_call x1, Pallas kernels, attend_long(): pl.pallas_call(long_kernel, in_specs=[SMEM] + [VMEM] * 11 + [HBM], out_sp...  5.36 us
    pallas_call x1, Pallas kernels, attend_short(): pl.pallas_call(short_kernel, in_specs=[SMEM] + [VMEM] * 5, out_specs=[HBM...  2.67 us
    unnamed x10, local copies, waits for them, and re-layouts  1.87 us
  transfers between devices with their start and end apart: 10, of which 5 were waited for; matrix products, arithmetic and copies ran while one was open for 2% of the time, Pallas kernels for 5%

profile of v3, /device:TPU:1, one launch (start us, length us, event | category | flops | bytes accessed | tf_op | source)
XLA Modules:
  0.0 88.7 jit_solution(12853288200201763103)
XLA Ops:
  0.7 1.0 %broadcast_select_fusion = (bf16[128,256]{1,0:T(8,128)(2,1)S(1)}, bf16[128,256]{1,0:T(8,128)(2,1)S(1)}, bf16[128,256]{1,0:T(8,128)(2,1)S(1)}, bf16[128,256]{1,0:T(8,128)(2,1)S(1)}) fusion(pred[]{:T(512)S(6)} %eq.10, bf16[128,512]{1,0:T(8,128)(2,1)} %bitcast.25, pred[]{:T(512)S(6)} %eq.9, bf16[128,512]{1,0:T(8,128)(2,1)} %bitcast.26), kind=kLoop, calls=%fused_computation.1 | loop fusion | flops 131072 | bytes 524290 | tf_op jit(solution)/shard_map/jit(_where)/select_n | solution.py:225
  1.8 0.7 constant_dynamic-update-slice_fusion.sel_ref
  2.5 5.0 %collective-permute-start.2 = (bf16[528,128]{1,0:T(8,128)(2,1)S(1)}, bf16[528,128]{1,0:T(8,128)(2,1)S(1)}, u32[]{:S(2)}, u32[]{:S(2)}) collective-permute-start(bf16[528,128]{1,0:T(8,128)(2,1)S(1)} %constant_dynamic-update-slice_fusion.sel_ref), channel_id=1, source_target_pairs={{0,16},{8,24},{16,32},{24,40},{32,48},{40,56},{48,64},{56,72},{64,... | collective-permute-start | bytes 405512 | tf_op jit(solution)/shard_map/ppermute | solution.py:209
  7.5 3.2 %collective-permute-start = (bf16[528,128]{1,0:T(8,128)(2,1)S(1)}, bf16[528,128]{1,0:T(8,128)(2,1)S(1)}, u32[]{:S(2)}, u32[]{:S(2)}) collective-permute-start(bf16[528,128]{1,0:T(8,128)(2,1)S(1)} %constant_dynamic-update-slice_fusion.sel_ref), channel_id=1, source_target_pairs={{0,8},{8,16},{16,24},{24,32},{32,40},{40,48},{48,56},{56,64},{64,7... | collective-permute-start | bytes 405512 | tf_op jit(solution)/shard_map/ppermute | solution.py:209
  10.8 4.4 %collective-permute-start.1 = (bf16[512,128]{1,0:T(8,128)(2,1)S(1)}, bf16[512,128]{1,0:T(8,128)(2,1)S(1)}, u32[]{:S(2)}, u32[]{:S(2)}) collective-permute-start(bf16[512,128]{1,0:T(8,128)(2,1)S(1)} %pad_maximum_fusion.oth_ref), channel_id=1, source_target_pairs={{0,8},{16,24},{32,40},{48,56},{64,72},{80,88},{96,104},{112,120},{... | collective-permute-start | bytes 393224 | tf_op jit(solution)/shard_map/ppermute | solution.py:209
  15.2 3.9 %collective-permute-done.one_ref = bf16[528,128]{1,0:T(8,128)(2,1)S(1)} collective-permute-done((bf16[528,128]{1,0:T(8,128)(2,1)S(1)}, bf16[528,128]{1,0:T(8,128)(2,1)S(1)}, u32[]{:S(2)}, u32[]{:S(2)}) %collective-permute-start) | collective-permute-done | bytes 135200 | tf_op jit(solution)/shard_map/ppermute | solution.py:209
  19.1 0.7 collective-permute-start.3
  19.8 0.0 copy-start.2
  19.8 0.1 pad_add_fusion.place_ref
  19.9 0.6 copy-done.2
  20.5 1.2 %copy-done.1 = bf16[1,128,4096]{2,1,0:T(8,128)(2,1)S(1)} copy-done((bf16[1,128,4096]{2,1,0:T(8,128)(2,1)S(1)}, bf16[1,128,4096]{2,1,0:T(8,128)(2,1)}, u32[]{:S(2)}) %copy-start.1) | copy-done | bytes 1048600
  21.7 2.7 %short.1 = (bf16[128,4096]{1,0:T(8,128)(2,1)}, bf16[288,128]{1,0:T(8,128)(2,1)S(1)}, bf16[512,128]{1,0:T(8,128)(2,1)S(1)}, bf16[512,128]{1,0:T(8,128)(2,1)S(1)}) custom-call(s32[2]{0:T(128)S(1)} %pad_add_fusion.place_ref, bf16[16,128]{1,0:T(8,128)(2,1)S(1)} %bitcast.23, bf16[528,128]{1,0:T(8,128)(2,1)S(1)} %constant_dynamic-update-slice_fusion.sel_ref, ...), custom_call_target="tpu_custom_call" | custom-call | flops 700000000 | bytes 3000000 | tf_op jit(solution)/shard_map/short/pallas_call | solution.py:240
  24.4 0.0 collective-permute-done.1.other_ref
  24.4 0.0 collective-permute-done.2.two_ref
  24.4 0.0 collective-permute-done.3.three_ref
  24.4 5.4 %long.1 = (bf16[128,4096]{1,0:T(8,128)(2,1)}, bf16[768,128]{1,0:T(8,128)(2,1)}, bf16[512,128]{1,0:T(8,128)(2,1)S(1)}, bf16[1024,128]{1,0:T(8,128)(2,1)S(1)}, bf1...) custom-call(s32[2]{0:T(128)S(1)} %pad_add_fusion.place_ref, ...), custom_call_target="tpu_custom_call", output_to_operand_aliasing={{0}: (12, {})} | custom-call | flops 1400000000 | bytes 4000000 | tf_op jit(solution)/shard_map/long/pallas_call | solution.py:258
  29.8 13.1 %all-to-all-start = ((bf16[32,24,128]{2,1,0:T(8,128)(2,1)}), bf16[32,24,128]{2,1,0:T(8,128)(2,1)S(1)}, u32[]{:S(2)}, u32[]{:S(2)}) async-start(bf16[32,24,128]{2,1,0:T(8,128)(2,1)} %bitcast.14), calls=%async_computation | async-start | bytes 393216 | tf_op jit(solution)/shard_map/all_to_all | solution.py:316
  42.9 6.5 %collective-permute-start.4 = (bf16[1024,128]{1,0:T(8,128)(2,1)S(1)}, bf16[1024,128]{1,0:T(8,128)(2,1)S(1)}, u32[]{:S(2)}, u32[]{:S(2)}) collective-permute-start(bf16[1024,128]{1,0:T(8,128)(2,1)S(1)} %get-tuple-element.25), channel_id=1, source_target_pairs={{0,504},{8,0},{16,8},{24,16},{32,24},{40,32},{48,40},{56,48},{64,5... | collective-permute-start | bytes 786440 | tf_op jit(solution)/shard_map/ppermute | solution.py:209
  49.3 1.4 %all-to-all-done = bf16[32,24,128]{2,1,0:T(8,128)(2,1)S(1)} async-done(((bf16[32,24,128]{2,1,0:T(8,128)(2,1)}), bf16[32,24,128]{2,1,0:T(8,128)(2,1)S(1)}, u32[]{:S(2)}, u32[]{:S(2)}) %all-to-all-start) | async-done | bytes 196640 | tf_op jit(solution)/shard_map/all_to_all | solution.py:316
  50.8 0.7 broadcast_in_dim.24
  51.4 11.0 %all-to-all-start.1 = ((bf16[16,24,128]{2,1,0:T(8,128)(2,1)}), bf16[16,24,128]{2,1,0:T(8,128)(2,1)S(1)}, u32[]{:S(2)}, u32[]{:S(2)}) async-start(bf16[16,24,128]{2,1,0:T(8,128)(2,1)} %broadcast_in_dim.24), calls=%async_computation.1 | async-start | bytes 196608 | tf_op jit(solution)/shard_map/all_to_all | solution.py:307
  62.5 5.9 %collective-permute-start.5 = (bf16[512,128]{1,0:T(8,128)(2,1)S(1)}, bf16[512,128]{1,0:T(8,128)(2,1)S(1)}, u32[]{:S(2)}, u32[]{:S(2)}) collective-permute-start(bf16[512,128]{1,0:T(8,128)(2,1)S(1)} %get-tuple-element.26), channel_id=1, source_target_pairs={{0,496},{8,504},{16,0},{24,8},{32,16},{40,24},{48,32},{56,40},{64,... | collective-permute-start | bytes 393224 | tf_op jit(solution)/shard_map/ppermute | solution.py:209
  68.4 1.3 %collective-permute-start.6 = (bf16[512,128]{1,0:T(8,128)(2,1)S(1)}, bf16[512,128]{1,0:T(8,128)(2,1)S(1)}, u32[]{:S(2)}, u32[]{:S(2)}) collective-permute-start(bf16[512,128]{1,0:T(8,128)(2,1)S(1)} %get-tuple-element.27), channel_id=1, source_target_pairs={{8,496},{24,0},{40,16},{56,32},{72,48},{88,64},{104,80},{120,96},{... | collective-permute-start | bytes 393224 | tf_op jit(solution)/shard_map/ppermute | solution.py:209
  69.7 4.3 %all-to-all-done.1 = bf16[16,24,128]{2,1,0:T(8,128)(2,1)S(1)} async-done(((bf16[16,24,128]{2,1,0:T(8,128)(2,1)}), bf16[16,24,128]{2,1,0:T(8,128)(2,1)S(1)}, u32[]{:S(2)}, u32[]{:S(2)}) %all-to-all-start.1) | async-done | bytes 98336 | tf_op jit(solution)/shard_map/all_to_all | solution.py:307
  74.0 0.7 broadcast_in_dim.25
  74.7 5.3 %all-to-all-start.2 = ((bf16[32,24,128]{2,1,0:T(8,128)(2,1)}), bf16[32,24,128]{2,1,0:T(8,128)(2,1)S(1)}, u32[]{:S(2)}, u32[]{:S(2)}) async-start(bf16[32,24,128]{2,1,0:T(8,128)(2,1)} %broadcast_in_dim.25), calls=%async_computation.2 | async-start | bytes 393216 | tf_op jit(solution)/shard_map/all_to_all | solution.py:307
  80.0 0.0 collective-permute-done.5.r2_ref
  80.0 2.4 %collective-permute-done.6.r3_ref = bf16[512,128]{1,0:T(8,128)(2,1)S(1)} collective-permute-done((bf16[512,128]{1,0:T(8,128)(2,1)S(1)}, bf16[512,128]{1,0:T(8,128)(2,1)S(1)}, u32[]{:S(2)}, u32[]{:S(2)}) %collective-permute-start.6) | collective-permute-done | bytes 131104 | tf_op jit(solution)/shard_map/ppermute | solution.py:209
  82.4 0.0 collective-permute-done.4.r1_ref
  82.4 1.4 %key_sums.1 = (bf16[128,512]{1,0:T(8,128)(2,1)}, bf16[128,512]{1,0:T(8,128)(2,1)}) custom-call(s32[2]{0:T(128)S(1)} %pad_add_fusion.place_ref, bf16[512,128]{1,0:T(8,128)(2,1)S(1)} %get-tuple-element.23.short_ref, bf16[512,128]{1,0:T(8,128)(2,1)S(1)} %get-tuple-element.24.long_ref, bf16[1024,128]{1,0:T(8,128)(2,1)S(1)} %collective-permute-done.4.r1_ref, ...), custom_call_target="tpu_custom_call" | custom-call | flops 20000000000 | bytes 2000000 | tf_op jit(solution)/shard_map/key_sums/pallas_call | solution.py:280
  83.7 4.2 %all-to-all-done.2 = bf16[32,24,128]{2,1,0:T(8,128)(2,1)S(1)} async-done(((bf16[32,24,128]{2,1,0:T(8,128)(2,1)}), bf16[32,24,128]{2,1,0:T(8,128)(2,1)S(1)}, u32[]{:S(2)}, u32[]{:S(2)}) %all-to-all-start.2) | async-done | bytes 196640 | tf_op jit(solution)/shard_map/all_to_all | solution.py:307
  87.9 0.7 adapter_out.1
  (12 shorter events, 0.1 us)
Async XLA Ops:
  0.6 19.3 %copy-start = (bf16[1,128,4096]{2,1,0:T(8,128)(2,1)S(1)}, bf16[1,128,4096]{2,1,0:T(8,128)(2,1)}, u32[]{:S(2)}) copy-start(bf16[1,128,4096]{2,1,0:T(8,128)(2,1)} %param.6) | copy-start | bytes 3145732
  2.5 21.9 %collective-permute-start.2 = (bf16[528,128]{1,0:T(8,128)(2,1)S(1)}, bf16[528,128]{1,0:T(8,128)(2,1)S(1)}, u32[]{:S(2)}, u32[]{:S(2)}) collective-permute-start(bf16[528,128]{1,0:T(8,128)(2,1)S(1)} %constant_dynamic-update-slice_fusion.sel_ref), channel_id=1, source_target_pairs={{0,16},{8,24},{16,32},{24,40},{32,48},{40,56},{48,64},{56,72},{64,... | collective-permute-start | bytes 405512 | tf_op jit(solution)/shard_map/ppermute | solution.py:209
  7.5 11.6 %collective-permute-start = (bf16[528,128]{1,0:T(8,128)(2,1)S(1)}, bf16[528,128]{1,0:T(8,128)(2,1)S(1)}, u32[]{:S(2)}, u32[]{:S(2)}) collective-permute-start(bf16[528,128]{1,0:T(8,128)(2,1)S(1)} %constant_dynamic-update-slice_fusion.sel_ref), channel_id=1, source_target_pairs={{0,8},{8,16},{16,24},{24,32},{32,40},{40,48},{48,56},{56,64},{64,7... | collective-permute-start | bytes 405512 | tf_op jit(solution)/shard_map/ppermute | solution.py:209
  10.8 13.6 %collective-permute-start.1 = (bf16[512,128]{1,0:T(8,128)(2,1)S(1)}, bf16[512,128]{1,0:T(8,128)(2,1)S(1)}, u32[]{:S(2)}, u32[]{:S(2)}) collective-permute-start(bf16[512,128]{1,0:T(8,128)(2,1)S(1)} %pad_maximum_fusion.oth_ref), channel_id=1, source_target_pairs={{0,8},{16,24},{32,40},{48,56},{64,72},{80,88},{96,104},{112,120},{... | collective-permute-start | bytes 393224 | tf_op jit(solution)/shard_map/ppermute | solution.py:209
  19.1 5.3 %collective-permute-start.3 = (bf16[528,128]{1,0:T(8,128)(2,1)S(1)}, bf16[528,128]{1,0:T(8,128)(2,1)S(1)}, u32[]{:S(2)}, u32[]{:S(2)}) collective-permute-start(bf16[528,128]{1,0:T(8,128)(2,1)S(1)} %collective-permute-done.one_ref), channel_id=1, source_target_pairs={{8,24},{24,40},{40,56},{56,72},{72,88},{88,104},{104,120},{120,136... | collective-permute-start | bytes 405512 | tf_op jit(solution)/shard_map/ppermute | solution.py:209
  19.8 0.7 copy-start.2
  20.5 1.2 %copy-start.1 = (bf16[1,128,4096]{2,1,0:T(8,128)(2,1)S(1)}, bf16[1,128,4096]{2,1,0:T(8,128)(2,1)}, u32[]{:S(2)}) copy-start(bf16[1,128,4096]{2,1,0:T(8,128)(2,1)} %param.9) | copy-start | bytes 3145732
  29.8 20.9 %all-to-all-start = ((bf16[32,24,128]{2,1,0:T(8,128)(2,1)}), bf16[32,24,128]{2,1,0:T(8,128)(2,1)S(1)}, u32[]{:S(2)}, u32[]{:S(2)}) async-start(bf16[32,24,128]{2,1,0:T(8,128)(2,1)} %bitcast.14), calls=%async_computation | async-start | bytes 393216 | tf_op jit(solution)/shard_map/all_to_all | solution.py:316
  42.9 39.5 %collective-permute-start.4 = (bf16[1024,128]{1,0:T(8,128)(2,1)S(1)}, bf16[1024,128]{1,0:T(8,128)(2,1)S(1)}, u32[]{:S(2)}, u32[]{:S(2)}) collective-permute-start(bf16[1024,128]{1,0:T(8,128)(2,1)S(1)} %get-tuple-element.25), channel_id=1, source_target_pairs={{0,504},{8,0},{16,8},{24,16},{32,24},{40,32},{48,40},{56,48},{64,5... | collective-permute-start | bytes 786440 | tf_op jit(solution)/shard_map/ppermute | solution.py:209
  51.4 22.6 %all-to-all-start.1 = ((bf16[16,24,128]{2,1,0:T(8,128)(2,1)}), bf16[16,24,128]{2,1,0:T(8,128)(2,1)S(1)}, u32[]{:S(2)}, u32[]{:S(2)}) async-start(bf16[16,24,128]{2,1,0:T(8,128)(2,1)} %broadcast_in_dim.24), calls=%async_computation.1 | async-start | bytes 196608 | tf_op jit(solution)/shard_map/all_to_all | solution.py:307
  62.5 17.5 %collective-permute-start.5 = (bf16[512,128]{1,0:T(8,128)(2,1)S(1)}, bf16[512,128]{1,0:T(8,128)(2,1)S(1)}, u32[]{:S(2)}, u32[]{:S(2)}) collective-permute-start(bf16[512,128]{1,0:T(8,128)(2,1)S(1)} %get-tuple-element.26), channel_id=1, source_target_pairs={{0,496},{8,504},{16,0},{24,8},{32,16},{40,24},{48,32},{56,40},{64,... | collective-permute-start | bytes 393224 | tf_op jit(solution)/shard_map/ppermute | solution.py:209
  68.4 14.0 %collective-permute-start.6 = (bf16[512,128]{1,0:T(8,128)(2,1)S(1)}, bf16[512,128]{1,0:T(8,128)(2,1)S(1)}, u32[]{:S(2)}, u32[]{:S(2)}) collective-permute-start(bf16[512,128]{1,0:T(8,128)(2,1)S(1)} %get-tuple-element.27), channel_id=1, source_target_pairs={{8,496},{24,0},{40,16},{56,32},{72,48},{88,64},{104,80},{120,96},{... | collective-permute-start | bytes 393224 | tf_op jit(solution)/shard_map/ppermute | solution.py:209
  74.7 13.2 %all-to-all-start.2 = ((bf16[32,24,128]{2,1,0:T(8,128)(2,1)}), bf16[32,24,128]{2,1,0:T(8,128)(2,1)S(1)}, u32[]{:S(2)}, u32[]{:S(2)}) async-start(bf16[32,24,128]{2,1,0:T(8,128)(2,1)} %broadcast_in_dim.25), calls=%async_computation.2 | async-start | bytes 393216 | tf_op jit(solution)/shard_map/all_to_all | solution.py:307

commit v4 on v3

--- a/solution.py
+++ b/solution.py
@@ -39,11 +39,16 @@
     return lax.dot_general(a, b, dims, preferred_element_type=f32)
 
 
+def group_place():
+    position = lax.axis_index(CTX) % GROUP_DEVS
+    return position // 2, position % 2
+
+
 def head_columns(head):
     return pl.ds(pl.multiple_of(head * WIDTH, WIDTH), WIDTH)
 
 
-def attend_head(q_wide, g_wide, put_dq, keys, values, av_t, aq_t):
+def attend_head(q_wide, g_wide, keys, values, av_t, aq_t):
     count = len(keys)
     key_all = jnp.concatenate(keys, axis=0) if count > 1 else keys[0]
     value_all = jnp.concatenate(values, axis=0) if count > 1 else values[0]
@@ -65,37 +70,25 @@
     logit_grad = (probs * (score_grad - delta)).astype(bf16)
     dq_t = (dot(key_all.T, logit_grad, NN) * SOFTMAX_SCALE).astype(bf16)
     dq = jnp.concatenate([dq_t[:, h].T for h in heads], axis=1)
-    put_dq(dq)
     dv = dot(probs.astype(bf16), grad, NN).astype(bf16)
     dk = (dot(logit_grad, q, NN) * SOFTMAX_SCALE).astype(bf16)
     av_all = jnp.concatenate(av_t, axis=1) if count > 1 else av_t[0]
-    return dk, dv, dot(aq_t, dq, NN).astype(bf16), dot(av_all, dv, NN).astype(bf16)
-
-
-def attend_half(half, q_ref, g_ref, dq_hbm, dq_ref, sems, variants, aq_t, put_adapter, put_value):
+    return dq, dk, dv, dot(aq_t, dq, NN).astype(bf16), dot(av_all, dv, NN).astype(bf16)
+
+
+def attend_half(half, q_ref, g_ref, dq_ref, variants, aq_t, put_adapter, put_value):
     def columns(g):
         return pl.ds(pl.multiple_of(half * HALF_COLUMNS + g * HEAD_COLUMNS, WIDTH), HEAD_COLUMNS)
-
-    copies = [
-        pltpu.make_async_copy(
-            dq_ref.at[:, pl.ds(g * HEAD_COLUMNS, HEAD_COLUMNS)], dq_hbm.at[:, columns(g)], sems.at[g]
-        )
-        for g in range(2)
-    ]
 
     def go(blocks, av_refs, outs):
         for g in range(2):
             keys = [ref[g * ROWS : (g + 1) * ROWS, :] for ref in blocks]
             values = [ref[(2 + g) * ROWS : (3 + g) * ROWS, :] for ref in blocks]
             av_t = [ref[UNIT:SEL_ROWS, :] for ref in av_refs]
-
-            def put_dq(dq, g=g):
-                dq_ref[:, g * HEAD_COLUMNS : (g + 1) * HEAD_COLUMNS] = dq
-                copies[g].start()
-
-            dk, dv, ad_q, ad_v = attend_head(
-                q_ref[:, columns(g)], g_ref[:, columns(g)], put_dq, keys, values, av_t, aq_t
+            dq, dk, dv, ad_q, ad_v = attend_head(
+                q_ref[:, columns(g)], g_ref[:, columns(g)], keys, values, av_t, aq_t
             )
+            dq_ref[:, g * HEAD_COLUMNS : (g + 1) * HEAD_COLUMNS] = dq
             for h in range(PER_HEAD):
                 put_adapter(g * PER_HEAD + h, ad_q[:, h * WIDTH : (h + 1) * WIDTH])
             put_value(g, ad_v)
@@ -106,14 +99,10 @@
 
     for condition, *rest in variants:
         pl.when(condition)(lambda rest=rest: go(*rest))
-    copies[0].wait()
-    copies[1].wait()
-
-
-def short_kernel(
-    place_ref, aq_ref, sel_ref, one_ref, q_ref, g_ref, dq_hbm, ad_ref, own_ref, back_ref, dq_ref, sems
-):
-    odd = place_ref[1]
+
+
+def short_kernel(aq_ref, sel_ref, one_ref, q_ref, g_ref, dq_ref, ad_ref, own_ref, back_ref):
+    short, odd = group_place()
 
     def put_adapter(h, value):
         ad_ref[h * RANK : (h + 1) * RANK, :] = value
@@ -125,15 +114,14 @@
         (odd == 0, [sel_ref], [sel_ref], [(own_ref, 0)]),
         (odd == 1, [sel_ref, one_ref], [sel_ref, one_ref], [(own_ref, 0), (back_ref, 0)]),
     ]
-    attend_half(place_ref[0], q_ref, g_ref, dq_hbm, dq_ref, sems, variants, aq_ref[...], put_adapter, put_value)
+    attend_half(short, q_ref, g_ref, dq_ref, variants, aq_ref[...], put_adapter, put_value)
 
 
 def long_kernel(
-    place_ref, aq_ref, sel_ref, oth_ref, one_ref, other_ref, two_ref, three_ref, ads_ref, backs_ref, q_ref, g_ref, dq_in,
-    dq_hbm, ad_ref, own_ref, r1_ref, r2_ref, r3_ref, dq_ref, sems,
+    aq_ref, sel_ref, oth_ref, one_ref, other_ref, two_ref, three_ref, ads_ref, backs_ref, q_ref, g_ref,
+    dq_ref, ad_ref, own_ref, r1_ref, r2_ref, r3_ref,
 ):
-    short = place_ref[0]
-    odd = place_ref[1]
+    short, odd = group_place()
     long = 1 - short
     n = HALF_HEADS * RANK
 
@@ -157,7 +145,7 @@
             [(own_ref, 0), (r1_ref, UNIT), (r2_ref, 0), (r3_ref, 0)],
         ),
     ]
-    attend_half(long, q_ref, g_ref, dq_hbm, dq_ref, sems, variants, aq_ref[...], put_adapter, put_value)
+    attend_half(long, q_ref, g_ref, dq_ref, variants, aq_ref[...], put_adapter, put_value)
     ad_ref[2 * n + 4 * RANK :, :] = jnp.zeros((ADAPTER_ROWS - 2 * n - 4 * RANK, WIDTH), bf16)
     ad_ref[pl.ds(pl.multiple_of(short * n, RANK), n), :] = ads_ref[:n, :]
     ad_ref[pl.ds(pl.multiple_of(2 * n + short * 2 * RANK, RANK), 2 * RANK), :] = ads_ref[n:, :]
@@ -171,9 +159,19 @@
         r1_ref[:UNIT, :] = backs_ref[...]
 
 
-def key_sum_kernel(place_ref, short_ref, long_ref, r1_ref, r2_ref, r3_ref, dk_ref, dv_ref):
-    short = place_ref[0]
-    even = place_ref[1] == 0
+def gradients_kernel(
+    dq_short_ref, dq_long_ref, short_ref, long_ref, r1_ref, r2_ref, r3_ref, dq_hbm, dk_ref, dv_ref, sems
+):
+    short, odd = group_place()
+    even = odd == 0
+
+    def half_out(ref, half, sem):
+        columns = pl.ds(pl.multiple_of(half * HALF_COLUMNS, WIDTH), HALF_COLUMNS)
+        return pltpu.make_async_copy(ref, dq_hbm.at[:, columns], sem)
+
+    copies = [half_out(dq_short_ref, short, sems.at[0]), half_out(dq_long_ref, 1 - short, sems.at[1])]
+    for copy in copies:
+        copy.start()
     for part, ref in ((0, dk_ref), (1, dv_ref)):
         for h in range(2):
             base = (part * 2 + h) * ROWS
@@ -185,6 +183,8 @@
             other = r1_ref[UNIT + base : UNIT + base + ROWS, :].astype(f32)
             total = long_ref[rows, :].astype(f32) + jnp.where(even, other, 0.0)
             ref[:, head_columns((1 - short) * 2 + h)] = total.astype(bf16)
+    for copy in copies:
+        copy.wait()
 
 
 def adapter_kernel(sum_ref, aq_ref, av_ref):
@@ -201,10 +201,6 @@
     return jax.ShapeDtypeStruct(dims, kind)
 
 
-def whole(dims):
-    return pl.BlockSpec(dims, lambda *_: (0,) * len(dims))
-
-
 def passed_along(block, distance, senders=range(CTX_SIZE)):
     return lax.ppermute(block, CTX, [(i, (i + distance) % CTX_SIZE) for i in senders])
 
@@ -213,7 +209,6 @@
 PARAMS = pltpu.CompilerParams(vmem_limit_bytes=40 * 1024 * 1024)
 HEAD_COLUMNS = PER_HEAD * WIDTH
 HALF_COLUMNS = 2 * HEAD_COLUMNS
-SMEM = pl.BlockSpec(memory_space=pltpu.SMEM)
 VMEM = pl.BlockSpec(memory_space=pltpu.VMEM)
 HBM = pl.BlockSpec(memory_space=pltpu.HBM)
 
@@ -233,59 +228,54 @@
     return sel, oth
 
 
-HALF_SCRATCH = [pltpu.VMEM((ROWS, HALF_COLUMNS), bf16), pltpu.SemaphoreType.DMA((2,))]
-
-
-def attend_short(place, aq_t, sel, one, q, grad):
+def attend_short(*operands):
     return pl.pallas_call(
         short_kernel,
-        in_specs=[SMEM] + [VMEM] * 5,
-        out_specs=[HBM, VMEM, VMEM, VMEM],
+        in_specs=[VMEM] * 5,
+        out_specs=[VMEM] * 4,
         out_shape=[
-            shape(q.shape),
+            shape((ROWS, HALF_COLUMNS)),
             shape((HALF_ADAPTER_ROWS, WIDTH)),
             shape((UNIT, WIDTH)),
             shape((UNIT, WIDTH)),
         ],
-        scratch_shapes=HALF_SCRATCH,
         compiler_params=PARAMS,
         cost_estimate=pl.CostEstimate(flops=700_000_000, bytes_accessed=3_000_000, transcendentals=0),
         name="short",
-    )(place, aq_t, sel, one, q, grad)
-
-
-def attend_long(place, aq_t, sel, oth, one, other, two, three, ads, backs, q, grad, dq):
+    )(*operands)
+
+
+def attend_long(*operands):
     return pl.pallas_call(
         long_kernel,
-        in_specs=[SMEM] + [VMEM] * 11 + [HBM],
-        out_specs=[HBM] + [VMEM] * 5,
+        in_specs=[VMEM] * 11,
+        out_specs=[VMEM] * 6,
         out_shape=[
-            shape(q.shape),
+            shape((ROWS, HALF_COLUMNS)),
             shape((ADAPTER_ROWS, WIDTH)),
             shape((UNIT, WIDTH)),
             shape((2 * UNIT, WIDTH)),
             shape((UNIT, WIDTH)),
             shape((UNIT, WIDTH)),
         ],
-        scratch_shapes=HALF_SCRATCH,
-        input_output_aliases={12: 0},
         compiler_params=PARAMS,
         cost_estimate=pl.CostEstimate(flops=1_400_000_000, bytes_accessed=4_000_000, transcendentals=0),
         name="long",
-    )(place, aq_t, sel, oth, one, other, two, three, ads, backs, q, grad, dq)
-
-
-def key_sums(place, short, long, r1, r2, r3):
+    )(*operands)
+
+
+def gradients_out(*operands):
     out = shape((ROWS, KEY_VALUE_HEADS * WIDTH))
     return pl.pallas_call(
-        key_sum_kernel,
-        in_specs=[SMEM] + [VMEM] * 5,
-        out_specs=[VMEM, VMEM],
-        out_shape=[out, out],
+        gradients_kernel,
+        in_specs=[VMEM] * 7,
+        out_specs=[HBM, VMEM, VMEM],
+        out_shape=[shape((ROWS, 2 * HALF_COLUMNS)), out, out],
+        scratch_shapes=[pltpu.SemaphoreType.DMA((2,))],
         compiler_params=PARAMS,
         cost_estimate=pl.CostEstimate(flops=SUM_FLOPS, bytes_accessed=2_000_000, transcendentals=0),
-        name="key_sums",
-    )(place, short, long, r1, r2, r3)
+        name="gradients_out",
+    )(*operands)
 
 
 def adapter_out(total):
@@ -319,22 +309,21 @@
 
 
 def body(queries, keys, values, output_gradient, adapter_query_down, adapter_value_down):
-    position = lax.axis_index(CTX) % GROUP_DEVS
-    place = jnp.stack([position // 2, position % 2]).astype(jnp.int32)
     q, grad, aq_t = queries[0], output_gradient[0], adapter_query_down[0].T
-    sel, oth = pack(position // 2, keys[0], values[0], adapter_value_down[0].T)
+    sel, oth = pack(group_place()[0], keys[0], values[0], adapter_value_down[0].T)
     one = passed_along(sel, 1)
-    two = passed_along(sel, 2)
+    later_sel, later_oth = lax.optimization_barrier((sel, oth))
+    two = passed_along(later_sel, 2)
+    other = passed_along(later_oth, 1, range(0, CTX_SIZE, 2))
     three = passed_along(one, 2, range(1, CTX_SIZE, 2))
-    other = passed_along(oth, 1, range(0, CTX_SIZE, 2))
-    dq, ads, own_short, backs = attend_short(place, aq_t, sel, one, q, grad)
-    dq, part, own_long, r1, r2, r3 = attend_long(
-        place, aq_t, sel, oth, one, other, two, three, ads, backs, q, grad, dq
+    dq_short, ads, own_short, backs = attend_short(aq_t, sel, one, q, grad)
+    dq_long, part, own_long, r1, r2, r3 = attend_long(
+        aq_t, sel, oth, one, other, two, three, ads, backs, q, grad
     )
     r1 = passed_along(r1, -1)
     r2 = passed_along(r2, -2)
     r3 = passed_along(r3, -3, range(1, CTX_SIZE, 2))
-    dk, dv = key_sums(place, own_short, own_long, r1, r2, r3)
+    dq, dk, dv = gradients_out(dq_short, dq_long, own_short, own_long, r1, r2, r3)
     total = sum_over_all(part)
     adapter_q, adapter_v = adapter_out(total)
     return dq[None], dk[None], dv[None], adapter_q, adapter_v

time: 89.3 us -> 85.3 us (0.955)
  starting transfers between devices: 56.4 us -> 51.7 us
  waiting for transfers between devices: 16.2 us -> 19.5 us
  Pallas kernels: 10.1 us -> 8.18 us
    all_to_all x1, starting transfers between devices: 13.1 us -> 8.59 us  [sum_over_all(): lax.all_to_all(part.reshape(size, part.shape[0] // size, WIDTH), NEAR, 0, 0)]
    ppermute x7, waiting for transfers between devices: 6.3 us -> 10.5 us  [passed_along(): lax.ppermute(block, CTX, [(i, (i + distance) % CTX_SIZE) for i in senders])]
    pallas_call x3, Pallas kernels: 9.39 us -> 7.46 us  [the longest x1 4.23 us: attend_long(): pl.pallas_call(long_kernel, in_specs=[VMEM] * 11, out_specs=[VMEM] * 6, o...]
    ppermute x7, starting transfers between devices: 27 us -> 25.2 us  [passed_along(): lax.ppermute(block, CTX, [(i, (i + distance) % CTX_SIZE) for i in senders])]
    all_to_all x2, starting transfers between devices: 16.3 us -> 17.9 us  [copies_to_all(): lax.all_to_all(jnp.broadcast_to(block[None], (size,) + block.shape), axes...]
    unnamed x10 -> x12, local copies, waits for them, and re-layouts: 1.87 us -> 1.27 us
  transfers between devices with their start and end apart: 10 -> 10, of which waited for: 5 -> 6; matrix products, arithmetic and copies ran while one was open for 2% -> 2% of each run, Pallas kernels for 5% -> 4%
where the time goes in v4:
time: 85.3 us; the launch traced here: 84.7 us
  starting transfers between devices  51.7 us (61%)
  waiting for transfers between devices  19.5 us (23%)
  Pallas kernels  8.18 us (10%)
  local copies, waits for them, and re-layouts  3.34 us (4%)
  other arithmetic  1.11 us (1%)
  between operations  0.87 us (1%)
    ppermute x7, starting transfers between devices, passed_along(): lax.ppermute(block, CTX, [(i, (i + distance) % CTX_SIZE) for i in senders])  25.2 us
    all_to_all x2, starting transfers between devices, copies_to_all(): lax.all_to_all(jnp.broadcast_to(block[None], (size,) + block.shape), axes...  17.9 us
    ppermute x7, waiting for transfers between devices, passed_along(): lax.ppermute(block, CTX, [(i, (i + distance) % CTX_SIZE) for i in senders])  10.5 us
    all_to_all x1, starting transfers between devices, sum_over_all(): lax.all_to_all(part.reshape(size, part.shape[0] // size, WIDTH), NEAR, 0, 0)  8.59 us
    all_to_all x2, waiting for transfers between devices, copies_to_all(): lax.all_to_all(jnp.broadcast_to(block[None], (size,) + block.shape), axes...  8.15 us
    pallas_call x1, Pallas kernels, attend_long(): pl.pallas_call(long_kernel, in_specs=[VMEM] * 11, out_specs=[VMEM] * 6, o...  4.23 us
    pallas_call x1, Pallas kernels, gradients_out(): pl.pallas_call(gradients_kernel, in_specs=[VMEM] * 7, out_specs=[HBM, VME...  1.71 us
  transfers between devices with their start and end apart: 10, of which 6 were waited for; matrix products, arithmetic and copies ran while one was open for 2% of the time, Pallas kernels for 4%

profile of v4, /device:TPU:1, one launch (start us, length us, event | category | flops | bytes accessed | tf_op | source)
XLA Modules:
  0.0 84.7 jit_solution(9195136177197233794)
XLA Ops:
  0.6 0.0 copy-start
  0.7 1.0 %broadcast_select_fusion = (bf16[128,256]{1,0:T(8,128)(2,1)S(1)}, bf16[128,256]{1,0:T(8,128)(2,1)S(1)}, bf16[128,256]{1,0:T(8,128)(2,1)S(1)}, bf16[128,256]{1,0:T(8,128)(2,1)S(1)}) fusion(pred[]{:T(512)S(6)} %eq.9, bf16[128,512]{1,0:T(8,128)(2,1)} %bitcast.23, pred[]{:T(512)S(6)} %eq.8, bf16[128,512]{1,0:T(8,128)(2,1)} %bitcast.24), kind=kLoop, calls=%fused_computation.1 | loop fusion | flops 131072 | bytes 524290 | tf_op jit(solution)/shard_map/jit(_where)/select_n | solution.py:220
  1.8 0.7 constant_dynamic-update-slice_fusion.sel_ref
  2.5 4.0 %collective-permute-start = (bf16[528,128]{1,0:T(8,128)(2,1)S(1)}, bf16[528,128]{1,0:T(8,128)(2,1)S(1)}, u32[]{:S(2)}, u32[]{:S(2)}) collective-permute-start(bf16[528,128]{1,0:T(8,128)(2,1)S(1)} %constant_dynamic-update-slice_fusion.sel_ref), channel_id=1, source_target_pairs={{0,8},{8,16},{16,24},{24,32},{32,40},{40,48},{48,56},{56,64},{64,7... | collective-permute-start | bytes 405512 | tf_op jit(solution)/shard_map/ppermute | solution.py:205
  6.6 0.0 copy-start.3
  6.6 4.2 %collective-permute-start.2 = (bf16[528,128]{1,0:T(8,128)(2,1)S(1)}, bf16[528,128]{1,0:T(8,128)(2,1)S(1)}, u32[]{:S(2)}, u32[]{:S(2)}) collective-permute-start(bf16[528,128]{1,0:T(8,128)(2,1)S(1)} %constant_dynamic-update-slice_fusion.sel_ref), channel_id=1, source_target_pairs={{0,16},{8,24},{16,32},{24,40},{32,48},{40,56},{48,64},{56,72},{64,... | collective-permute-start | bytes 405512 | tf_op jit(solution)/shard_map/ppermute | solution.py:205
  10.8 4.0 %collective-permute-done.one_ref = bf16[528,128]{1,0:T(8,128)(2,1)S(1)} collective-permute-done((bf16[528,128]{1,0:T(8,128)(2,1)S(1)}, bf16[528,128]{1,0:T(8,128)(2,1)S(1)}, u32[]{:S(2)}, u32[]{:S(2)}) %collective-permute-start) | collective-permute-done | bytes 135200 | tf_op jit(solution)/shard_map/ppermute | solution.py:205
  14.8 0.7 collective-permute-start.3
  15.5 2.2 %collective-permute-start.1 = (bf16[512,128]{1,0:T(8,128)(2,1)S(1)}, bf16[512,128]{1,0:T(8,128)(2,1)S(1)}, u32[]{:S(2)}, u32[]{:S(2)}) collective-permute-start(bf16[512,128]{1,0:T(8,128)(2,1)S(1)} %pad_maximum_fusion.oth_ref), channel_id=1, source_target_pairs={{0,8},{16,24},{32,40},{48,56},{64,72},{80,88},{96,104},{112,120},{... | collective-permute-start | bytes 393224 | tf_op jit(solution)/shard_map/ppermute | solution.py:205
  17.7 0.0 copy-start.1
  17.7 1.2 %copy-done.1 = bf16[1,128,4096]{2,1,0:T(8,128)(2,1)S(1)} copy-done((bf16[1,128,4096]{2,1,0:T(8,128)(2,1)S(1)}, bf16[1,128,4096]{2,1,0:T(8,128)(2,1)}, u32[]{:S(2)}) %copy-start.1) | copy-done | bytes 1048600
  18.9 1.5 %short.1 = (bf16[128,2048]{1,0:T(8,128)(2,1)S(1)}, bf16[288,128]{1,0:T(8,128)(2,1)S(1)}, bf16[512,128]{1,0:T(8,128)(2,1)S(1)}, bf16[512,128]{1,0:T(8,128)(2,1)S(1)}) custom-call(bf16[16,128]{1,0:T(8,128)(2,1)S(1)} %bitcast.21, bf16[528,128]{1,0:T(8,128)(2,1)S(1)} %constant_dynamic-update-slice_fusion.sel_ref, ...), custom_call_target="tpu_custom_call" | custom-call | flops 700000000 | bytes 3000000 | tf_op jit(solution)/shard_map/short/pallas_call | solution.py:232
  20.4 4.1 %collective-permute-done.1.other_ref = bf16[512,128]{1,0:T(8,128)(2,1)S(1)} collective-permute-done((bf16[512,128]{1,0:T(8,128)(2,1)S(1)}, bf16[512,128]{1,0:T(8,128)(2,1)S(1)}, u32[]{:S(2)}, u32[]{:S(2)}) %collective-permute-start.1) | collective-permute-done | bytes 131104 | tf_op jit(solution)/shard_map/ppermute | solution.py:205
  24.5 0.0 collective-permute-done.2.two_ref
  24.5 0.0 collective-permute-done.3.three_ref
  24.5 4.2 %long.1 = (bf16[128,2048]{1,0:T(8,128)(2,1)S(1)}, bf16[768,128]{1,0:T(8,128)(2,1)}, bf16[512,128]{1,0:T(8,128)(2,1)S(1)}, bf16[1024,128]{1,0:T(8,128)(2,1)S(1)},...) custom-call(bf16[16,128]{1,0:T(8,128)(2,1)S(1)} %bitcast.22, ...), custom_call_target="tpu_custom_call" | custom-call | flops 1400000000 | bytes 4000000 | tf_op jit(solution)/shard_map/long/pallas_call | solution.py:249
  28.8 8.6 %all-to-all-start = ((bf16[32,24,128]{2,1,0:T(8,128)(2,1)}), bf16[32,24,128]{2,1,0:T(8,128)(2,1)S(1)}, u32[]{:S(2)}, u32[]{:S(2)}) async-start(bf16[32,24,128]{2,1,0:T(8,128)(2,1)} %bitcast.12), calls=%async_computation | async-start | bytes 393216 | tf_op jit(solution)/shard_map/all_to_all | solution.py:306
  37.4 6.9 %collective-permute-start.4 = (bf16[1024,128]{1,0:T(8,128)(2,1)S(1)}, bf16[1024,128]{1,0:T(8,128)(2,1)S(1)}, u32[]{:S(2)}, u32[]{:S(2)}) collective-permute-start(bf16[1024,128]{1,0:T(8,128)(2,1)S(1)} %get-tuple-element.30), channel_id=1, source_target_pairs={{0,504},{8,0},{16,8},{24,16},{32,24},{40,32},{48,40},{56,48},{64,5... | collective-permute-start | bytes 786440 | tf_op jit(solution)/shard_map/ppermute | solution.py:205
  44.3 0.9 %all-to-all-done = bf16[32,24,128]{2,1,0:T(8,128)(2,1)S(1)} async-done(((bf16[32,24,128]{2,1,0:T(8,128)(2,1)}), bf16[32,24,128]{2,1,0:T(8,128)(2,1)S(1)}, u32[]{:S(2)}, u32[]{:S(2)}) %all-to-all-start) | async-done | bytes 196640 | tf_op jit(solution)/shard_map/all_to_all | solution.py:306
  45.2 0.7 broadcast_in_dim.24
  45.9 12.6 %all-to-all-start.1 = ((bf16[16,24,128]{2,1,0:T(8,128)(2,1)}), bf16[16,24,128]{2,1,0:T(8,128)(2,1)S(1)}, u32[]{:S(2)}, u32[]{:S(2)}) async-start(bf16[16,24,128]{2,1,0:T(8,128)(2,1)} %broadcast_in_dim.24), calls=%async_computation.1 | async-start | bytes 196608 | tf_op jit(solution)/shard_map/all_to_all | solution.py:297
  58.5 5.9 %collective-permute-start.5 = (bf16[512,128]{1,0:T(8,128)(2,1)S(1)}, bf16[512,128]{1,0:T(8,128)(2,1)S(1)}, u32[]{:S(2)}, u32[]{:S(2)}) collective-permute-start(bf16[512,128]{1,0:T(8,128)(2,1)S(1)} %get-tuple-element.31), channel_id=1, source_target_pairs={{0,496},{8,504},{16,0},{24,8},{32,16},{40,24},{48,32},{56,40},{64,... | collective-permute-start | bytes 393224 | tf_op jit(solution)/shard_map/ppermute | solution.py:205
  64.4 1.3 %collective-permute-start.6 = (bf16[512,128]{1,0:T(8,128)(2,1)S(1)}, bf16[512,128]{1,0:T(8,128)(2,1)S(1)}, u32[]{:S(2)}, u32[]{:S(2)}) collective-permute-start(bf16[512,128]{1,0:T(8,128)(2,1)S(1)} %get-tuple-element.32), channel_id=1, source_target_pairs={{8,496},{24,0},{40,16},{56,32},{72,48},{88,64},{104,80},{120,96},{... | collective-permute-start | bytes 393224 | tf_op jit(solution)/shard_map/ppermute | solution.py:205
  65.7 4.3 %all-to-all-done.1 = bf16[16,24,128]{2,1,0:T(8,128)(2,1)S(1)} async-done(((bf16[16,24,128]{2,1,0:T(8,128)(2,1)}), bf16[16,24,128]{2,1,0:T(8,128)(2,1)S(1)}, u32[]{:S(2)}, u32[]{:S(2)}) %all-to-all-start.1) | async-done | bytes 98336 | tf_op jit(solution)/shard_map/all_to_all | solution.py:297
  70.0 0.7 broadcast_in_dim.25
  70.7 5.3 %all-to-all-start.2 = ((bf16[32,24,128]{2,1,0:T(8,128)(2,1)}), bf16[32,24,128]{2,1,0:T(8,128)(2,1)S(1)}, u32[]{:S(2)}, u32[]{:S(2)}) async-start(bf16[32,24,128]{2,1,0:T(8,128)(2,1)} %broadcast_in_dim.25), calls=%async_computation.2 | async-start | bytes 393216 | tf_op jit(solution)/shard_map/all_to_all | solution.py:297
  76.0 0.0 collective-permute-done.5.r2_ref
  76.0 2.4 %collective-permute-done.6.r3_ref = bf16[512,128]{1,0:T(8,128)(2,1)S(1)} collective-permute-done((bf16[512,128]{1,0:T(8,128)(2,1)S(1)}, bf16[512,128]{1,0:T(8,128)(2,1)S(1)}, u32[]{:S(2)}, u32[]{:S(2)}) %collective-permute-start.6) | collective-permute-done | bytes 131104 | tf_op jit(solution)/shard_map/ppermute | solution.py:205
  78.4 0.0 collective-permute-done.4.r1_ref
  78.4 1.7 %gradients_out.1 = (bf16[128,4096]{1,0:T(8,128)(2,1)}, bf16[128,512]{1,0:T(8,128)(2,1)}, bf16[128,512]{1,0:T(8,128)(2,1)}) custom-call(bf16[128,2048]{1,0:T(8,128)(2,1)S(1)} %get-tuple-element.22.dq_short_ref, bf16[128,2048]{1,0:T(8,128)(2,1)S(1)} %get-tuple-element.27.dq_long_ref, bf16[512,128]{1,0:T(8,128)(2,1)S(1)} %get-tuple-element.28.short_ref, ...), custom_call_target="tpu_custom_call" | custom-call | flops 20000000000 | bytes 2000000 | tf_op jit(solution)/shard_map/gradients_out/pallas_call | solution.py:269
  80.1 3.8 %all-to-all-done.2 = bf16[32,24,128]{2,1,0:T(8,128)(2,1)S(1)} async-done(((bf16[32,24,128]{2,1,0:T(8,128)(2,1)}), bf16[32,24,128]{2,1,0:T(8,128)(2,1)S(1)}, u32[]{:S(2)}, u32[]{:S(2)}) %all-to-all-start.2) | async-done | bytes 196640 | tf_op jit(solution)/shard_map/all_to_all | solution.py:297
  84.0 0.7 adapter_out.1
  (13 shorter events, 0.1 us)
Async XLA Ops:
  0.6 17.0 %copy-start = (bf16[1,128,4096]{2,1,0:T(8,128)(2,1)S(1)}, bf16[1,128,4096]{2,1,0:T(8,128)(2,1)}, u32[]{:S(2)}) copy-start(bf16[1,128,4096]{2,1,0:T(8,128)(2,1)} %param.6) | copy-start | bytes 3145732
  2.5 12.3 %collective-permute-start = (bf16[528,128]{1,0:T(8,128)(2,1)S(1)}, bf16[528,128]{1,0:T(8,128)(2,1)S(1)}, u32[]{:S(2)}, u32[]{:S(2)}) collective-permute-start(bf16[528,128]{1,0:T(8,128)(2,1)S(1)} %constant_dynamic-update-slice_fusion.sel_ref), channel_id=1, source_target_pairs={{0,8},{8,16},{16,24},{24,32},{32,40},{40,48},{48,56},{56,64},{64,7... | collective-permute-start | bytes 405512 | tf_op jit(solution)/shard_map/ppermute | solution.py:205
  6.6 11.1 %copy-start.3 = (bf16[1,128,16]{1,2,0:T(8,128)(2,1)S(1)}, bf16[1,128,16]{1,2,0:T(8,128)(2,1)}, u32[]{:S(2)}) copy-start(bf16[1,128,16]{1,2,0:T(8,128)(2,1)} %param.10) | copy-start | bytes 12292
  6.6 18.0 %collective-permute-start.2 = (bf16[528,128]{1,0:T(8,128)(2,1)S(1)}, bf16[528,128]{1,0:T(8,128)(2,1)S(1)}, u32[]{:S(2)}, u32[]{:S(2)}) collective-permute-start(bf16[528,128]{1,0:T(8,128)(2,1)S(1)} %constant_dynamic-update-slice_fusion.sel_ref), channel_id=1, source_target_pairs={{0,16},{8,24},{16,32},{24,40},{32,48},{40,56},{48,64},{56,72},{64,... | collective-permute-start | bytes 405512 | tf_op jit(solution)/shard_map/ppermute | solution.py:205
  14.8 9.7 %collective-permute-start.3 = (bf16[528,128]{1,0:T(8,128)(2,1)S(1)}, bf16[528,128]{1,0:T(8,128)(2,1)S(1)}, u32[]{:S(2)}, u32[]{:S(2)}) collective-permute-start(bf16[528,128]{1,0:T(8,128)(2,1)S(1)} %collective-permute-done.one_ref), channel_id=1, source_target_pairs={{8,24},{24,40},{40,56},{56,72},{72,88},{88,104},{104,120},{120,136... | collective-permute-start | bytes 405512 | tf_op jit(solution)/shard_map/ppermute | solution.py:205
  15.5 9.1 %collective-permute-start.1 = (bf16[512,128]{1,0:T(8,128)(2,1)S(1)}, bf16[512,128]{1,0:T(8,128)(2,1)S(1)}, u32[]{:S(2)}, u32[]{:S(2)}) collective-permute-start(bf16[512,128]{1,0:T(8,128)(2,1)S(1)} %pad_maximum_fusion.oth_ref), channel_id=1, source_target_pairs={{0,8},{16,24},{32,40},{48,56},{64,72},{80,88},{96,104},{112,120},{... | collective-permute-start | bytes 393224 | tf_op jit(solution)/shard_map/ppermute | solution.py:205
  17.7 1.2 %copy-start.1 = (bf16[1,128,4096]{2,1,0:T(8,128)(2,1)S(1)}, bf16[1,128,4096]{2,1,0:T(8,128)(2,1)}, u32[]{:S(2)}) copy-start(bf16[1,128,4096]{2,1,0:T(8,128)(2,1)} %param.9) | copy-start | bytes 3145732
  18.9 5.6 %copy-start.2 = (bf16[1,128,4096]{2,1,0:T(8,128)(2,1)S(1)}, bf16[1,128,4096]{2,1,0:T(8,128)(2,1)}, u32[]{:S(2)}) copy-start(bf16[1,128,4096]{2,1,0:T(8,128)(2,1)} %param.9) | copy-start | bytes 3145732
  28.8 16.4 %all-to-all-start = ((bf16[32,24,128]{2,1,0:T(8,128)(2,1)}), bf16[32,24,128]{2,1,0:T(8,128)(2,1)S(1)}, u32[]{:S(2)}, u32[]{:S(2)}) async-start(bf16[32,24,128]{2,1,0:T(8,128)(2,1)} %bitcast.12), calls=%async_computation | async-start | bytes 393216 | tf_op jit(solution)/shard_map/all_to_all | solution.py:306
  37.4 41.1 %collective-permute-start.4 = (bf16[1024,128]{1,0:T(8,128)(2,1)S(1)}, bf16[1024,128]{1,0:T(8,128)(2,1)S(1)}, u32[]{:S(2)}, u32[]{:S(2)}) collective-permute-start(bf16[1024,128]{1,0:T(8,128)(2,1)S(1)} %get-tuple-element.30), channel_id=1, source_target_pairs={{0,504},{8,0},{16,8},{24,16},{32,24},{40,32},{48,40},{56,48},{64,5... | collective-permute-start | bytes 786440 | tf_op jit(solution)/shard_map/ppermute | solution.py:205
  45.9 24.1 %all-to-all-start.1 = ((bf16[16,24,128]{2,1,0:T(8,128)(2,1)}), bf16[16,24,128]{2,1,0:T(8,128)(2,1)S(1)}, u32[]{:S(2)}, u32[]{:S(2)}) async-start(bf16[16,24,128]{2,1,0:T(8,128)(2,1)} %broadcast_in_dim.24), calls=%async_computation.1 | async-start | bytes 196608 | tf_op jit(solution)/shard_map/all_to_all | solution.py:297
  58.5 17.5 %collective-permute-start.5 = (bf16[512,128]{1,0:T(8,128)(2,1)S(1)}, bf16[512,128]{1,0:T(8,128)(2,1)S(1)}, u32[]{:S(2)}, u32[]{:S(2)}) collective-permute-start(bf16[512,128]{1,0:T(8,128)(2,1)S(1)} %get-tuple-element.31), channel_id=1, source_target_pairs={{0,496},{8,504},{16,0},{24,8},{32,16},{40,24},{48,32},{56,40},{64,... | collective-permute-start | bytes 393224 | tf_op jit(solution)/shard_map/ppermute | solution.py:205
  64.4 14.0 %collective-permute-start.6 = (bf16[512,128]{1,0:T(8,128)(2,1)S(1)}, bf16[512,128]{1,0:T(8,128)(2,1)S(1)}, u32[]{:S(2)}, u32[]{:S(2)}) collective-permute-start(bf16[512,128]{1,0:T(8,128)(2,1)S(1)} %get-tuple-element.32), channel_id=1, source_target_pairs={{8,496},{24,0},{40,16},{56,32},{72,48},{88,64},{104,80},{120,96},{... | collective-permute-start | bytes 393224 | tf_op jit(solution)/shard_map/ppermute | solution.py:205
  70.7 13.2 %all-to-all-start.2 = ((bf16[32,24,128]{2,1,0:T(8,128)(2,1)}), bf16[32,24,128]{2,1,0:T(8,128)(2,1)S(1)}, u32[]{:S(2)}, u32[]{:S(2)}) async-start(bf16[32,24,128]{2,1,0:T(8,128)(2,1)} %broadcast_in_dim.25), calls=%async_computation.2 | async-start | bytes 393216 | tf_op jit(solution)/shard_map/all_to_all | solution.py:297

commit v5 on v4

--- a/solution.py
+++ b/solution.py
@@ -101,7 +101,7 @@
         pl.when(condition)(lambda rest=rest: go(*rest))
 
 
-def short_kernel(aq_ref, sel_ref, one_ref, q_ref, g_ref, dq_ref, ad_ref, own_ref, back_ref):
+def short_kernel(aq_ref, sel_ref, one_ref, _, q_ref, g_ref, dq_ref, ad_ref, own_ref, back_ref):
     short, odd = group_place()
 
     def put_adapter(h, value):
@@ -231,7 +231,7 @@
 def attend_short(*operands):
     return pl.pallas_call(
         short_kernel,
-        in_specs=[VMEM] * 5,
+        in_specs=[VMEM] * 6,
         out_specs=[VMEM] * 4,
         out_shape=[
             shape((ROWS, HALF_COLUMNS)),
@@ -312,11 +312,10 @@
     q, grad, aq_t = queries[0], output_gradient[0], adapter_query_down[0].T
     sel, oth = pack(group_place()[0], keys[0], values[0], adapter_value_down[0].T)
     one = passed_along(sel, 1)
-    later_sel, later_oth = lax.optimization_barrier((sel, oth))
-    two = passed_along(later_sel, 2)
-    other = passed_along(later_oth, 1, range(0, CTX_SIZE, 2))
+    other = passed_along(oth, 1, range(0, CTX_SIZE, 2))
+    two = passed_along(one, 1)
     three = passed_along(one, 2, range(1, CTX_SIZE, 2))
-    dq_short, ads, own_short, backs = attend_short(aq_t, sel, one, q, grad)
+    dq_short, ads, own_short, backs = attend_short(aq_t, sel, one, other, q, grad)
     dq_long, part, own_long, r1, r2, r3 = attend_long(
         aq_t, sel, oth, one, other, two, three, ads, backs, q, grad
     )

time: 85.3 us -> 85.2 us (level)
    all_to_all x2, starting transfers between devices: 17.9 us -> 13.8 us  [copies_to_all(): lax.all_to_all(jnp.broadcast_to(block[None], (size,) + block.shape), axes...]
    all_to_all x1, starting transfers between devices: 8.59 us -> 12.3 us  [sum_over_all(): lax.all_to_all(part.reshape(size, part.shape[0] // size, WIDTH), NEAR, 0, 0)]
    ppermute x7, waiting for transfers between devices: 10.5 us -> 12 us  [passed_along(): lax.ppermute(block, CTX, [(i, (i + distance) % CTX_SIZE) for i in senders])]
    all_to_all x1, waiting for transfers between devices: 0.9 us -> 0.01 us  [sum_over_all(): lax.all_to_all(part.reshape(size, part.shape[0] // size, WIDTH), NEAR, 0, 0)]
  transfers between devices with their start and end apart: 10 -> 10, of which waited for: 6 -> 5; matrix products, arithmetic and copies ran while one was open for 2% -> 2% of each run, Pallas kernels for 4% -> 4%
where the time goes in v5:
time: 85.2 us; the launch traced here: 84.6 us
  starting transfers between devices  51 us (60%)
  waiting for transfers between devices  20.1 us (24%)
  Pallas kernels  8.19 us (10%)
  local copies, waits for them, and re-layouts  3.34 us (4%)
  other arithmetic  1.11 us (1%)
  between operations  0.89 us (1%)
    ppermute x7, starting transfers between devices, passed_along(): lax.ppermute(block, CTX, [(i, (i + distance) % CTX_SIZE) for i in senders])  24.8 us
    all_to_all x2, starting transfers between devices, copies_to_all(): lax.all_to_all(jnp.broadcast_to(block[None], (size,) + block.shape), axes...  13.8 us
    all_to_all x1, starting transfers between devices, sum_over_all(): lax.all_to_all(part.reshape(size, part.shape[0] // size, WIDTH), NEAR, 0, 0)  12.3 us
    ppermute x7, waiting for transfers between devices, passed_along(): lax.ppermute(block, CTX, [(i, (i + distance) % CTX_SIZE) for i in senders])  12 us
    all_to_all x2, waiting for transfers between devices, copies_to_all(): lax.all_to_all(jnp.broadcast_to(block[None], (size,) + block.shape), axes...  8.15 us
    pallas_call x1, Pallas kernels, attend_long(): pl.pallas_call(long_kernel, in_specs=[VMEM] * 11, out_specs=[VMEM] * 6, o...  4.22 us
    pallas_call x1, Pallas kernels, gradients_out(): pl.pallas_call(gradients_kernel, in_specs=[VMEM] * 7, out_specs=[HBM, VME...  1.71 us
  transfers between devices with their start and end apart: 10, of which 5 were waited for; matrix products, arithmetic and copies ran while one was open for 2% of the time, Pallas kernels for 4%

profile of v5, /device:TPU:1, one launch (start us, length us, event | category | flops | bytes accessed | tf_op | source)
XLA Modules:
  0.0 84.6 jit_solution(12079918924733700347)
XLA Ops:
  0.6 0.0 copy-start
  0.7 1.0 %broadcast_select_fusion = (bf16[128,256]{1,0:T(8,128)(2,1)S(1)}, bf16[128,256]{1,0:T(8,128)(2,1)S(1)}, bf16[128,256]{1,0:T(8,128)(2,1)S(1)}, bf16[128,256]{1,0:T(8,128)(2,1)S(1)}) fusion(pred[]{:T(512)S(6)} %eq.9, bf16[128,512]{1,0:T(8,128)(2,1)} %bitcast.23, pred[]{:T(512)S(6)} %eq.8, bf16[128,512]{1,0:T(8,128)(2,1)} %bitcast.24), kind=kLoop, calls=%fused_computation.1 | loop fusion | flops 131072 | bytes 524290 | tf_op jit(solution)/shard_map/jit(_where)/select_n | solution.py:220
  1.8 0.7 constant_dynamic-update-slice_fusion.sel_ref
  2.5 4.0 %collective-permute-start = (bf16[528,128]{1,0:T(8,128)(2,1)S(1)}, bf16[528,128]{1,0:T(8,128)(2,1)S(1)}, u32[]{:S(2)}, u32[]{:S(2)}) collective-permute-start(bf16[528,128]{1,0:T(8,128)(2,1)S(1)} %constant_dynamic-update-slice_fusion.sel_ref), channel_id=1, source_target_pairs={{0,8},{8,16},{16,24},{24,32},{32,40},{40,48},{48,56},{56,64},{64,7... | collective-permute-start | bytes 405512 | tf_op jit(solution)/shard_map/ppermute | solution.py:205
  6.6 0.0 copy-start.3
  6.6 3.2 %collective-permute-start.1 = (bf16[512,128]{1,0:T(8,128)(2,1)S(1)}, bf16[512,128]{1,0:T(8,128)(2,1)S(1)}, u32[]{:S(2)}, u32[]{:S(2)}) collective-permute-start(bf16[512,128]{1,0:T(8,128)(2,1)S(1)} %pad_maximum_fusion.oth_ref), channel_id=1, source_target_pairs={{0,8},{16,24},{32,40},{48,56},{64,72},{80,88},{96,104},{112,120},{... | collective-permute-start | bytes 393224 | tf_op jit(solution)/shard_map/ppermute | solution.py:205
  9.8 5.0 %collective-permute-done.one_ref = bf16[528,128]{1,0:T(8,128)(2,1)S(1)} collective-permute-done((bf16[528,128]{1,0:T(8,128)(2,1)S(1)}, bf16[528,128]{1,0:T(8,128)(2,1)S(1)}, u32[]{:S(2)}, u32[]{:S(2)}) %collective-permute-start) | collective-permute-done | bytes 135200 | tf_op jit(solution)/shard_map/ppermute | solution.py:205
  14.8 1.9 %collective-permute-start.2 = (bf16[528,128]{1,0:T(8,128)(2,1)S(1)}, bf16[528,128]{1,0:T(8,128)(2,1)S(1)}, u32[]{:S(2)}, u32[]{:S(2)}) collective-permute-start(bf16[528,128]{1,0:T(8,128)(2,1)S(1)} %collective-permute-done.one_ref), channel_id=1, source_target_pairs={{0,8},{8,16},{16,24},{24,32},{32,40},{40,48},{48,56},{56,64},{64,7... | collective-permute-start | bytes 405512 | tf_op jit(solution)/shard_map/ppermute | solution.py:205
  16.7 0.7 collective-permute-start.3
  17.4 0.0 collective-permute-done.1._.other_ref
  17.4 0.0 copy-start.1
  17.4 1.2 %copy-done.1 = bf16[1,128,4096]{2,1,0:T(8,128)(2,1)S(1)} copy-done((bf16[1,128,4096]{2,1,0:T(8,128)(2,1)S(1)}, bf16[1,128,4096]{2,1,0:T(8,128)(2,1)}, u32[]{:S(2)}) %copy-start.1) | copy-done | bytes 1048600
  18.6 1.5 %short.1 = (bf16[128,2048]{1,0:T(8,128)(2,1)S(1)}, bf16[288,128]{1,0:T(8,128)(2,1)S(1)}, bf16[512,128]{1,0:T(8,128)(2,1)S(1)}, bf16[512,128]{1,0:T(8,128)(2,1)S(1)}) custom-call(bf16[16,128]{1,0:T(8,128)(2,1)S(1)} %bitcast.21, bf16[528,128]{1,0:T(8,128)(2,1)S(1)} %constant_dynamic-update-slice_fusion.sel_ref, ...), custom_call_target="tpu_custom_call" | custom-call | flops 700000000 | bytes 3000000 | tf_op jit(solution)/shard_map/short/pallas_call | solution.py:232
  20.2 4.6 %collective-permute-done.2.two_ref = bf16[528,128]{1,0:T(8,128)(2,1)S(1)} collective-permute-done((bf16[528,128]{1,0:T(8,128)(2,1)S(1)}, bf16[528,128]{1,0:T(8,128)(2,1)S(1)}, u32[]{:S(2)}, u32[]{:S(2)}) %collective-permute-start.2) | collective-permute-done | bytes 135200 | tf_op jit(solution)/shard_map/ppermute | solution.py:205
  24.8 0.0 collective-permute-done.3.three_ref
  24.8 4.2 %long.1 = (bf16[128,2048]{1,0:T(8,128)(2,1)S(1)}, bf16[768,128]{1,0:T(8,128)(2,1)}, bf16[512,128]{1,0:T(8,128)(2,1)S(1)}, bf16[1024,128]{1,0:T(8,128)(2,1)S(1)},...) custom-call(bf16[16,128]{1,0:T(8,128)(2,1)S(1)} %bitcast.22, ...), custom_call_target="tpu_custom_call" | custom-call | flops 1400000000 | bytes 4000000 | tf_op jit(solution)/shard_map/long/pallas_call | solution.py:249
  29.0 12.3 %all-to-all-start = ((bf16[32,24,128]{2,1,0:T(8,128)(2,1)}), bf16[32,24,128]{2,1,0:T(8,128)(2,1)S(1)}, u32[]{:S(2)}, u32[]{:S(2)}) async-start(bf16[32,24,128]{2,1,0:T(8,128)(2,1)} %bitcast.12), calls=%async_computation | async-start | bytes 393216 | tf_op jit(solution)/shard_map/all_to_all | solution.py:306
  41.3 7.8 %collective-permute-start.4 = (bf16[1024,128]{1,0:T(8,128)(2,1)S(1)}, bf16[1024,128]{1,0:T(8,128)(2,1)S(1)}, u32[]{:S(2)}, u32[]{:S(2)}) collective-permute-start(bf16[1024,128]{1,0:T(8,128)(2,1)S(1)} %get-tuple-element.26), channel_id=1, source_target_pairs={{0,504},{8,0},{16,8},{24,16},{32,24},{40,32},{48,40},{56,48},{64,5... | collective-permute-start | bytes 786440 | tf_op jit(solution)/shard_map/ppermute | solution.py:205
  49.1 0.0 all-to-all-done
  49.2 0.7 broadcast_in_dim.24
  49.9 8.5 %all-to-all-start.1 = ((bf16[16,24,128]{2,1,0:T(8,128)(2,1)}), bf16[16,24,128]{2,1,0:T(8,128)(2,1)S(1)}, u32[]{:S(2)}, u32[]{:S(2)}) async-start(bf16[16,24,128]{2,1,0:T(8,128)(2,1)} %broadcast_in_dim.24), calls=%async_computation.1 | async-start | bytes 196608 | tf_op jit(solution)/shard_map/all_to_all | solution.py:297
  58.4 5.9 %collective-permute-start.5 = (bf16[512,128]{1,0:T(8,128)(2,1)S(1)}, bf16[512,128]{1,0:T(8,128)(2,1)S(1)}, u32[]{:S(2)}, u32[]{:S(2)}) collective-permute-start(bf16[512,128]{1,0:T(8,128)(2,1)S(1)} %get-tuple-element.27), channel_id=1, source_target_pairs={{0,496},{8,504},{16,0},{24,8},{32,16},{40,24},{48,32},{56,40},{64,... | collective-permute-start | bytes 393224 | tf_op jit(solution)/shard_map/ppermute | solution.py:205
  64.3 1.3 %collective-permute-start.6 = (bf16[512,128]{1,0:T(8,128)(2,1)S(1)}, bf16[512,128]{1,0:T(8,128)(2,1)S(1)}, u32[]{:S(2)}, u32[]{:S(2)}) collective-permute-start(bf16[512,128]{1,0:T(8,128)(2,1)S(1)} %get-tuple-element.28), channel_id=1, source_target_pairs={{8,496},{24,0},{40,16},{56,32},{72,48},{88,64},{104,80},{120,96},{... | collective-permute-start | bytes 393224 | tf_op jit(solution)/shard_map/ppermute | solution.py:205
  65.6 4.3 %all-to-all-done.1 = bf16[16,24,128]{2,1,0:T(8,128)(2,1)S(1)} async-done(((bf16[16,24,128]{2,1,0:T(8,128)(2,1)}), bf16[16,24,128]{2,1,0:T(8,128)(2,1)S(1)}, u32[]{:S(2)}, u32[]{:S(2)}) %all-to-all-start.1) | async-done | bytes 98336 | tf_op jit(solution)/shard_map/all_to_all | solution.py:297
  70.0 0.7 broadcast_in_dim.25
  70.7 5.3 %all-to-all-start.2 = ((bf16[32,24,128]{2,1,0:T(8,128)(2,1)}), bf16[32,24,128]{2,1,0:T(8,128)(2,1)S(1)}, u32[]{:S(2)}, u32[]{:S(2)}) async-start(bf16[32,24,128]{2,1,0:T(8,128)(2,1)} %broadcast_in_dim.25), calls=%async_computation.2 | async-start | bytes 393216 | tf_op jit(solution)/shard_map/all_to_all | solution.py:297
  76.0 0.0 collective-permute-done.5.r2_ref
  76.0 2.4 %collective-permute-done.6.r3_ref = bf16[512,128]{1,0:T(8,128)(2,1)S(1)} collective-permute-done((bf16[512,128]{1,0:T(8,128)(2,1)S(1)}, bf16[512,128]{1,0:T(8,128)(2,1)S(1)}, u32[]{:S(2)}, u32[]{:S(2)}) %collective-permute-start.6) | collective-permute-done | bytes 131104 | tf_op jit(solution)/shard_map/ppermute | solution.py:205
  78.3 0.0 collective-permute-done.4.r1_ref
  78.4 1.7 %gradients_out.1 = (bf16[128,4096]{1,0:T(8,128)(2,1)}, bf16[128,512]{1,0:T(8,128)(2,1)}, bf16[128,512]{1,0:T(8,128)(2,1)}) custom-call(bf16[128,2048]{1,0:T(8,128)(2,1)S(1)} %get-tuple-element.20.dq_short_ref, bf16[128,2048]{1,0:T(8,128)(2,1)S(1)} %get-tuple-element.23.dq_long_ref, bf16[512,128]{1,0:T(8,128)(2,1)S(1)} %get-tuple-element.24.short_ref, ...), custom_call_target="tpu_custom_call" | custom-call | flops 20000000000 | bytes 2000000 | tf_op jit(solution)/shard_map/gradients_out/pallas_call | solution.py:269
  80.1 3.8 %all-to-all-done.2 = bf16[32,24,128]{2,1,0:T(8,128)(2,1)S(1)} async-done(((bf16[32,24,128]{2,1,0:T(8,128)(2,1)}), bf16[32,24,128]{2,1,0:T(8,128)(2,1)S(1)}, u32[]{:S(2)}, u32[]{:S(2)}) %all-to-all-start.2) | async-done | bytes 196640 | tf_op jit(solution)/shard_map/all_to_all | solution.py:297
  83.9 0.7 adapter_out.1
  (13 shorter events, 0.1 us)
Async XLA Ops:
  0.6 16.8 %copy-start = (bf16[1,128,4096]{2,1,0:T(8,128)(2,1)S(1)}, bf16[1,128,4096]{2,1,0:T(8,128)(2,1)}, u32[]{:S(2)}) copy-start(bf16[1,128,4096]{2,1,0:T(8,128)(2,1)} %param.6) | copy-start | bytes 3145732
  2.5 12.3 %collective-permute-start = (bf16[528,128]{1,0:T(8,128)(2,1)S(1)}, bf16[528,128]{1,0:T(8,128)(2,1)S(1)}, u32[]{:S(2)}, u32[]{:S(2)}) collective-permute-start(bf16[528,128]{1,0:T(8,128)(2,1)S(1)} %constant_dynamic-update-slice_fusion.sel_ref), channel_id=1, source_target_pairs={{0,8},{8,16},{16,24},{24,32},{32,40},{40,48},{48,56},{56,64},{64,7... | collective-permute-start | bytes 405512 | tf_op jit(solution)/shard_map/ppermute | solution.py:205
  6.6 10.8 %copy-start.3 = (bf16[1,128,16]{1,2,0:T(8,128)(2,1)S(1)}, bf16[1,128,16]{1,2,0:T(8,128)(2,1)}, u32[]{:S(2)}) copy-start(bf16[1,128,16]{1,2,0:T(8,128)(2,1)} %param.10) | copy-start | bytes 12292
  6.6 10.8 %collective-permute-start.1 = (bf16[512,128]{1,0:T(8,128)(2,1)S(1)}, bf16[512,128]{1,0:T(8,128)(2,1)S(1)}, u32[]{:S(2)}, u32[]{:S(2)}) collective-permute-start(bf16[512,128]{1,0:T(8,128)(2,1)S(1)} %pad_maximum_fusion.oth_ref), channel_id=1, source_target_pairs={{0,8},{16,24},{32,40},{48,56},{64,72},{80,88},{96,104},{112,120},{... | collective-permute-start | bytes 393224 | tf_op jit(solution)/shard_map/ppermute | solution.py:205
  14.8 10.0 %collective-permute-start.2 = (bf16[528,128]{1,0:T(8,128)(2,1)S(1)}, bf16[528,128]{1,0:T(8,128)(2,1)S(1)}, u32[]{:S(2)}, u32[]{:S(2)}) collective-permute-start(bf16[528,128]{1,0:T(8,128)(2,1)S(1)} %collective-permute-done.one_ref), channel_id=1, source_target_pairs={{0,8},{8,16},{16,24},{24,32},{32,40},{40,48},{48,56},{56,64},{64,7... | collective-permute-start | bytes 405512 | tf_op jit(solution)/shard_map/ppermute | solution.py:205
  16.7 8.0 %collective-permute-start.3 = (bf16[528,128]{1,0:T(8,128)(2,1)S(1)}, bf16[528,128]{1,0:T(8,128)(2,1)S(1)}, u32[]{:S(2)}, u32[]{:S(2)}) collective-permute-start(bf16[528,128]{1,0:T(8,128)(2,1)S(1)} %collective-permute-done.one_ref), channel_id=1, source_target_pairs={{8,24},{24,40},{40,56},{56,72},{72,88},{88,104},{104,120},{120,136... | collective-permute-start | bytes 405512 | tf_op jit(solution)/shard_map/ppermute | solution.py:205
  17.4 1.2 %copy-start.1 = (bf16[1,128,4096]{2,1,0:T(8,128)(2,1)S(1)}, bf16[1,128,4096]{2,1,0:T(8,128)(2,1)}, u32[]{:S(2)}) copy-start(bf16[1,128,4096]{2,1,0:T(8,128)(2,1)} %param.9) | copy-start | bytes 3145732
  18.6 6.1 %copy-start.2 = (bf16[1,128,4096]{2,1,0:T(8,128)(2,1)S(1)}, bf16[1,128,4096]{2,1,0:T(8,128)(2,1)}, u32[]{:S(2)}) copy-start(bf16[1,128,4096]{2,1,0:T(8,128)(2,1)} %param.9) | copy-start | bytes 3145732
  29.0 20.2 %all-to-all-start = ((bf16[32,24,128]{2,1,0:T(8,128)(2,1)}), bf16[32,24,128]{2,1,0:T(8,128)(2,1)S(1)}, u32[]{:S(2)}, u32[]{:S(2)}) async-start(bf16[32,24,128]{2,1,0:T(8,128)(2,1)} %bitcast.12), calls=%async_computation | async-start | bytes 393216 | tf_op jit(solution)/shard_map/all_to_all | solution.py:306
  41.3 37.0 %collective-permute-start.4 = (bf16[1024,128]{1,0:T(8,128)(2,1)S(1)}, bf16[1024,128]{1,0:T(8,128)(2,1)S(1)}, u32[]{:S(2)}, u32[]{:S(2)}) collective-permute-start(bf16[1024,128]{1,0:T(8,128)(2,1)S(1)} %get-tuple-element.26), channel_id=1, source_target_pairs={{0,504},{8,0},{16,8},{24,16},{32,24},{40,32},{48,40},{56,48},{64,5... | collective-permute-start | bytes 786440 | tf_op jit(solution)/shard_map/ppermute | solution.py:205
  49.9 20.1 %all-to-all-start.1 = ((bf16[16,24,128]{2,1,0:T(8,128)(2,1)}), bf16[16,24,128]{2,1,0:T(8,128)(2,1)S(1)}, u32[]{:S(2)}, u32[]{:S(2)}) async-start(bf16[16,24,128]{2,1,0:T(8,128)(2,1)} %broadcast_in_dim.24), calls=%async_computation.1 | async-start | bytes 196608 | tf_op jit(solution)/shard_map/all_to_all | solution.py:297
  58.4 17.5 %collective-permute-start.5 = (bf16[512,128]{1,0:T(8,128)(2,1)S(1)}, bf16[512,128]{1,0:T(8,128)(2,1)S(1)}, u32[]{:S(2)}, u32[]{:S(2)}) collective-permute-start(bf16[512,128]{1,0:T(8,128)(2,1)S(1)} %get-tuple-element.27), channel_id=1, source_target_pairs={{0,496},{8,504},{16,0},{24,8},{32,16},{40,24},{48,32},{56,40},{64,... | collective-permute-start | bytes 393224 | tf_op jit(solution)/shard_map/ppermute | solution.py:205
  64.3 14.0 %collective-permute-start.6 = (bf16[512,128]{1,0:T(8,128)(2,1)S(1)}, bf16[512,128]{1,0:T(8,128)(2,1)S(1)}, u32[]{:S(2)}, u32[]{:S(2)}) collective-permute-start(bf16[512,128]{1,0:T(8,128)(2,1)S(1)} %get-tuple-element.28), channel_id=1, source_target_pairs={{8,496},{24,0},{40,16},{56,32},{72,48},{88,64},{104,80},{120,96},{... | collective-permute-start | bytes 393224 | tf_op jit(solution)/shard_map/ppermute | solution.py:205
  70.7 13.2 %all-to-all-start.2 = ((bf16[32,24,128]{2,1,0:T(8,128)(2,1)}), bf16[32,24,128]{2,1,0:T(8,128)(2,1)S(1)}, u32[]{:S(2)}, u32[]{:S(2)}) async-start(bf16[32,24,128]{2,1,0:T(8,128)(2,1)} %broadcast_in_dim.25), calls=%async_computation.2 | async-start | bytes 393216 | tf_op jit(solution)/shard_map/all_to_all | solution.py:297

commit v6 on v5

--- a/solution.py
+++ b/solution.py
@@ -301,11 +301,12 @@
     return jnp.sum(pieces.astype(f32), axis=0).astype(bf16)
 
 
-def sum_over_all(part):
+def sum_over_all(part, beside):
     size = lax.axis_size(NEAR)
     mine = summed(lax.all_to_all(part.reshape(size, part.shape[0] // size, WIDTH), NEAR, 0, 0))
     mine = summed(copies_to_all(mine, FAR))
-    return copies_to_all(mine, NEAR).reshape(part.shape)
+    mine, beside = lax.optimization_barrier((mine, beside))
+    return copies_to_all(mine, NEAR).reshape(part.shape), beside
 
 
 def body(queries, keys, values, output_gradient, adapter_query_down, adapter_value_down):
@@ -313,8 +314,8 @@
     sel, oth = pack(group_place()[0], keys[0], values[0], adapter_value_down[0].T)
     one = passed_along(sel, 1)
     other = passed_along(oth, 1, range(0, CTX_SIZE, 2))
+    three = passed_along(one, 2, range(1, CTX_SIZE, 2))
     two = passed_along(one, 1)
-    three = passed_along(one, 2, range(1, CTX_SIZE, 2))
     dq_short, ads, own_short, backs = attend_short(aq_t, sel, one, other, q, grad)
     dq_long, part, own_long, r1, r2, r3 = attend_long(
         aq_t, sel, oth, one, other, two, three, ads, backs, q, grad
@@ -323,7 +324,7 @@
     r2 = passed_along(r2, -2)
     r3 = passed_along(r3, -3, range(1, CTX_SIZE, 2))
     dq, dk, dv = gradients_out(dq_short, dq_long, own_short, own_long, r1, r2, r3)
-    total = sum_over_all(part)
+    total, (dk, dv) = sum_over_all(part, (dk, dv))
     adapter_q, adapter_v = adapter_out(total)
     return dq[None], dk[None], dv[None], adapter_q, adapter_v
 

time: 85.2 us -> 87.7 us (1.029)
  blocking collectives: 0 us -> 16.8 us
  starting transfers between devices: 51 us -> 36.7 us
    all_to_all x0 -> x1, blocking collectives: none -> 16.8 us  [copies_to_all(): lax.all_to_all(jnp.broadcast_to(block[None], (size,) + block.shape), axes...]
    ppermute x7, starting transfers between devices: 24.8 us -> 18.7 us  [passed_along(): lax.ppermute(block, CTX, [(i, (i + distance) % CTX_SIZE) for i in senders])]
    all_to_all x2 -> x1, starting transfers between devices: 13.8 us -> 8.34 us  [copies_to_all(): lax.all_to_all(jnp.broadcast_to(block[None], (size,) + block.shape), axes...]
    all_to_all x1, starting transfers between devices: 12.3 us -> 9.61 us  [sum_over_all(): lax.all_to_all(part.reshape(size, part.shape[0] // size, WIDTH), NEAR, 0, 0)]
    all_to_all x2 -> x1, waiting for transfers between devices: 8.15 us -> 8.78 us  [copies_to_all(): lax.all_to_all(jnp.broadcast_to(block[None], (size,) + block.shape), axes...]
  transfers between devices with their start and end apart: 10 -> 9, of which waited for: 5 -> 4; matrix products, arithmetic and copies ran while one was open for 2% -> 1% of each run, Pallas kernels for 4% -> 4%
where the time goes in v6:
time: 87.7 us; the launch traced here: 87.1 us
  starting transfers between devices  36.7 us (42%)
  waiting for transfers between devices  20.8 us (24%)
  blocking collectives  16.8 us (19%)
  Pallas kernels  8.16 us (9%)
  local copies, waits for them, and re-layouts  2.66 us (3%)
  other arithmetic  1.11 us (1%)
  between operations  0.88 us (1%)
    ppermute x7, starting transfers between devices, passed_along(): lax.ppermute(block, CTX, [(i, (i + distance) % CTX_SIZE) for i in senders])  18.7 us
    all_to_all x1, blocking collectives, copies_to_all(): lax.all_to_all(jnp.broadcast_to(block[None], (size,) + block.shape), axes...  16.8 us
    ppermute x7, waiting for transfers between devices, passed_along(): lax.ppermute(block, CTX, [(i, (i + distance) % CTX_SIZE) for i in senders])  12 us
    all_to_all x1, starting transfers between devices, sum_over_all(): lax.all_to_all(part.reshape(size, part.shape[0] // size, WIDTH), NEAR, 0, 0)  9.61 us
    all_to_all x1, waiting for transfers between devices, copies_to_all(): lax.all_to_all(jnp.broadcast_to(block[None], (size,) + block.shape), axes...  8.78 us
    all_to_all x1, starting transfers between devices, copies_to_all(): lax.all_to_all(jnp.broadcast_to(block[None], (size,) + block.shape), axes...  8.34 us
    pallas_call x1, Pallas kernels, attend_long(): pl.pallas_call(long_kernel, in_specs=[VMEM] * 11, out_specs=[VMEM] * 6, o...  4.19 us
  transfers between devices with their start and end apart: 9, of which 4 were waited for; matrix products, arithmetic and copies ran while one was open for 1% of the time, Pallas kernels for 4%

profile of v6, /device:TPU:1, one launch (start us, length us, event | category | flops | bytes accessed | tf_op | source)
XLA Modules:
  0.0 87.1 jit_solution(12945603747195836927)
XLA Ops:
  0.6 0.0 copy-start
  0.7 1.0 %broadcast_select_fusion = (bf16[128,256]{1,0:T(8,128)(2,1)S(1)}, bf16[128,256]{1,0:T(8,128)(2,1)S(1)}, bf16[128,256]{1,0:T(8,128)(2,1)S(1)}, bf16[128,256]{1,0:T(8,128)(2,1)S(1)}) fusion(pred[]{:T(512)S(6)} %eq.9, bf16[128,512]{1,0:T(8,128)(2,1)} %bitcast.23, pred[]{:T(512)S(6)} %eq.8, bf16[128,512]{1,0:T(8,128)(2,1)} %bitcast.24), kind=kLoop, calls=%fused_computation.1 | loop fusion | flops 131072 | bytes 524290 | tf_op jit(solution)/shard_map/jit(_where)/select_n | solution.py:220
  1.8 0.7 constant_dynamic-update-slice_fusion.sel_ref
  2.5 4.0 %collective-permute-start = (bf16[528,128]{1,0:T(8,128)(2,1)S(1)}, bf16[528,128]{1,0:T(8,128)(2,1)S(1)}, u32[]{:S(2)}, u32[]{:S(2)}) collective-permute-start(bf16[528,128]{1,0:T(8,128)(2,1)S(1)} %constant_dynamic-update-slice_fusion.sel_ref), channel_id=1, source_target_pairs={{0,8},{8,16},{16,24},{24,32},{32,40},{40,48},{48,56},{56,64},{64,7... | collective-permute-start | bytes 405512 | tf_op jit(solution)/shard_map/ppermute | solution.py:205
  6.6 0.0 copy-start.3
  6.6 3.2 %collective-permute-start.1 = (bf16[512,128]{1,0:T(8,128)(2,1)S(1)}, bf16[512,128]{1,0:T(8,128)(2,1)S(1)}, u32[]{:S(2)}, u32[]{:S(2)}) collective-permute-start(bf16[512,128]{1,0:T(8,128)(2,1)S(1)} %pad_maximum_fusion.oth_ref), channel_id=1, source_target_pairs={{0,8},{16,24},{32,40},{48,56},{64,72},{80,88},{96,104},{112,120},{... | collective-permute-start | bytes 393224 | tf_op jit(solution)/shard_map/ppermute | solution.py:205
  9.8 5.0 %collective-permute-done.one_ref = bf16[528,128]{1,0:T(8,128)(2,1)S(1)} collective-permute-done((bf16[528,128]{1,0:T(8,128)(2,1)S(1)}, bf16[528,128]{1,0:T(8,128)(2,1)S(1)}, u32[]{:S(2)}, u32[]{:S(2)}) %collective-permute-start) | collective-permute-done | bytes 135200 | tf_op jit(solution)/shard_map/ppermute | solution.py:205
  14.8 0.7 collective-permute-start.3
  15.5 1.9 %collective-permute-start.2 = (bf16[528,128]{1,0:T(8,128)(2,1)S(1)}, bf16[528,128]{1,0:T(8,128)(2,1)S(1)}, u32[]{:S(2)}, u32[]{:S(2)}) collective-permute-start(bf16[528,128]{1,0:T(8,128)(2,1)S(1)} %collective-permute-done.one_ref), channel_id=1, source_target_pairs={{0,8},{8,16},{16,24},{24,32},{32,40},{40,48},{48,56},{56,64},{64,7... | collective-permute-start | bytes 405512 | tf_op jit(solution)/shard_map/ppermute | solution.py:205
  17.4 0.0 collective-permute-done.1._.other_ref
  17.4 0.0 copy-done
  17.4 0.0 copy-start.1
  17.4 1.2 %copy-done.1 = bf16[1,128,4096]{2,1,0:T(8,128)(2,1)S(1)} copy-done((bf16[1,128,4096]{2,1,0:T(8,128)(2,1)S(1)}, bf16[1,128,4096]{2,1,0:T(8,128)(2,1)}, u32[]{:S(2)}) %copy-start.1) | copy-done | bytes 1048600
  18.6 1.5 %short.1 = (bf16[128,2048]{1,0:T(8,128)(2,1)S(1)}, bf16[288,128]{1,0:T(8,128)(2,1)S(1)}, bf16[512,128]{1,0:T(8,128)(2,1)S(1)}, bf16[512,128]{1,0:T(8,128)(2,1)S(1)}) custom-call(bf16[16,128]{1,0:T(8,128)(2,1)S(1)} %bitcast.21, bf16[528,128]{1,0:T(8,128)(2,1)S(1)} %constant_dynamic-update-slice_fusion.sel_ref, ...), custom_call_target="tpu_custom_call" | custom-call | flops 700000000 | bytes 3000000 | tf_op jit(solution)/shard_map/short/pallas_call | solution.py:232
  20.2 0.0 collective-permute-done.3.three_ref
  20.2 6.0 %collective-permute-done.2.two_ref = bf16[528,128]{1,0:T(8,128)(2,1)S(1)} collective-permute-done((bf16[528,128]{1,0:T(8,128)(2,1)S(1)}, bf16[528,128]{1,0:T(8,128)(2,1)S(1)}, u32[]{:S(2)}, u32[]{:S(2)}) %collective-permute-start.2) | collective-permute-done | bytes 135200 | tf_op jit(solution)/shard_map/ppermute | solution.py:205
  26.2 0.0 copy-done.2
  26.2 4.2 %long.1 = (bf16[128,2048]{1,0:T(8,128)(2,1)S(1)}, bf16[768,128]{1,0:T(8,128)(2,1)}, bf16[512,128]{1,0:T(8,128)(2,1)S(1)}, bf16[1024,128]{1,0:T(8,128)(2,1)S(1)},...) custom-call(bf16[16,128]{1,0:T(8,128)(2,1)S(1)} %bitcast.22, ...), custom_call_target="tpu_custom_call" | custom-call | flops 1400000000 | bytes 4000000 | tf_op jit(solution)/shard_map/long/pallas_call | solution.py:249
  30.4 9.6 %all-to-all-start = ((bf16[32,24,128]{2,1,0:T(8,128)(2,1)}), bf16[32,24,128]{2,1,0:T(8,128)(2,1)S(1)}, u32[]{:S(2)}, u32[]{:S(2)}) async-start(bf16[32,24,128]{2,1,0:T(8,128)(2,1)} %bitcast.10), calls=%async_computation | async-start | bytes 393216 | tf_op jit(solution)/shard_map/all_to_all | solution.py:306
  40.0 5.7 %collective-permute-start.4 = (bf16[1024,128]{1,0:T(8,128)(2,1)S(1)}, bf16[1024,128]{1,0:T(8,128)(2,1)S(1)}, u32[]{:S(2)}, u32[]{:S(2)}) collective-permute-start(bf16[1024,128]{1,0:T(8,128)(2,1)S(1)} %get-tuple-element.29), channel_id=1, source_target_pairs={{0,504},{8,0},{16,8},{24,16},{32,24},{40,32},{48,40},{56,48},{64,5... | collective-permute-start | bytes 786440 | tf_op jit(solution)/shard_map/ppermute | solution.py:205
  45.8 1.9 %collective-permute-start.5 = (bf16[512,128]{1,0:T(8,128)(2,1)S(1)}, bf16[512,128]{1,0:T(8,128)(2,1)S(1)}, u32[]{:S(2)}, u32[]{:S(2)}) collective-permute-start(bf16[512,128]{1,0:T(8,128)(2,1)S(1)} %get-tuple-element.30), channel_id=1, source_target_pairs={{0,496},{8,504},{16,0},{24,8},{32,16},{40,24},{48,32},{56,40},{64,... | collective-permute-start | bytes 393224 | tf_op jit(solution)/shard_map/ppermute | solution.py:205
  47.7 1.3 %collective-permute-start.6 = (bf16[512,128]{1,0:T(8,128)(2,1)S(1)}, bf16[512,128]{1,0:T(8,128)(2,1)S(1)}, u32[]{:S(2)}, u32[]{:S(2)}) collective-permute-start(bf16[512,128]{1,0:T(8,128)(2,1)S(1)} %get-tuple-element.31), channel_id=1, source_target_pairs={{8,496},{24,0},{40,16},{56,32},{72,48},{88,64},{104,80},{120,96},{... | collective-permute-start | bytes 393224 | tf_op jit(solution)/shard_map/ppermute | solution.py:205
  49.0 0.0 all-to-all-done
  49.0 0.7 broadcast_in_dim.22
  49.7 8.3 %all-to-all-start.1 = ((bf16[16,24,128]{2,1,0:T(8,128)(2,1)}), bf16[16,24,128]{2,1,0:T(8,128)(2,1)S(1)}, u32[]{:S(2)}, u32[]{:S(2)}) async-start(bf16[16,24,128]{2,1,0:T(8,128)(2,1)} %broadcast_in_dim.22), calls=%async_computation.1 | async-start | bytes 196608 | tf_op jit(solution)/shard_map/all_to_all | solution.py:297
  58.0 1.0 %collective-permute-done.5.r2_ref = bf16[512,128]{1,0:T(8,128)(2,1)S(1)} collective-permute-done((bf16[512,128]{1,0:T(8,128)(2,1)S(1)}, bf16[512,128]{1,0:T(8,128)(2,1)S(1)}, u32[]{:S(2)}, u32[]{:S(2)}) %collective-permute-start.5) | collective-permute-done | bytes 131104 | tf_op jit(solution)/shard_map/ppermute | solution.py:205
  59.0 0.0 collective-permute-done.6.r3_ref
  59.0 0.0 collective-permute-done.4.r1_ref
  59.0 1.7 %gradients_out.1 = (bf16[128,4096]{1,0:T(8,128)(2,1)}, bf16[128,512]{1,0:T(8,128)(2,1)}, bf16[128,512]{1,0:T(8,128)(2,1)}) custom-call(bf16[128,2048]{1,0:T(8,128)(2,1)S(1)} %get-tuple-element.23.dq_short_ref, bf16[128,2048]{1,0:T(8,128)(2,1)S(1)} %get-tuple-element.26.dq_long_ref, bf16[512,128]{1,0:T(8,128)(2,1)S(1)} %get-tuple-element.27.short_ref, ...), custom_call_target="tpu_custom_call" | custom-call | flops 20000000000 | bytes 2000000 | tf_op jit(solution)/shard_map/gradients_out/pallas_call | solution.py:269
  60.7 8.8 %all-to-all-done.1 = bf16[16,24,128]{2,1,0:T(8,128)(2,1)S(1)} async-done(((bf16[16,24,128]{2,1,0:T(8,128)(2,1)}), bf16[16,24,128]{2,1,0:T(8,128)(2,1)S(1)}, u32[]{:S(2)}, u32[]{:S(2)}) %all-to-all-start.1) | async-done | bytes 98336 | tf_op jit(solution)/shard_map/all_to_all | solution.py:297
  69.6 16.8 %all_to_all.15 = bf16[32,24,128]{2,1,0:T(8,128)(2,1)S(1)} all-to-all(bf16[32,24,128]{2,1,0:T(8,128)(2,1)S(1)} %broadcast_in_dim.25), channel_id=1, replica_groups=mesh['x'=4,'zl'=2,'yh'=4,'yl'=2,'zh'=4,'core'=2] {'x','zl','yl','core'}, dimensions={0} | all-to-all | bytes 393216 | tf_op jit(solution)/shard_map/all_to_all | solution.py:297
  86.4 0.7 adapter_out.1
  (12 shorter events, 0.2 us)
Async XLA Ops:
  0.6 16.8 %copy-start = (bf16[1,128,4096]{2,1,0:T(8,128)(2,1)S(1)}, bf16[1,128,4096]{2,1,0:T(8,128)(2,1)}, u32[]{:S(2)}) copy-start(bf16[1,128,4096]{2,1,0:T(8,128)(2,1)} %param.6) | copy-start | bytes 3145732
  2.5 12.3 %collective-permute-start = (bf16[528,128]{1,0:T(8,128)(2,1)S(1)}, bf16[528,128]{1,0:T(8,128)(2,1)S(1)}, u32[]{:S(2)}, u32[]{:S(2)}) collective-permute-start(bf16[528,128]{1,0:T(8,128)(2,1)S(1)} %constant_dynamic-update-slice_fusion.sel_ref), channel_id=1, source_target_pairs={{0,8},{8,16},{16,24},{24,32},{32,40},{40,48},{48,56},{56,64},{64,7... | collective-permute-start | bytes 405512 | tf_op jit(solution)/shard_map/ppermute | solution.py:205
  6.6 10.8 %copy-start.3 = (bf16[1,128,16]{1,2,0:T(8,128)(2,1)S(1)}, bf16[1,128,16]{1,2,0:T(8,128)(2,1)}, u32[]{:S(2)}) copy-start(bf16[1,128,16]{1,2,0:T(8,128)(2,1)} %param.10) | copy-start | bytes 12292
  6.6 10.8 %collective-permute-start.1 = (bf16[512,128]{1,0:T(8,128)(2,1)S(1)}, bf16[512,128]{1,0:T(8,128)(2,1)S(1)}, u32[]{:S(2)}, u32[]{:S(2)}) collective-permute-start(bf16[512,128]{1,0:T(8,128)(2,1)S(1)} %pad_maximum_fusion.oth_ref), channel_id=1, source_target_pairs={{0,8},{16,24},{32,40},{48,56},{64,72},{80,88},{96,104},{112,120},{... | collective-permute-start | bytes 393224 | tf_op jit(solution)/shard_map/ppermute | solution.py:205
  14.8 5.4 %collective-permute-start.3 = (bf16[528,128]{1,0:T(8,128)(2,1)S(1)}, bf16[528,128]{1,0:T(8,128)(2,1)S(1)}, u32[]{:S(2)}, u32[]{:S(2)}) collective-permute-start(bf16[528,128]{1,0:T(8,128)(2,1)S(1)} %collective-permute-done.one_ref), channel_id=1, source_target_pairs={{8,24},{24,40},{40,56},{56,72},{72,88},{88,104},{104,120},{120,136... | collective-permute-start | bytes 405512 | tf_op jit(solution)/shard_map/ppermute | solution.py:205
  15.5 10.8 %collective-permute-start.2 = (bf16[528,128]{1,0:T(8,128)(2,1)S(1)}, bf16[528,128]{1,0:T(8,128)(2,1)S(1)}, u32[]{:S(2)}, u32[]{:S(2)}) collective-permute-start(bf16[528,128]{1,0:T(8,128)(2,1)S(1)} %collective-permute-done.one_ref), channel_id=1, source_target_pairs={{0,8},{8,16},{16,24},{24,32},{32,40},{40,48},{48,56},{56,64},{64,7... | collective-permute-start | bytes 405512 | tf_op jit(solution)/shard_map/ppermute | solution.py:205
  17.4 1.2 %copy-start.1 = (bf16[1,128,4096]{2,1,0:T(8,128)(2,1)S(1)}, bf16[1,128,4096]{2,1,0:T(8,128)(2,1)}, u32[]{:S(2)}) copy-start(bf16[1,128,4096]{2,1,0:T(8,128)(2,1)} %param.9) | copy-start | bytes 3145732
  18.6 7.6 %copy-start.2 = (bf16[1,128,4096]{2,1,0:T(8,128)(2,1)S(1)}, bf16[1,128,4096]{2,1,0:T(8,128)(2,1)}, u32[]{:S(2)}) copy-start(bf16[1,128,4096]{2,1,0:T(8,128)(2,1)} %param.9) | copy-start | bytes 3145732
  30.4 18.6 %all-to-all-start = ((bf16[32,24,128]{2,1,0:T(8,128)(2,1)}), bf16[32,24,128]{2,1,0:T(8,128)(2,1)S(1)}, u32[]{:S(2)}, u32[]{:S(2)}) async-start(bf16[32,24,128]{2,1,0:T(8,128)(2,1)} %bitcast.10), calls=%async_computation | async-start | bytes 393216 | tf_op jit(solution)/shard_map/all_to_all | solution.py:306
  40.0 19.0 %collective-permute-start.4 = (bf16[1024,128]{1,0:T(8,128)(2,1)S(1)}, bf16[1024,128]{1,0:T(8,128)(2,1)S(1)}, u32[]{:S(2)}, u32[]{:S(2)}) collective-permute-start(bf16[1024,128]{1,0:T(8,128)(2,1)S(1)} %get-tuple-element.29), channel_id=1, source_target_pairs={{0,504},{8,0},{16,8},{24,16},{32,24},{40,32},{48,40},{56,48},{64,5... | collective-permute-start | bytes 786440 | tf_op jit(solution)/shard_map/ppermute | solution.py:205
  45.8 13.2 %collective-permute-start.5 = (bf16[512,128]{1,0:T(8,128)(2,1)S(1)}, bf16[512,128]{1,0:T(8,128)(2,1)S(1)}, u32[]{:S(2)}, u32[]{:S(2)}) collective-permute-start(bf16[512,128]{1,0:T(8,128)(2,1)S(1)} %get-tuple-element.30), channel_id=1, source_target_pairs={{0,496},{8,504},{16,0},{24,8},{32,16},{40,24},{48,32},{56,40},{64,... | collective-permute-start | bytes 393224 | tf_op jit(solution)/shard_map/ppermute | solution.py:205
  47.7 11.3 %collective-permute-start.6 = (bf16[512,128]{1,0:T(8,128)(2,1)S(1)}, bf16[512,128]{1,0:T(8,128)(2,1)S(1)}, u32[]{:S(2)}, u32[]{:S(2)}) collective-permute-start(bf16[512,128]{1,0:T(8,128)(2,1)S(1)} %get-tuple-element.31), channel_id=1, source_target_pairs={{8,496},{24,0},{40,16},{56,32},{72,48},{88,64},{104,80},{120,96},{... | collective-permute-start | bytes 393224 | tf_op jit(solution)/shard_map/ppermute | solution.py:205
  49.7 19.8 %all-to-all-start.1 = ((bf16[16,24,128]{2,1,0:T(8,128)(2,1)}), bf16[16,24,128]{2,1,0:T(8,128)(2,1)S(1)}, u32[]{:S(2)}, u32[]{:S(2)}) async-start(bf16[16,24,128]{2,1,0:T(8,128)(2,1)} %broadcast_in_dim.22), calls=%async_computation.1 | async-start | bytes 196608 | tf_op jit(solution)/shard_map/all_to_all | solution.py:297

commit v7 on v5

--- a/solution.py
+++ b/solution.py
@@ -14,10 +14,10 @@
 ADAPTER_SCALE = 2.0
 SOFTMAX_SCALE = WIDTH ** (-0.5)
 LOG2E = 1.4426950408889634
+STRIP = ROWS
 PER_HEAD = QUERY_HEAD_COUNT // KEY_VALUE_HEADS
 HALF_HEADS = QUERY_HEAD_COUNT // 2
 UNIT = 4 * ROWS
-SEL_ROWS = UNIT + RANK
 ADAPTER_ROWS = 768
 HALF_ADAPTER_ROWS = (HALF_HEADS + 2) * RANK
 
@@ -48,32 +48,46 @@
     return pl.ds(pl.multiple_of(head * WIDTH, WIDTH), WIDTH)
 
 
-def attend_head(q_wide, g_wide, keys, values, av_t, aq_t):
-    count = len(keys)
-    key_all = jnp.concatenate(keys, axis=0) if count > 1 else keys[0]
-    value_all = jnp.concatenate(values, axis=0) if count > 1 else values[0]
-    rows = PER_HEAD * ROWS
-    allowed = lax.broadcasted_iota(jnp.int32, (ROWS, rows), 0) <= (
-        lax.broadcasted_iota(jnp.int32, (ROWS, rows), 1) % ROWS
+def stacked(wide):
+    return jnp.concatenate([wide[:, h * WIDTH : (h + 1) * WIDTH] for h in range(PER_HEAD)], axis=0)
+
+
+def joined(blocks, axis):
+    return jnp.concatenate(blocks, axis=axis) if len(blocks) > 1 else blocks[0]
+
+
+def logits(scores, score_grad):
+    columns = scores.shape[1]
+    allowed = lax.broadcasted_iota(jnp.int32, (ROWS, columns), 0) <= (
+        lax.broadcasted_iota(jnp.int32, (ROWS, columns), 1) % ROWS
     )
-    heads = [slice(h * WIDTH, (h + 1) * WIDTH) for h in range(PER_HEAD)]
-    q = jnp.concatenate([q_wide[:, h] for h in heads], axis=0)
-    grad = jnp.concatenate([g_wide[:, h] for h in heads], axis=0)
-    scores = dot(key_all, q, NT)
-    score_grad = dot(value_all, grad, NT)
     diagonal = jnp.where(allowed, scores[:ROWS], -1e30)
-    scores = jnp.concatenate([diagonal, scores[ROWS:]], axis=0) if count > 1 else diagonal
+    scores = joined([diagonal, scores[ROWS:]], 0) if scores.shape[0] > ROWS else diagonal
     top = jnp.max(scores, axis=0, keepdims=True)
     raised = jnp.exp2((scores - top) * (SOFTMAX_SCALE * LOG2E))
     probs = raised * (1.0 / jnp.sum(raised, axis=0, keepdims=True))
     delta = jnp.sum(probs * score_grad, axis=0, keepdims=True)
-    logit_grad = (probs * (score_grad - delta)).astype(bf16)
-    dq_t = (dot(key_all.T, logit_grad, NN) * SOFTMAX_SCALE).astype(bf16)
-    dq = jnp.concatenate([dq_t[:, h].T for h in heads], axis=1)
-    dv = dot(probs.astype(bf16), grad, NN).astype(bf16)
-    dk = (dot(logit_grad, q, NN) * SOFTMAX_SCALE).astype(bf16)
-    av_all = jnp.concatenate(av_t, axis=1) if count > 1 else av_t[0]
-    return dq, dk, dv, dot(aq_t, dq, NN).astype(bf16), dot(av_all, dv, NN).astype(bf16)
+    return probs.astype(bf16), (probs * (score_grad - delta)).astype(bf16)
+
+
+def attend(heads, aq_t):
+    ready = []
+    for q_wide, g_wide, keys, values, av_t in heads:
+        q, grad, key_all = stacked(q_wide), stacked(g_wide), joined(keys, 0)
+        ready.append((q, grad, key_all, dot(key_all, q, NT), dot(joined(values, 0), grad, NT), joined(av_t, 1)))
+    out = []
+    for q, grad, key_all, scores, score_grad, av_all in ready:
+        strips = [
+            logits(scores[:, c : c + STRIP], score_grad[:, c : c + STRIP])
+            for c in range(0, PER_HEAD * ROWS, STRIP)
+        ]
+        weights, logit_grad = joined([w for w, _ in strips], 1), joined([l for _, l in strips], 1)
+        dq_t = (dot(key_all.T, logit_grad, NN) * SOFTMAX_SCALE).astype(bf16)
+        dq = jnp.concatenate([dq_t[:, h * ROWS : (h + 1) * ROWS].T for h in range(PER_HEAD)], axis=1)
+        dv = dot(weights, grad, NN).astype(bf16)
+        dk = (dot(logit_grad, q, NN) * SOFTMAX_SCALE).astype(bf16)
+        out.append((dq, dk, dv, dot(aq_t, dq, NN).astype(bf16), dot(av_all, dv, NN).astype(bf16)))
+    return out
 
 
 def attend_half(half, q_ref, g_ref, dq_ref, variants, aq_t, put_adapter, put_value):
@@ -81,13 +95,13 @@
         return pl.ds(pl.multiple_of(half * HALF_COLUMNS + g * HEAD_COLUMNS, WIDTH), HEAD_COLUMNS)
 
     def go(blocks, av_refs, outs):
+        heads = []
         for g in range(2):
             keys = [ref[g * ROWS : (g + 1) * ROWS, :] for ref in blocks]
             values = [ref[(2 + g) * ROWS : (3 + g) * ROWS, :] for ref in blocks]
-            av_t = [ref[UNIT:SEL_ROWS, :] for ref in av_refs]
-            dq, dk, dv, ad_q, ad_v = attend_head(
-                q_ref[:, columns(g)], g_ref[:, columns(g)], keys, values, av_t, aq_t
-            )
+            av_t = [ref[first : first + RANK, :] for ref, first in av_refs]
+            heads.append((q_ref[:, columns(g)], g_ref[:, columns(g)], keys, values, av_t))
+        for g, (dq, dk, dv, ad_q, ad_v) in enumerate(attend(heads, aq_t)):
             dq_ref[:, g * HEAD_COLUMNS : (g + 1) * HEAD_COLUMNS] = dq
             for h in range(PER_HEAD):
                 put_adapter(g * PER_HEAD + h, ad_q[:, h * WIDTH : (h + 1) * WIDTH])
@@ -101,7 +115,7 @@
         pl.when(condition)(lambda rest=rest: go(*rest))
 
 
-def short_kernel(aq_ref, sel_ref, one_ref, _, q_ref, g_ref, dq_ref, ad_ref, own_ref, back_ref):
+def short_kernel(aq_ref, av_ref, av1_ref, sel_ref, one_ref, _, q_ref, g_ref, dq_ref, ad_ref, own_ref, back_ref):
     short, odd = group_place()
 
     def put_adapter(h, value):
@@ -111,14 +125,14 @@
         ad_ref[(HALF_HEADS + g) * RANK : (HALF_HEADS + g + 1) * RANK, :] = value
 
     variants = [
-        (odd == 0, [sel_ref], [sel_ref], [(own_ref, 0)]),
-        (odd == 1, [sel_ref, one_ref], [sel_ref, one_ref], [(own_ref, 0), (back_ref, 0)]),
+        (odd == 0, [sel_ref], [(av_ref, 0)], [(own_ref, 0)]),
+        (odd == 1, [sel_ref, one_ref], [(av_ref, 0), (av1_ref, 0)], [(own_ref, 0), (back_ref, 0)]),
     ]
     attend_half(short, q_ref, g_ref, dq_ref, variants, aq_ref[...], put_adapter, put_value)
 
 
 def long_kernel(
-    aq_ref, sel_ref, oth_ref, one_ref, other_ref, two_ref, three_ref, ads_ref, backs_ref, q_ref, g_ref,
+    aq_ref, av_ref, av1_ref, far_ref, oth_ref, one_ref, other_ref, three_ref, two_ref, ads_ref, backs_ref, q_ref, g_ref,
     dq_ref, ad_ref, own_ref, r1_ref, r2_ref, r3_ref,
 ):
     short, odd = group_place()
@@ -135,13 +149,13 @@
         (
             odd == 0,
             [oth_ref, one_ref, two_ref],
-            [sel_ref, one_ref, two_ref],
+            [(av_ref, 0), (av1_ref, 0), (far_ref, 0)],
             [(own_ref, 0), (r1_ref, 0), (r2_ref, 0)],
         ),
         (
             odd == 1,
             [oth_ref, other_ref, two_ref, three_ref],
-            [sel_ref, one_ref, two_ref, three_ref],
+            [(av_ref, 0), (av1_ref, 0), (far_ref, 0), (far_ref, RANK)],
             [(own_ref, 0), (r1_ref, UNIT), (r2_ref, 0), (r3_ref, 0)],
         ),
     ]
@@ -213,25 +227,23 @@
 HBM = pl.BlockSpec(memory_space=pltpu.HBM)
 
 
-def pack(short, k, v, av_t):
+def pack(short, k, v):
     half = 2 * WIDTH
 
     def chosen(array, first):
         return jnp.where(first, array[:, :half], array[:, half:])
 
-    def stacked(first):
+    def stacked_rows(first):
         pieces = [chosen(k, first), chosen(v, first)]
-        return [piece[:, h * WIDTH : (h + 1) * WIDTH] for piece in pieces for h in range(2)]
-
-    sel = jnp.concatenate(stacked(short == 0) + [av_t], axis=0)
-    oth = jnp.concatenate(stacked(short == 1), axis=0)
-    return sel, oth
+        return jnp.concatenate([p[:, h * WIDTH : (h + 1) * WIDTH] for p in pieces for h in range(2)], axis=0)
+
+    return stacked_rows(short == 0), stacked_rows(short == 1)
 
 
 def attend_short(*operands):
     return pl.pallas_call(
         short_kernel,
-        in_specs=[VMEM] * 6,
+        in_specs=[VMEM] * 8,
         out_specs=[VMEM] * 4,
         out_shape=[
             shape((ROWS, HALF_COLUMNS)),
@@ -248,7 +260,7 @@
 def attend_long(*operands):
     return pl.pallas_call(
         long_kernel,
-        in_specs=[VMEM] * 11,
+        in_specs=[VMEM] * 13,
         out_specs=[VMEM] * 6,
         out_shape=[
             shape((ROWS, HALF_COLUMNS)),
@@ -310,14 +322,18 @@
 
 def body(queries, keys, values, output_gradient, adapter_query_down, adapter_value_down):
     q, grad, aq_t = queries[0], output_gradient[0], adapter_query_down[0].T
-    sel, oth = pack(group_place()[0], keys[0], values[0], adapter_value_down[0].T)
+    av_t = adapter_value_down[0].T
+    sel, oth = pack(group_place()[0], keys[0], values[0])
     one = passed_along(sel, 1)
     other = passed_along(oth, 1, range(0, CTX_SIZE, 2))
+    av1 = passed_along(av_t, 1)
+    near_av = jnp.concatenate([av_t, av1], axis=0)
     two = passed_along(one, 1)
     three = passed_along(one, 2, range(1, CTX_SIZE, 2))
-    dq_short, ads, own_short, backs = attend_short(aq_t, sel, one, other, q, grad)
+    far = passed_along(near_av, 2)
+    dq_short, ads, own_short, backs = attend_short(aq_t, av_t, av1, sel, one, other, q, grad)
     dq_long, part, own_long, r1, r2, r3 = attend_long(
-        aq_t, sel, oth, one, other, two, three, ads, backs, q, grad
+        aq_t, av_t, av1, far, oth, one, other, three, two, ads, backs, q, grad
     )
     r1 = passed_along(r1, -1)
     r2 = passed_along(r2, -2)

time: 85.2 us -> 87.4 us (1.026)
  starting transfers between devices: 51 us -> 55 us
    ppermute x7 -> x9, starting transfers between devices: 24.8 us -> 31.3 us  [passed_along(): lax.ppermute(block, CTX, [(i, (i + distance) % CTX_SIZE) for i in senders])]
    all_to_all x1, starting transfers between devices: 12.3 us -> 7.44 us  [sum_over_all(): lax.all_to_all(part.reshape(size, part.shape[0] // size, WIDTH), NEAR, 0, 0)]
    all_to_all x2, starting transfers between devices: 13.8 us -> 16.3 us  [copies_to_all(): lax.all_to_all(jnp.broadcast_to(block[None], (size,) + block.shape), axes...]
    ppermute x7 -> x9, waiting for transfers between devices: 12 us -> 10 us  [passed_along(): lax.ppermute(block, CTX, [(i, (i + distance) % CTX_SIZE) for i in senders])]
    all_to_all x1, waiting for transfers between devices: 0.01 us -> 1.33 us  [sum_over_all(): lax.all_to_all(part.reshape(size, part.shape[0] // size, WIDTH), NEAR, 0, 0)]
  transfers between devices with their start and end apart: 10 -> 12, of which waited for: 5 -> 6; matrix products, arithmetic and copies ran while one was open for 2% -> 2% of each run, Pallas kernels for 4% -> 3%
where the time goes in v7:
time: 87.4 us; the launch traced here: 86.8 us
  starting transfers between devices  55 us (63%)
  waiting for transfers between devices  19.5 us (22%)
  Pallas kernels  7.59 us (9%)
  local copies, waits for them, and re-layouts  2.62 us (3%)
  other arithmetic  1.13 us (1%)
  between operations  0.93 us (1%)
    ppermute x9, starting transfers between devices, passed_along(): lax.ppermute(block, CTX, [(i, (i + distance) % CTX_SIZE) for i in senders])  31.3 us
    all_to_all x2, starting transfers between devices, copies_to_all(): lax.all_to_all(jnp.broadcast_to(block[None], (size,) + block.shape), axes...  16.3 us
    ppermute x9, waiting for transfers between devices, passed_along(): lax.ppermute(block, CTX, [(i, (i + distance) % CTX_SIZE) for i in senders])  10 us
    all_to_all x2, waiting for transfers between devices, copies_to_all(): lax.all_to_all(jnp.broadcast_to(block[None], (size,) + block.shape), axes...  8.15 us
    all_to_all x1, starting transfers between devices, sum_over_all(): lax.all_to_all(part.reshape(size, part.shape[0] // size, WIDTH), NEAR, 0, 0)  7.44 us
    pallas_call x1, Pallas kernels, attend_long(): pl.pallas_call(long_kernel, in_specs=[VMEM] * 13, out_specs=[VMEM] * 6, o...  3.83 us
  transfers between devices with their start and end apart: 12, of which 6 were waited for; matrix products, arithmetic and copies ran while one was open for 2% of the time, Pallas kernels for 3%

profile of v7, /device:TPU:1, one launch (start us, length us, event | category | flops | bytes accessed | tf_op | source)
XLA Modules:
  0.0 86.8 jit_solution(2106626295178232792)
XLA Ops:
  0.7 1.0 %broadcast_select_fusion = (bf16[128,256]{1,0:T(8,128)(2,1)S(1)}, bf16[128,256]{1,0:T(8,128)(2,1)S(1)}, bf16[128,256]{1,0:T(8,128)(2,1)S(1)}, bf16[128,256]{1,0:T(8,128)(2,1)S(1)}) fusion(pred[]{:T(512)S(6)} %eq.9, bf16[128,512]{1,0:T(8,128)(2,1)} %bitcast.26, pred[]{:T(512)S(6)} %eq.8, bf16[128,512]{1,0:T(8,128)(2,1)} %bitcast.27), kind=kLoop, calls=%fused_computation.2 | loop fusion | flops 131072 | bytes 524290 | tf_op jit(solution)/shard_map/jit(_where)/select_n | solution.py:234
  1.8 4.0 %collective-permute-start.1 = (bf16[512,128]{1,0:T(8,128)(2,1)S(1)}, bf16[512,128]{1,0:T(8,128)(2,1)S(1)}, u32[]{:S(2)}, u32[]{:S(2)}) collective-permute-start(bf16[512,128]{1,0:T(8,128)(2,1)S(1)} %pad_maximum_fusion.sel_ref), channel_id=1, source_target_pairs={{0,8},{8,16},{16,24},{24,32},{32,40},{40,48},{48,56},{56,64},{64,7... | collective-permute-start | bytes 393224 | tf_op jit(solution)/shard_map/ppermute | solution.py:219
  5.8 0.0 copy-start
  5.9 3.2 %collective-permute-start.2 = (bf16[512,128]{1,0:T(8,128)(2,1)S(1)}, bf16[512,128]{1,0:T(8,128)(2,1)S(1)}, u32[]{:S(2)}, u32[]{:S(2)}) collective-permute-start(bf16[512,128]{1,0:T(8,128)(2,1)S(1)} %pad_maximum_fusion.1.oth_ref), channel_id=1, source_target_pairs={{0,8},{16,24},{32,40},{48,56},{64,72},{80,88},{96,104},{112,120},{... | collective-permute-start | bytes 393224 | tf_op jit(solution)/shard_map/ppermute | solution.py:219
  9.1 1.9 %collective-permute-start = (bf16[16,128]{1,0:T(8,128)(2,1)S(1)}, bf16[16,128]{1,0:T(8,128)(2,1)S(1)}, u32[]{:S(2)}, u32[]{:S(2)}) collective-permute-start(bf16[16,128]{1,0:T(8,128)(2,1)S(1)} %bitcast.16), channel_id=1, source_target_pairs={{0,8},{8,16},{16,24},{24,32},{32,40},{40,48},{48,56},{56,64},{64,7... | collective-permute-start | bytes 12296 | tf_op jit(solution)/shard_map/ppermute | solution.py:219
  11.0 3.0 %collective-permute-done.1.one_ref = bf16[512,128]{1,0:T(8,128)(2,1)S(1)} collective-permute-done((bf16[512,128]{1,0:T(8,128)(2,1)S(1)}, bf16[512,128]{1,0:T(8,128)(2,1)S(1)}, u32[]{:S(2)}, u32[]{:S(2)}) %collective-permute-start.1) | collective-permute-done | bytes 131104 | tf_op jit(solution)/shard_map/ppermute | solution.py:219
  14.1 0.7 collective-permute-start.4
  14.7 4.5 %collective-permute-start.5 = (bf16[512,128]{1,0:T(8,128)(2,1)S(1)}, bf16[512,128]{1,0:T(8,128)(2,1)S(1)}, u32[]{:S(2)}, u32[]{:S(2)}) collective-permute-start(bf16[512,128]{1,0:T(8,128)(2,1)S(1)} %collective-permute-done.1.one_ref), channel_id=1, source_target_pairs={{0,8},{8,16},{16,24},{24,32},{32,40},{40,48},{48,56},{56,64},{64,7... | collective-permute-start | bytes 393224 | tf_op jit(solution)/shard_map/ppermute | solution.py:219
  19.2 0.0 collective-permute-done.av1_ref
  19.2 0.0 copy-start.3
  19.2 3.3 %collective-permute-start.3 = (bf16[32,128]{1,0:T(8,128)(2,1)S(1)}, bf16[32,128]{1,0:T(8,128)(2,1)S(1)}, u32[]{:S(2)}, u32[]{:S(2)}) collective-permute-start(bf16[32,128]{1,0:T(8,128)(2,1)S(1)} %pad_maximum_fusion.2), channel_id=1, source_target_pairs={{0,16},{8,24},{16,32},{24,40},{32,48},{40,56},{48,64},{56,72},{64,... | collective-permute-start | bytes 24584 | tf_op jit(solution)/shard_map/ppermute | solution.py:219
  22.6 0.0 copy-start.2
  22.6 1.2 %copy-done.2 = bf16[1,128,4096]{2,1,0:T(8,128)(2,1)S(1)} copy-done((bf16[1,128,4096]{2,1,0:T(8,128)(2,1)S(1)}, bf16[1,128,4096]{2,1,0:T(8,128)(2,1)}, u32[]{:S(2)}) %copy-start.2) | copy-done | bytes 1048600
  23.8 1.3 %short.1 = (bf16[128,2048]{1,0:T(8,128)(2,1)S(1)}, bf16[288,128]{1,0:T(8,128)(2,1)S(1)}, bf16[512,128]{1,0:T(8,128)(2,1)S(1)}, bf16[512,128]{1,0:T(8,128)(2,1)S(1)}) custom-call(bf16[16,128]{1,0:T(8,128)(2,1)S(1)} %bitcast.24, bf16[16,128]{1,0:T(8,128)(2,1)S(1)} %bitcast.18, bf16[16,128]{1,0:T(8,128)(2,1)S(1)} %collective-permute-done.av1_ref, ...), custom_call_target="tpu_custom_call" | custom-call | flops 700000000 | bytes 3000000 | tf_op jit(solution)/shard_map/short/pallas_call | solution.py:244
  25.1 4.6 %collective-permute-done.3.far_ref = bf16[32,128]{1,0:T(8,128)(2,1)S(1)} collective-permute-done((bf16[32,128]{1,0:T(8,128)(2,1)S(1)}, bf16[32,128]{1,0:T(8,128)(2,1)S(1)}, u32[]{:S(2)}, u32[]{:S(2)}) %collective-permute-start.3) | collective-permute-done | bytes 8224 | tf_op jit(solution)/shard_map/ppermute | solution.py:219
  29.7 0.0 collective-permute-done.4.three_ref
  29.7 0.0 collective-permute-done.5.two_ref
  29.7 3.8 %long.1 = (bf16[128,2048]{1,0:T(8,128)(2,1)S(1)}, bf16[768,128]{1,0:T(8,128)(2,1)}, bf16[512,128]{1,0:T(8,128)(2,1)S(1)}, bf16[1024,128]{1,0:T(8,128)(2,1)S(1)},...) custom-call(bf16[16,128]{1,0:T(8,128)(2,1)S(1)} %bitcast.25, bf16[16,128]{1,0:T(8,128)(2,1)S(1)} %bitcast.19, ...), custom_call_target="tpu_custom_call" | custom-call | flops 1400000000 | bytes 4000000 | tf_op jit(solution)/shard_map/long/pallas_call | solution.py:261
  33.6 7.4 %all-to-all-start = ((bf16[32,24,128]{2,1,0:T(8,128)(2,1)}), bf16[32,24,128]{2,1,0:T(8,128)(2,1)S(1)}, u32[]{:S(2)}, u32[]{:S(2)}) async-start(bf16[32,24,128]{2,1,0:T(8,128)(2,1)} %bitcast.13), calls=%async_computation | async-start | bytes 393216 | tf_op jit(solution)/shard_map/all_to_all | solution.py:318
  41.0 6.5 %collective-permute-start.6 = (bf16[1024,128]{1,0:T(8,128)(2,1)S(1)}, bf16[1024,128]{1,0:T(8,128)(2,1)S(1)}, u32[]{:S(2)}, u32[]{:S(2)}) collective-permute-start(bf16[1024,128]{1,0:T(8,128)(2,1)S(1)} %get-tuple-element.26), channel_id=1, source_target_pairs={{0,504},{8,0},{16,8},{24,16},{32,24},{40,32},{48,40},{56,48},{64,5... | collective-permute-start | bytes 786440 | tf_op jit(solution)/shard_map/ppermute | solution.py:219
  47.5 1.3 %all-to-all-done = bf16[32,24,128]{2,1,0:T(8,128)(2,1)S(1)} async-done(((bf16[32,24,128]{2,1,0:T(8,128)(2,1)}), bf16[32,24,128]{2,1,0:T(8,128)(2,1)S(1)}, u32[]{:S(2)}, u32[]{:S(2)}) %all-to-all-start) | async-done | bytes 196640 | tf_op jit(solution)/shard_map/all_to_all | solution.py:318
  48.9 0.7 broadcast_in_dim.24
  49.6 11.0 %all-to-all-start.1 = ((bf16[16,24,128]{2,1,0:T(8,128)(2,1)}), bf16[16,24,128]{2,1,0:T(8,128)(2,1)S(1)}, u32[]{:S(2)}, u32[]{:S(2)}) async-start(bf16[16,24,128]{2,1,0:T(8,128)(2,1)} %broadcast_in_dim.24), calls=%async_computation.1 | async-start | bytes 196608 | tf_op jit(solution)/shard_map/all_to_all | solution.py:309
  60.6 5.9 %collective-permute-start.7 = (bf16[512,128]{1,0:T(8,128)(2,1)S(1)}, bf16[512,128]{1,0:T(8,128)(2,1)S(1)}, u32[]{:S(2)}, u32[]{:S(2)}) collective-permute-start(bf16[512,128]{1,0:T(8,128)(2,1)S(1)} %get-tuple-element.27), channel_id=1, source_target_pairs={{0,496},{8,504},{16,0},{24,8},{32,16},{40,24},{48,32},{56,40},{64,... | collective-permute-start | bytes 393224 | tf_op jit(solution)/shard_map/ppermute | solution.py:219
  66.5 1.3 %collective-permute-start.8 = (bf16[512,128]{1,0:T(8,128)(2,1)S(1)}, bf16[512,128]{1,0:T(8,128)(2,1)S(1)}, u32[]{:S(2)}, u32[]{:S(2)}) collective-permute-start(bf16[512,128]{1,0:T(8,128)(2,1)S(1)} %get-tuple-element.28), channel_id=1, source_target_pairs={{8,496},{24,0},{40,16},{56,32},{72,48},{88,64},{104,80},{120,96},{... | collective-permute-start | bytes 393224 | tf_op jit(solution)/shard_map/ppermute | solution.py:219
  67.8 4.3 %all-to-all-done.1 = bf16[16,24,128]{2,1,0:T(8,128)(2,1)S(1)} async-done(((bf16[16,24,128]{2,1,0:T(8,128)(2,1)}), bf16[16,24,128]{2,1,0:T(8,128)(2,1)S(1)}, u32[]{:S(2)}, u32[]{:S(2)}) %all-to-all-start.1) | async-done | bytes 98336 | tf_op jit(solution)/shard_map/all_to_all | solution.py:309
  72.1 0.7 broadcast_in_dim.25
  72.8 5.3 %all-to-all-start.2 = ((bf16[32,24,128]{2,1,0:T(8,128)(2,1)}), bf16[32,24,128]{2,1,0:T(8,128)(2,1)S(1)}, u32[]{:S(2)}, u32[]{:S(2)}) async-start(bf16[32,24,128]{2,1,0:T(8,128)(2,1)} %broadcast_in_dim.25), calls=%async_computation.2 | async-start | bytes 393216 | tf_op jit(solution)/shard_map/all_to_all | solution.py:309
  78.1 2.4 %collective-permute-done.8.r3_ref = bf16[512,128]{1,0:T(8,128)(2,1)S(1)} collective-permute-done((bf16[512,128]{1,0:T(8,128)(2,1)S(1)}, bf16[512,128]{1,0:T(8,128)(2,1)S(1)}, u32[]{:S(2)}, u32[]{:S(2)}) %collective-permute-start.8) | collective-permute-done | bytes 131104 | tf_op jit(solution)/shard_map/ppermute | solution.py:219
  80.5 1.7 %gradients_out.1 = (bf16[128,4096]{1,0:T(8,128)(2,1)}, bf16[128,512]{1,0:T(8,128)(2,1)}, bf16[128,512]{1,0:T(8,128)(2,1)}) custom-call(bf16[128,2048]{1,0:T(8,128)(2,1)S(1)} %get-tuple-element.20.dq_short_ref, bf16[128,2048]{1,0:T(8,128)(2,1)S(1)} %get-tuple-element.23.dq_long_ref, bf16[512,128]{1,0:T(8,128)(2,1)S(1)} %get-tuple-element.24.short_ref, ...), custom_call_target="tpu_custom_call" | custom-call | flops 20000000000 | bytes 2000000 | tf_op jit(solution)/shard_map/gradients_out/pallas_call | solution.py:281
  82.2 3.8 %all-to-all-done.2 = bf16[32,24,128]{2,1,0:T(8,128)(2,1)S(1)} async-done(((bf16[32,24,128]{2,1,0:T(8,128)(2,1)}), bf16[32,24,128]{2,1,0:T(8,128)(2,1)S(1)}, u32[]{:S(2)}, u32[]{:S(2)}) %all-to-all-start.2) | async-done | bytes 196640 | tf_op jit(solution)/shard_map/all_to_all | solution.py:309
  86.1 0.7 adapter_out.1
  (16 shorter events, 0.1 us)
Async XLA Ops:
  0.6 21.9 %copy-start.1 = (bf16[1,128,4096]{2,1,0:T(8,128)(2,1)S(1)}, bf16[1,128,4096]{2,1,0:T(8,128)(2,1)}, u32[]{:S(2)}) copy-start(bf16[1,128,4096]{2,1,0:T(8,128)(2,1)} %param.6) | copy-start | bytes 3145732
  1.8 12.3 %collective-permute-start.1 = (bf16[512,128]{1,0:T(8,128)(2,1)S(1)}, bf16[512,128]{1,0:T(8,128)(2,1)S(1)}, u32[]{:S(2)}, u32[]{:S(2)}) collective-permute-start(bf16[512,128]{1,0:T(8,128)(2,1)S(1)} %pad_maximum_fusion.sel_ref), channel_id=1, source_target_pairs={{0,8},{8,16},{16,24},{24,32},{32,40},{40,48},{48,56},{56,64},{64,7... | collective-permute-start | bytes 393224 | tf_op jit(solution)/shard_map/ppermute | solution.py:219
  5.8 3.2 %copy-start = (bf16[1,128,16]{1,2,0:T(8,128)(2,1)S(1)}, bf16[1,128,16]{1,2,0:T(8,128)(2,1)}, u32[]{:S(2)}) copy-start(bf16[1,128,16]{1,2,0:T(8,128)(2,1)} %param.11) | copy-start | bytes 12292
  5.9 16.7 %collective-permute-start.2 = (bf16[512,128]{1,0:T(8,128)(2,1)S(1)}, bf16[512,128]{1,0:T(8,128)(2,1)S(1)}, u32[]{:S(2)}, u32[]{:S(2)}) collective-permute-start(bf16[512,128]{1,0:T(8,128)(2,1)S(1)} %pad_maximum_fusion.1.oth_ref), channel_id=1, source_target_pairs={{0,8},{16,24},{32,40},{48,56},{64,72},{80,88},{96,104},{112,120},{... | collective-permute-start | bytes 393224 | tf_op jit(solution)/shard_map/ppermute | solution.py:219
  9.1 10.1 %collective-permute-start = (bf16[16,128]{1,0:T(8,128)(2,1)S(1)}, bf16[16,128]{1,0:T(8,128)(2,1)S(1)}, u32[]{:S(2)}, u32[]{:S(2)}) collective-permute-start(bf16[16,128]{1,0:T(8,128)(2,1)S(1)} %bitcast.16), channel_id=1, source_target_pairs={{0,8},{8,16},{16,24},{24,32},{32,40},{40,48},{48,56},{56,64},{64,7... | collective-permute-start | bytes 12296 | tf_op jit(solution)/shard_map/ppermute | solution.py:219
  14.1 15.7 %collective-permute-start.4 = (bf16[512,128]{1,0:T(8,128)(2,1)S(1)}, bf16[512,128]{1,0:T(8,128)(2,1)S(1)}, u32[]{:S(2)}, u32[]{:S(2)}) collective-permute-start(bf16[512,128]{1,0:T(8,128)(2,1)S(1)} %collective-permute-done.1.one_ref), channel_id=1, source_target_pairs={{8,24},{24,40},{40,56},{56,72},{72,88},{88,104},{104,120},{120,136... | collective-permute-start | bytes 393224 | tf_op jit(solution)/shard_map/ppermute | solution.py:219
  14.7 15.0 %collective-permute-start.5 = (bf16[512,128]{1,0:T(8,128)(2,1)S(1)}, bf16[512,128]{1,0:T(8,128)(2,1)S(1)}, u32[]{:S(2)}, u32[]{:S(2)}) collective-permute-start(bf16[512,128]{1,0:T(8,128)(2,1)S(1)} %collective-permute-done.1.one_ref), channel_id=1, source_target_pairs={{0,8},{8,16},{16,24},{24,32},{32,40},{40,48},{48,56},{56,64},{64,7... | collective-permute-start | bytes 393224 | tf_op jit(solution)/shard_map/ppermute | solution.py:219
  19.2 3.4 %copy-start.3 = (bf16[1,128,16]{1,2,0:T(8,128)(2,1)S(1)}, bf16[1,128,16]{1,2,0:T(8,128)(2,1)}, u32[]{:S(2)}) copy-start(bf16[1,128,16]{1,2,0:T(8,128)(2,1)} %param.10) | copy-start | bytes 12292
  19.2 10.5 %collective-permute-start.3 = (bf16[32,128]{1,0:T(8,128)(2,1)S(1)}, bf16[32,128]{1,0:T(8,128)(2,1)S(1)}, u32[]{:S(2)}, u32[]{:S(2)}) collective-permute-start(bf16[32,128]{1,0:T(8,128)(2,1)S(1)} %pad_maximum_fusion.2), channel_id=1, source_target_pairs={{0,16},{8,24},{16,32},{24,40},{32,48},{40,56},{48,64},{56,72},{64,... | collective-permute-start | bytes 24584 | tf_op jit(solution)/shard_map/ppermute | solution.py:219
  22.6 1.2 %copy-start.2 = (bf16[1,128,4096]{2,1,0:T(8,128)(2,1)S(1)}, bf16[1,128,4096]{2,1,0:T(8,128)(2,1)}, u32[]{:S(2)}) copy-start(bf16[1,128,4096]{2,1,0:T(8,128)(2,1)} %param.9) | copy-start | bytes 3145732
  33.6 15.3 %all-to-all-start = ((bf16[32,24,128]{2,1,0:T(8,128)(2,1)}), bf16[32,24,128]{2,1,0:T(8,128)(2,1)S(1)}, u32[]{:S(2)}, u32[]{:S(2)}) async-start(bf16[32,24,128]{2,1,0:T(8,128)(2,1)} %bitcast.13), calls=%async_computation | async-start | bytes 393216 | tf_op jit(solution)/shard_map/all_to_all | solution.py:318
  41.0 39.5 %collective-permute-start.6 = (bf16[1024,128]{1,0:T(8,128)(2,1)S(1)}, bf16[1024,128]{1,0:T(8,128)(2,1)S(1)}, u32[]{:S(2)}, u32[]{:S(2)}) collective-permute-start(bf16[1024,128]{1,0:T(8,128)(2,1)S(1)} %get-tuple-element.26), channel_id=1, source_target_pairs={{0,504},{8,0},{16,8},{24,16},{32,24},{40,32},{48,40},{56,48},{64,5... | collective-permute-start | bytes 786440 | tf_op jit(solution)/shard_map/ppermute | solution.py:219
  49.6 22.5 %all-to-all-start.1 = ((bf16[16,24,128]{2,1,0:T(8,128)(2,1)}), bf16[16,24,128]{2,1,0:T(8,128)(2,1)S(1)}, u32[]{:S(2)}, u32[]{:S(2)}) async-start(bf16[16,24,128]{2,1,0:T(8,128)(2,1)} %broadcast_in_dim.24), calls=%async_computation.1 | async-start | bytes 196608 | tf_op jit(solution)/shard_map/all_to_all | solution.py:309
  60.6 17.5 %collective-permute-start.7 = (bf16[512,128]{1,0:T(8,128)(2,1)S(1)}, bf16[512,128]{1,0:T(8,128)(2,1)S(1)}, u32[]{:S(2)}, u32[]{:S(2)}) collective-permute-start(bf16[512,128]{1,0:T(8,128)(2,1)S(1)} %get-tuple-element.27), channel_id=1, source_target_pairs={{0,496},{8,504},{16,0},{24,8},{32,16},{40,24},{48,32},{56,40},{64,... | collective-permute-start | bytes 393224 | tf_op jit(solution)/shard_map/ppermute | solution.py:219
  66.5 14.0 %collective-permute-start.8 = (bf16[512,128]{1,0:T(8,128)(2,1)S(1)}, bf16[512,128]{1,0:T(8,128)(2,1)S(1)}, u32[]{:S(2)}, u32[]{:S(2)}) collective-permute-start(bf16[512,128]{1,0:T(8,128)(2,1)S(1)} %get-tuple-element.28), channel_id=1, source_target_pairs={{8,496},{24,0},{40,16},{56,32},{72,48},{88,64},{104,80},{120,96},{... | collective-permute-start | bytes 393224 | tf_op jit(solution)/shard_map/ppermute | solution.py:219
  72.8 13.2 %all-to-all-start.2 = ((bf16[32,24,128]{2,1,0:T(8,128)(2,1)}), bf16[32,24,128]{2,1,0:T(8,128)(2,1)S(1)}, u32[]{:S(2)}, u32[]{:S(2)}) async-start(bf16[32,24,128]{2,1,0:T(8,128)(2,1)} %broadcast_in_dim.25), calls=%async_computation.2 | async-start | bytes 393216 | tf_op jit(solution)/shard_map/all_to_all | solution.py:309

commit v8 on v7

--- a/solution.py
+++ b/solution.py
@@ -18,6 +18,7 @@
 PER_HEAD = QUERY_HEAD_COUNT // KEY_VALUE_HEADS
 HALF_HEADS = QUERY_HEAD_COUNT // 2
 UNIT = 4 * ROWS
+SEL_ROWS = UNIT + RANK
 ADAPTER_ROWS = 768
 HALF_ADAPTER_ROWS = (HALF_HEADS + 2) * RANK
 
@@ -99,7 +100,7 @@
         for g in range(2):
             keys = [ref[g * ROWS : (g + 1) * ROWS, :] for ref in blocks]
             values = [ref[(2 + g) * ROWS : (3 + g) * ROWS, :] for ref in blocks]
-            av_t = [ref[first : first + RANK, :] for ref, first in av_refs]
+            av_t = [ref[UNIT:SEL_ROWS, :] for ref in av_refs]
             heads.append((q_ref[:, columns(g)], g_ref[:, columns(g)], keys, values, av_t))
         for g, (dq, dk, dv, ad_q, ad_v) in enumerate(attend(heads, aq_t)):
             dq_ref[:, g * HEAD_COLUMNS : (g + 1) * HEAD_COLUMNS] = dq
@@ -115,7 +116,7 @@
         pl.when(condition)(lambda rest=rest: go(*rest))
 
 
-def short_kernel(aq_ref, av_ref, av1_ref, sel_ref, one_ref, _, q_ref, g_ref, dq_ref, ad_ref, own_ref, back_ref):
+def short_kernel(aq_ref, sel_ref, one_ref, _, q_ref, g_ref, dq_ref, ad_ref, own_ref, back_ref):
     short, odd = group_place()
 
     def put_adapter(h, value):
@@ -125,14 +126,14 @@
         ad_ref[(HALF_HEADS + g) * RANK : (HALF_HEADS + g + 1) * RANK, :] = value
 
     variants = [
-        (odd == 0, [sel_ref], [(av_ref, 0)], [(own_ref, 0)]),
-        (odd == 1, [sel_ref, one_ref], [(av_ref, 0), (av1_ref, 0)], [(own_ref, 0), (back_ref, 0)]),
+        (odd == 0, [sel_ref], [sel_ref], [(own_ref, 0)]),
+        (odd == 1, [sel_ref, one_ref], [sel_ref, one_ref], [(own_ref, 0), (back_ref, 0)]),
     ]
     attend_half(short, q_ref, g_ref, dq_ref, variants, aq_ref[...], put_adapter, put_value)
 
 
 def long_kernel(
-    aq_ref, av_ref, av1_ref, far_ref, oth_ref, one_ref, other_ref, three_ref, two_ref, ads_ref, backs_ref, q_ref, g_ref,
+    aq_ref, sel_ref, oth_ref, one_ref, other_ref, three_ref, two_ref, ads_ref, backs_ref, q_ref, g_ref,
     dq_ref, ad_ref, own_ref, r1_ref, r2_ref, r3_ref,
 ):
     short, odd = group_place()
@@ -149,13 +150,13 @@
         (
             odd == 0,
             [oth_ref, one_ref, two_ref],
-            [(av_ref, 0), (av1_ref, 0), (far_ref, 0)],
+            [sel_ref, one_ref, two_ref],
             [(own_ref, 0), (r1_ref, 0), (r2_ref, 0)],
         ),
         (
             odd == 1,
             [oth_ref, other_ref, two_ref, three_ref],
-            [(av_ref, 0), (av1_ref, 0), (far_ref, 0), (far_ref, RANK)],
+            [sel_ref, one_ref, two_ref, three_ref],
             [(own_ref, 0), (r1_ref, UNIT), (r2_ref, 0), (r3_ref, 0)],
         ),
     ]
@@ -227,23 +228,25 @@
 HBM = pl.BlockSpec(memory_space=pltpu.HBM)
 
 
-def pack(short, k, v):
+def pack(short, k, v, av_t):
     half = 2 * WIDTH
 
     def chosen(array, first):
         return jnp.where(first, array[:, :half], array[:, half:])
 
-    def stacked_rows(first):
+    def stacked(first):
         pieces = [chosen(k, first), chosen(v, first)]
-        return jnp.concatenate([p[:, h * WIDTH : (h + 1) * WIDTH] for p in pieces for h in range(2)], axis=0)
-
-    return stacked_rows(short == 0), stacked_rows(short == 1)
+        return [piece[:, h * WIDTH : (h + 1) * WIDTH] for piece in pieces for h in range(2)]
+
+    sel = jnp.concatenate(stacked(short == 0) + [av_t], axis=0)
+    oth = jnp.concatenate(stacked(short == 1), axis=0)
+    return sel, oth
 
 
 def attend_short(*operands):
     return pl.pallas_call(
         short_kernel,
-        in_specs=[VMEM] * 8,
+        in_specs=[VMEM] * 6,
         out_specs=[VMEM] * 4,
         out_shape=[
             shape((ROWS, HALF_COLUMNS)),
@@ -260,7 +263,7 @@
 def attend_long(*operands):
     return pl.pallas_call(
         long_kernel,
-        in_specs=[VMEM] * 13,
+        in_specs=[VMEM] * 11,
         out_specs=[VMEM] * 6,
         out_shape=[
             shape((ROWS, HALF_COLUMNS)),
@@ -322,18 +325,14 @@
 
 def body(queries, keys, values, output_gradient, adapter_query_down, adapter_value_down):
     q, grad, aq_t = queries[0], output_gradient[0], adapter_query_down[0].T
-    av_t = adapter_value_down[0].T
-    sel, oth = pack(group_place()[0], keys[0], values[0])
+    sel, oth = pack(group_place()[0], keys[0], values[0], adapter_value_down[0].T)
     one = passed_along(sel, 1)
     other = passed_along(oth, 1, range(0, CTX_SIZE, 2))
-    av1 = passed_along(av_t, 1)
-    near_av = jnp.concatenate([av_t, av1], axis=0)
+    three = passed_along(one, 2, range(1, CTX_SIZE, 2))
     two = passed_along(one, 1)
-    three = passed_along(one, 2, range(1, CTX_SIZE, 2))
-    far = passed_along(near_av, 2)
-    dq_short, ads, own_short, backs = attend_short(aq_t, av_t, av1, sel, one, other, q, grad)
+    dq_short, ads, own_short, backs = attend_short(aq_t, sel, one, other, q, grad)
     dq_long, part, own_long, r1, r2, r3 = attend_long(
-        aq_t, av_t, av1, far, oth, one, other, three, two, ads, backs, q, grad
+        aq_t, sel, oth, one, other, three, two, ads, backs, q, grad
     )
     r1 = passed_along(r1, -1)
     r2 = passed_along(r2, -2)

time: 87.4 us -> 83.4 us (0.954)
  starting transfers between devices: 55 us -> 45.7 us
  waiting for transfers between devices: 19.5 us -> 24.1 us
    ppermute x9 -> x7, starting transfers between devices: 31.3 us -> 22.6 us  [passed_along(): lax.ppermute(block, CTX, [(i, (i + distance) % CTX_SIZE) for i in senders])]
    ppermute x9 -> x7, waiting for transfers between devices: 10 us -> 13.7 us  [passed_along(): lax.ppermute(block, CTX, [(i, (i + distance) % CTX_SIZE) for i in senders])]
    all_to_all x2, starting transfers between devices: 16.3 us -> 13.5 us  [copies_to_all(): lax.all_to_all(jnp.broadcast_to(block[None], (size,) + block.shape), axes...]
    all_to_all x1, starting transfers between devices: 7.44 us -> 9.61 us  [sum_over_all(): lax.all_to_all(part.reshape(size, part.shape[0] // size, WIDTH), NEAR, 0, 0)]
    all_to_all x1, waiting for transfers between devices: 1.33 us -> 2.33 us  [sum_over_all(): lax.all_to_all(part.reshape(size, part.shape[0] // size, WIDTH), NEAR, 0, 0)]
  transfers between devices with their start and end apart: 12 -> 10, of which waited for: 6 -> 6; matrix products, arithmetic and copies ran while one was open for 2% -> 2% of each run, Pallas kernels for 3% -> 4%
where the time goes in v8:
time: 83.4 us; the launch traced here: 82.8 us
  starting transfers between devices  45.7 us (55%)
  waiting for transfers between devices  24.1 us (29%)
  Pallas kernels  7.58 us (9%)
  local copies, waits for them, and re-layouts  3.34 us (4%)
  other arithmetic  1.11 us (1%)
  between operations  0.88 us (1%)
    ppermute x7, starting transfers between devices, passed_along(): lax.ppermute(block, CTX, [(i, (i + distance) % CTX_SIZE) for i in senders])  22.6 us
    ppermute x7, waiting for transfers between devices, passed_along(): lax.ppermute(block, CTX, [(i, (i + distance) % CTX_SIZE) for i in senders])  13.7 us
    all_to_all x2, starting transfers between devices, copies_to_all(): lax.all_to_all(jnp.broadcast_to(block[None], (size,) + block.shape), axes...  13.5 us
    all_to_all x1, starting transfers between devices, sum_over_all(): lax.all_to_all(part.reshape(size, part.shape[0] // size, WIDTH), NEAR, 0, 0)  9.61 us
    all_to_all x2, waiting for transfers between devices, copies_to_all(): lax.all_to_all(jnp.broadcast_to(block[None], (size,) + block.shape), axes...  8.15 us
    pallas_call x1, Pallas kernels, attend_long(): pl.pallas_call(long_kernel, in_specs=[VMEM] * 11, out_specs=[VMEM] * 6, o...  3.82 us
    all_to_all x1, waiting for transfers between devices, sum_over_all(): lax.all_to_all(part.reshape(size, part.shape[0] // size, WIDTH), NEAR, 0, 0)  2.33 us
    pallas_call x1, Pallas kernels, gradients_out(): pl.pallas_call(gradients_kernel, in_specs=[VMEM] * 7, out_specs=[HBM, VME...  1.71 us
  transfers between devices with their start and end apart: 10, of which 6 were waited for; matrix products, arithmetic and copies ran while one was open for 2% of the time, Pallas kernels for 4%

profile of v8, /device:TPU:1, one launch (start us, length us, event | category | flops | bytes accessed | tf_op | source)
XLA Modules:
  0.0 82.8 jit_solution(13735110053467033998)
XLA Ops:
  0.6 0.0 copy-start
  0.7 1.0 %broadcast_select_fusion = (bf16[128,256]{1,0:T(8,128)(2,1)S(1)}, bf16[128,256]{1,0:T(8,128)(2,1)S(1)}, bf16[128,256]{1,0:T(8,128)(2,1)S(1)}, bf16[128,256]{1,0:T(8,128)(2,1)S(1)}) fusion(pred[]{:T(512)S(6)} %eq.9, bf16[128,512]{1,0:T(8,128)(2,1)} %bitcast.23, pred[]{:T(512)S(6)} %eq.8, bf16[128,512]{1,0:T(8,128)(2,1)} %bitcast.24), kind=kLoop, calls=%fused_computation.1 | loop fusion | flops 131072 | bytes 524290 | tf_op jit(solution)/shard_map/jit(_where)/select_n | solution.py:235
  1.8 0.7 constant_dynamic-update-slice_fusion.sel_ref
  2.5 4.0 %collective-permute-start = (bf16[528,128]{1,0:T(8,128)(2,1)S(1)}, bf16[528,128]{1,0:T(8,128)(2,1)S(1)}, u32[]{:S(2)}, u32[]{:S(2)}) collective-permute-start(bf16[528,128]{1,0:T(8,128)(2,1)S(1)} %constant_dynamic-update-slice_fusion.sel_ref), channel_id=1, source_target_pairs={{0,8},{8,16},{16,24},{24,32},{32,40},{40,48},{48,56},{56,64},{64,7... | collective-permute-start | bytes 405512 | tf_op jit(solution)/shard_map/ppermute | solution.py:220
  6.6 0.0 copy-start.3
  6.6 3.2 %collective-permute-start.1 = (bf16[512,128]{1,0:T(8,128)(2,1)S(1)}, bf16[512,128]{1,0:T(8,128)(2,1)S(1)}, u32[]{:S(2)}, u32[]{:S(2)}) collective-permute-start(bf16[512,128]{1,0:T(8,128)(2,1)S(1)} %pad_maximum_fusion.oth_ref), channel_id=1, source_target_pairs={{0,8},{16,24},{32,40},{48,56},{64,72},{80,88},{96,104},{112,120},{... | collective-permute-start | bytes 393224 | tf_op jit(solution)/shard_map/ppermute | solution.py:220
  9.8 5.0 %collective-permute-done.one_ref = bf16[528,128]{1,0:T(8,128)(2,1)S(1)} collective-permute-done((bf16[528,128]{1,0:T(8,128)(2,1)S(1)}, bf16[528,128]{1,0:T(8,128)(2,1)S(1)}, u32[]{:S(2)}, u32[]{:S(2)}) %collective-permute-start) | collective-permute-done | bytes 135200 | tf_op jit(solution)/shard_map/ppermute | solution.py:220
  14.8 0.7 collective-permute-start.2
  15.5 1.9 %collective-permute-start.3 = (bf16[528,128]{1,0:T(8,128)(2,1)S(1)}, bf16[528,128]{1,0:T(8,128)(2,1)S(1)}, u32[]{:S(2)}, u32[]{:S(2)}) collective-permute-start(bf16[528,128]{1,0:T(8,128)(2,1)S(1)} %collective-permute-done.one_ref), channel_id=1, source_target_pairs={{0,8},{8,16},{16,24},{24,32},{32,40},{40,48},{48,56},{56,64},{64,7... | collective-permute-start | bytes 405512 | tf_op jit(solution)/shard_map/ppermute | solution.py:220
  17.4 0.0 collective-permute-done.1._.other_ref
  17.4 0.0 copy-start.1
  17.4 1.2 %copy-done.1 = bf16[1,128,4096]{2,1,0:T(8,128)(2,1)S(1)} copy-done((bf16[1,128,4096]{2,1,0:T(8,128)(2,1)S(1)}, bf16[1,128,4096]{2,1,0:T(8,128)(2,1)}, u32[]{:S(2)}) %copy-start.1) | copy-done | bytes 1048600
  18.6 1.3 %short.1 = (bf16[128,2048]{1,0:T(8,128)(2,1)S(1)}, bf16[288,128]{1,0:T(8,128)(2,1)S(1)}, bf16[512,128]{1,0:T(8,128)(2,1)S(1)}, bf16[512,128]{1,0:T(8,128)(2,1)S(1)}) custom-call(bf16[16,128]{1,0:T(8,128)(2,1)S(1)} %bitcast.21, bf16[528,128]{1,0:T(8,128)(2,1)S(1)} %constant_dynamic-update-slice_fusion.sel_ref, ...), custom_call_target="tpu_custom_call" | custom-call | flops 700000000 | bytes 3000000 | tf_op jit(solution)/shard_map/short/pallas_call | solution.py:247
  20.0 0.0 collective-permute-done.2.three_ref
  20.0 6.3 %collective-permute-done.3.two_ref = bf16[528,128]{1,0:T(8,128)(2,1)S(1)} collective-permute-done((bf16[528,128]{1,0:T(8,128)(2,1)S(1)}, bf16[528,128]{1,0:T(8,128)(2,1)S(1)}, u32[]{:S(2)}, u32[]{:S(2)}) %collective-permute-start.3) | collective-permute-done | bytes 135200 | tf_op jit(solution)/shard_map/ppermute | solution.py:220
  26.2 3.8 %long.1 = (bf16[128,2048]{1,0:T(8,128)(2,1)S(1)}, bf16[768,128]{1,0:T(8,128)(2,1)}, bf16[512,128]{1,0:T(8,128)(2,1)S(1)}, bf16[1024,128]{1,0:T(8,128)(2,1)S(1)},...) custom-call(bf16[16,128]{1,0:T(8,128)(2,1)S(1)} %bitcast.22, ...), custom_call_target="tpu_custom_call" | custom-call | flops 1400000000 | bytes 4000000 | tf_op jit(solution)/shard_map/long/pallas_call | solution.py:264
  30.1 9.6 %all-to-all-start = ((bf16[32,24,128]{2,1,0:T(8,128)(2,1)}), bf16[32,24,128]{2,1,0:T(8,128)(2,1)S(1)}, u32[]{:S(2)}, u32[]{:S(2)}) async-start(bf16[32,24,128]{2,1,0:T(8,128)(2,1)} %bitcast.12), calls=%async_computation | async-start | bytes 393216 | tf_op jit(solution)/shard_map/all_to_all | solution.py:321
  39.7 5.6 %collective-permute-start.4 = (bf16[1024,128]{1,0:T(8,128)(2,1)S(1)}, bf16[1024,128]{1,0:T(8,128)(2,1)S(1)}, u32[]{:S(2)}, u32[]{:S(2)}) collective-permute-start(bf16[1024,128]{1,0:T(8,128)(2,1)S(1)} %get-tuple-element.26), channel_id=1, source_target_pairs={{0,504},{8,0},{16,8},{24,16},{32,24},{40,32},{48,40},{56,48},{64,5... | collective-permute-start | bytes 786440 | tf_op jit(solution)/shard_map/ppermute | solution.py:220
  45.3 2.3 %all-to-all-done = bf16[32,24,128]{2,1,0:T(8,128)(2,1)S(1)} async-done(((bf16[32,24,128]{2,1,0:T(8,128)(2,1)}), bf16[32,24,128]{2,1,0:T(8,128)(2,1)S(1)}, u32[]{:S(2)}, u32[]{:S(2)}) %all-to-all-start) | async-done | bytes 196640 | tf_op jit(solution)/shard_map/all_to_all | solution.py:321
  47.7 0.7 broadcast_in_dim.24
  48.3 8.2 %all-to-all-start.1 = ((bf16[16,24,128]{2,1,0:T(8,128)(2,1)}), bf16[16,24,128]{2,1,0:T(8,128)(2,1)S(1)}, u32[]{:S(2)}, u32[]{:S(2)}) async-start(bf16[16,24,128]{2,1,0:T(8,128)(2,1)} %broadcast_in_dim.24), calls=%async_computation.1 | async-start | bytes 196608 | tf_op jit(solution)/shard_map/all_to_all | solution.py:312
  56.6 5.9 %collective-permute-start.5 = (bf16[512,128]{1,0:T(8,128)(2,1)S(1)}, bf16[512,128]{1,0:T(8,128)(2,1)S(1)}, u32[]{:S(2)}, u32[]{:S(2)}) collective-permute-start(bf16[512,128]{1,0:T(8,128)(2,1)S(1)} %get-tuple-element.27), channel_id=1, source_target_pairs={{0,496},{8,504},{16,0},{24,8},{32,16},{40,24},{48,32},{56,40},{64,... | collective-permute-start | bytes 393224 | tf_op jit(solution)/shard_map/ppermute | solution.py:220
  62.5 1.3 %collective-permute-start.6 = (bf16[512,128]{1,0:T(8,128)(2,1)S(1)}, bf16[512,128]{1,0:T(8,128)(2,1)S(1)}, u32[]{:S(2)}, u32[]{:S(2)}) collective-permute-start(bf16[512,128]{1,0:T(8,128)(2,1)S(1)} %get-tuple-element.28), channel_id=1, source_target_pairs={{8,496},{24,0},{40,16},{56,32},{72,48},{88,64},{104,80},{120,96},{... | collective-permute-start | bytes 393224 | tf_op jit(solution)/shard_map/ppermute | solution.py:220
  63.8 4.3 %all-to-all-done.1 = bf16[16,24,128]{2,1,0:T(8,128)(2,1)S(1)} async-done(((bf16[16,24,128]{2,1,0:T(8,128)(2,1)}), bf16[16,24,128]{2,1,0:T(8,128)(2,1)S(1)}, u32[]{:S(2)}, u32[]{:S(2)}) %all-to-all-start.1) | async-done | bytes 98336 | tf_op jit(solution)/shard_map/all_to_all | solution.py:312
  68.1 0.7 broadcast_in_dim.25
  68.8 5.3 %all-to-all-start.2 = ((bf16[32,24,128]{2,1,0:T(8,128)(2,1)}), bf16[32,24,128]{2,1,0:T(8,128)(2,1)S(1)}, u32[]{:S(2)}, u32[]{:S(2)}) async-start(bf16[32,24,128]{2,1,0:T(8,128)(2,1)} %broadcast_in_dim.25), calls=%async_computation.2 | async-start | bytes 393216 | tf_op jit(solution)/shard_map/all_to_all | solution.py:312
  74.1 0.0 collective-permute-done.5.r2_ref
  74.1 2.4 %collective-permute-done.6.r3_ref = bf16[512,128]{1,0:T(8,128)(2,1)S(1)} collective-permute-done((bf16[512,128]{1,0:T(8,128)(2,1)S(1)}, bf16[512,128]{1,0:T(8,128)(2,1)S(1)}, u32[]{:S(2)}, u32[]{:S(2)}) %collective-permute-start.6) | collective-permute-done | bytes 131104 | tf_op jit(solution)/shard_map/ppermute | solution.py:220
  76.5 0.0 collective-permute-done.4.r1_ref
  76.5 1.7 %gradients_out.1 = (bf16[128,4096]{1,0:T(8,128)(2,1)}, bf16[128,512]{1,0:T(8,128)(2,1)}, bf16[128,512]{1,0:T(8,128)(2,1)}) custom-call(bf16[128,2048]{1,0:T(8,128)(2,1)S(1)} %get-tuple-element.20.dq_short_ref, bf16[128,2048]{1,0:T(8,128)(2,1)S(1)} %get-tuple-element.23.dq_long_ref, bf16[512,128]{1,0:T(8,128)(2,1)S(1)} %get-tuple-element.24.short_ref, ...), custom_call_target="tpu_custom_call" | custom-call | flops 20000000000 | bytes 2000000 | tf_op jit(solution)/shard_map/gradients_out/pallas_call | solution.py:284
  78.2 3.8 %all-to-all-done.2 = bf16[32,24,128]{2,1,0:T(8,128)(2,1)S(1)} async-done(((bf16[32,24,128]{2,1,0:T(8,128)(2,1)}), bf16[32,24,128]{2,1,0:T(8,128)(2,1)S(1)}, u32[]{:S(2)}, u32[]{:S(2)}) %all-to-all-start.2) | async-done | bytes 196640 | tf_op jit(solution)/shard_map/all_to_all | solution.py:312
  82.1 0.7 adapter_out.1
  (13 shorter events, 0.1 us)
Async XLA Ops:
  0.6 16.8 %copy-start = (bf16[1,128,4096]{2,1,0:T(8,128)(2,1)S(1)}, bf16[1,128,4096]{2,1,0:T(8,128)(2,1)}, u32[]{:S(2)}) copy-start(bf16[1,128,4096]{2,1,0:T(8,128)(2,1)} %param.6) | copy-start | bytes 3145732
  2.5 12.3 %collective-permute-start = (bf16[528,128]{1,0:T(8,128)(2,1)S(1)}, bf16[528,128]{1,0:T(8,128)(2,1)S(1)}, u32[]{:S(2)}, u32[]{:S(2)}) collective-permute-start(bf16[528,128]{1,0:T(8,128)(2,1)S(1)} %constant_dynamic-update-slice_fusion.sel_ref), channel_id=1, source_target_pairs={{0,8},{8,16},{16,24},{24,32},{32,40},{40,48},{48,56},{56,64},{64,7... | collective-permute-start | bytes 405512 | tf_op jit(solution)/shard_map/ppermute | solution.py:220
  6.6 10.8 %copy-start.3 = (bf16[1,128,16]{1,2,0:T(8,128)(2,1)S(1)}, bf16[1,128,16]{1,2,0:T(8,128)(2,1)}, u32[]{:S(2)}) copy-start(bf16[1,128,16]{1,2,0:T(8,128)(2,1)} %param.10) | copy-start | bytes 12292
  6.6 10.8 %collective-permute-start.1 = (bf16[512,128]{1,0:T(8,128)(2,1)S(1)}, bf16[512,128]{1,0:T(8,128)(2,1)S(1)}, u32[]{:S(2)}, u32[]{:S(2)}) collective-permute-start(bf16[512,128]{1,0:T(8,128)(2,1)S(1)} %pad_maximum_fusion.oth_ref), channel_id=1, source_target_pairs={{0,8},{16,24},{32,40},{48,56},{64,72},{80,88},{96,104},{112,120},{... | collective-permute-start | bytes 393224 | tf_op jit(solution)/shard_map/ppermute | solution.py:220
  14.8 5.2 %collective-permute-start.2 = (bf16[528,128]{1,0:T(8,128)(2,1)S(1)}, bf16[528,128]{1,0:T(8,128)(2,1)S(1)}, u32[]{:S(2)}, u32[]{:S(2)}) collective-permute-start(bf16[528,128]{1,0:T(8,128)(2,1)S(1)} %collective-permute-done.one_ref), channel_id=1, source_target_pairs={{8,24},{24,40},{40,56},{56,72},{72,88},{88,104},{104,120},{120,136... | collective-permute-start | bytes 405512 | tf_op jit(solution)/shard_map/ppermute | solution.py:220
  15.5 10.8 %collective-permute-start.3 = (bf16[528,128]{1,0:T(8,128)(2,1)S(1)}, bf16[528,128]{1,0:T(8,128)(2,1)S(1)}, u32[]{:S(2)}, u32[]{:S(2)}) collective-permute-start(bf16[528,128]{1,0:T(8,128)(2,1)S(1)} %collective-permute-done.one_ref), channel_id=1, source_target_pairs={{0,8},{8,16},{16,24},{24,32},{32,40},{40,48},{48,56},{56,64},{64,7... | collective-permute-start | bytes 405512 | tf_op jit(solution)/shard_map/ppermute | solution.py:220
  17.4 1.2 %copy-start.1 = (bf16[1,128,4096]{2,1,0:T(8,128)(2,1)S(1)}, bf16[1,128,4096]{2,1,0:T(8,128)(2,1)}, u32[]{:S(2)}) copy-start(bf16[1,128,4096]{2,1,0:T(8,128)(2,1)} %param.9) | copy-start | bytes 3145732
  18.6 7.6 %copy-start.2 = (bf16[1,128,4096]{2,1,0:T(8,128)(2,1)S(1)}, bf16[1,128,4096]{2,1,0:T(8,128)(2,1)}, u32[]{:S(2)}) copy-start(bf16[1,128,4096]{2,1,0:T(8,128)(2,1)} %param.9) | copy-start | bytes 3145732
  30.1 17.6 %all-to-all-start = ((bf16[32,24,128]{2,1,0:T(8,128)(2,1)}), bf16[32,24,128]{2,1,0:T(8,128)(2,1)S(1)}, u32[]{:S(2)}, u32[]{:S(2)}) async-start(bf16[32,24,128]{2,1,0:T(8,128)(2,1)} %bitcast.12), calls=%async_computation | async-start | bytes 393216 | tf_op jit(solution)/shard_map/all_to_all | solution.py:321
  39.7 36.8 %collective-permute-start.4 = (bf16[1024,128]{1,0:T(8,128)(2,1)S(1)}, bf16[1024,128]{1,0:T(8,128)(2,1)S(1)}, u32[]{:S(2)}, u32[]{:S(2)}) collective-permute-start(bf16[1024,128]{1,0:T(8,128)(2,1)S(1)} %get-tuple-element.26), channel_id=1, source_target_pairs={{0,504},{8,0},{16,8},{24,16},{32,24},{40,32},{48,40},{56,48},{64,5... | collective-permute-start | bytes 786440 | tf_op jit(solution)/shard_map/ppermute | solution.py:220
  48.3 19.8 %all-to-all-start.1 = ((bf16[16,24,128]{2,1,0:T(8,128)(2,1)}), bf16[16,24,128]{2,1,0:T(8,128)(2,1)S(1)}, u32[]{:S(2)}, u32[]{:S(2)}) async-start(bf16[16,24,128]{2,1,0:T(8,128)(2,1)} %broadcast_in_dim.24), calls=%async_computation.1 | async-start | bytes 196608 | tf_op jit(solution)/shard_map/all_to_all | solution.py:312
  56.6 17.5 %collective-permute-start.5 = (bf16[512,128]{1,0:T(8,128)(2,1)S(1)}, bf16[512,128]{1,0:T(8,128)(2,1)S(1)}, u32[]{:S(2)}, u32[]{:S(2)}) collective-permute-start(bf16[512,128]{1,0:T(8,128)(2,1)S(1)} %get-tuple-element.27), channel_id=1, source_target_pairs={{0,496},{8,504},{16,0},{24,8},{32,16},{40,24},{48,32},{56,40},{64,... | collective-permute-start | bytes 393224 | tf_op jit(solution)/shard_map/ppermute | solution.py:220
  62.5 14.0 %collective-permute-start.6 = (bf16[512,128]{1,0:T(8,128)(2,1)S(1)}, bf16[512,128]{1,0:T(8,128)(2,1)S(1)}, u32[]{:S(2)}, u32[]{:S(2)}) collective-permute-start(bf16[512,128]{1,0:T(8,128)(2,1)S(1)} %get-tuple-element.28), channel_id=1, source_target_pairs={{8,496},{24,0},{40,16},{56,32},{72,48},{88,64},{104,80},{120,96},{... | collective-permute-start | bytes 393224 | tf_op jit(solution)/shard_map/ppermute | solution.py:220
  68.8 13.2 %all-to-all-start.2 = ((bf16[32,24,128]{2,1,0:T(8,128)(2,1)}), bf16[32,24,128]{2,1,0:T(8,128)(2,1)S(1)}, u32[]{:S(2)}, u32[]{:S(2)}) async-start(bf16[32,24,128]{2,1,0:T(8,128)(2,1)} %broadcast_in_dim.25), calls=%async_computation.2 | async-start | bytes 393216 | tf_op jit(solution)/shard_map/all_to_all | solution.py:312

commit v9 on v8

--- a/solution.py
+++ b/solution.py
@@ -134,7 +134,7 @@
 
 def long_kernel(
     aq_ref, sel_ref, oth_ref, one_ref, other_ref, three_ref, two_ref, ads_ref, backs_ref, q_ref, g_ref,
-    dq_ref, ad_ref, own_ref, r1_ref, r2_ref, r3_ref,
+    dq_ref, ad_ref, own_ref, r1_ref, r2_ref,
 ):
     short, odd = group_place()
     long = 1 - short
@@ -157,7 +157,7 @@
             odd == 1,
             [oth_ref, other_ref, two_ref, three_ref],
             [sel_ref, one_ref, two_ref, three_ref],
-            [(own_ref, 0), (r1_ref, UNIT), (r2_ref, 0), (r3_ref, 0)],
+            [(own_ref, 0), (r1_ref, UNIT), (r2_ref, 0), (r2_ref, UNIT)],
         ),
     ]
     attend_half(long, q_ref, g_ref, dq_ref, variants, aq_ref[...], put_adapter, put_value)
@@ -264,14 +264,13 @@
     return pl.pallas_call(
         long_kernel,
         in_specs=[VMEM] * 11,
-        out_specs=[VMEM] * 6,
+        out_specs=[VMEM] * 5,
         out_shape=[
             shape((ROWS, HALF_COLUMNS)),
             shape((ADAPTER_ROWS, WIDTH)),
             shape((UNIT, WIDTH)),
             shape((2 * UNIT, WIDTH)),
-            shape((UNIT, WIDTH)),
-            shape((UNIT, WIDTH)),
+            shape((2 * UNIT, WIDTH)),
         ],
         compiler_params=PARAMS,
         cost_estimate=pl.CostEstimate(flops=1_400_000_000, bytes_accessed=4_000_000, transcendentals=0),
@@ -331,12 +330,12 @@
     three = passed_along(one, 2, range(1, CTX_SIZE, 2))
     two = passed_along(one, 1)
     dq_short, ads, own_short, backs = attend_short(aq_t, sel, one, other, q, grad)
-    dq_long, part, own_long, r1, r2, r3 = attend_long(
+    dq_long, part, own_long, r1, r2 = attend_long(
         aq_t, sel, oth, one, other, three, two, ads, backs, q, grad
     )
     r1 = passed_along(r1, -1)
     r2 = passed_along(r2, -2)
-    r3 = passed_along(r3, -3, range(1, CTX_SIZE, 2))
+    r3 = passed_along(r2[UNIT:], -1, range(1, CTX_SIZE, 2))
     dq, dk, dv = gradients_out(dq_short, dq_long, own_short, own_long, r1, r2, r3)
     total = sum_over_all(part)
     adapter_q, adapter_v = adapter_out(total)

time: 83.4 us -> 85.9 us (1.030)
  waiting for transfers between devices: 24.1 us -> 28 us
  starting transfers between devices: 45.7 us -> 44.3 us
    all_to_all x2, waiting for transfers between devices: 8.15 us -> 16.3 us  [copies_to_all(): lax.all_to_all(jnp.broadcast_to(block[None], (size,) + block.shape), axes...]
    ppermute x7, starting transfers between devices: 22.6 us -> 18.6 us  [passed_along(): lax.ppermute(block, CTX, [(i, (i + distance) % CTX_SIZE) for i in senders])]
    all_to_all x2, starting transfers between devices: 13.5 us -> 16.1 us  [copies_to_all(): lax.all_to_all(jnp.broadcast_to(block[None], (size,) + block.shape), axes...]
    ppermute x7, waiting for transfers between devices: 13.7 us -> 11.3 us  [passed_along(): lax.ppermute(block, CTX, [(i, (i + distance) % CTX_SIZE) for i in senders])]
    all_to_all x1, waiting for transfers between devices: 2.33 us -> 0.4 us  [sum_over_all(): lax.all_to_all(part.reshape(size, part.shape[0] // size, WIDTH), NEAR, 0, 0)]
  transfers between devices with their start and end apart: 10 -> 10, of which waited for: 6 -> 5; matrix products, arithmetic and copies ran while one was open for 2% -> 2% of each run, Pallas kernels for 4% -> 4%
where the time goes in v9:
time: 85.9 us; the launch traced here: 85.3 us
  starting transfers between devices  44.3 us (52%)
  waiting for transfers between devices  28 us (33%)
  Pallas kernels  7.58 us (9%)
  local copies, waits for them, and re-layouts  3.35 us (4%)
  other arithmetic  1.11 us (1%)
  between operations  0.9 us (1%)
    ppermute x7, starting transfers between devices, passed_along(): lax.ppermute(block, CTX, [(i, (i + distance) % CTX_SIZE) for i in senders])  18.6 us
    all_to_all x2, waiting for transfers between devices, copies_to_all(): lax.all_to_all(jnp.broadcast_to(block[None], (size,) + block.shape), axes...  16.3 us
    all_to_all x2, starting transfers between devices, copies_to_all(): lax.all_to_all(jnp.broadcast_to(block[None], (size,) + block.shape), axes...  16.1 us
    ppermute x7, waiting for transfers between devices, passed_along(): lax.ppermute(block, CTX, [(i, (i + distance) % CTX_SIZE) for i in senders])  11.3 us
    all_to_all x1, starting transfers between devices, sum_over_all(): lax.all_to_all(part.reshape(size, part.shape[0] // size, WIDTH), NEAR, 0, 0)  9.61 us
    pallas_call x1, Pallas kernels, attend_long(): pl.pallas_call(long_kernel, in_specs=[VMEM] * 11, out_specs=[VMEM] * 5, o...  3.82 us
  transfers between devices with their start and end apart: 10, of which 5 were waited for; matrix products, arithmetic and copies ran while one was open for 2% of the time, Pallas kernels for 4%

profile of v9, /device:TPU:1, one launch (start us, length us, event | category | flops | bytes accessed | tf_op | source)
XLA Modules:
  0.0 85.3 jit_solution(12217566941245115686)
XLA Ops:
  0.7 1.0 %broadcast_select_fusion = (bf16[128,256]{1,0:T(8,128)(2,1)S(1)}, bf16[128,256]{1,0:T(8,128)(2,1)S(1)}, bf16[128,256]{1,0:T(8,128)(2,1)S(1)}, bf16[128,256]{1,0:T(8,128)(2,1)S(1)}) fusion(pred[]{:T(512)S(6)} %eq.9, bf16[128,512]{1,0:T(8,128)(2,1)} %bitcast.23, pred[]{:T(512)S(6)} %eq.8, bf16[128,512]{1,0:T(8,128)(2,1)} %bitcast.24), kind=kLoop, calls=%fused_computation.1 | loop fusion | flops 131072 | bytes 524290 | tf_op jit(solution)/shard_map/jit(_where)/select_n | solution.py:235
  1.8 0.7 constant_dynamic-update-slice_fusion.sel_ref
  2.5 4.0 %collective-permute-start = (bf16[528,128]{1,0:T(8,128)(2,1)S(1)}, bf16[528,128]{1,0:T(8,128)(2,1)S(1)}, u32[]{:S(2)}, u32[]{:S(2)}) collective-permute-start(bf16[528,128]{1,0:T(8,128)(2,1)S(1)} %constant_dynamic-update-slice_fusion.sel_ref), channel_id=1, source_target_pairs={{0,8},{8,16},{16,24},{24,32},{32,40},{40,48},{48,56},{56,64},{64,7... | collective-permute-start | bytes 405512 | tf_op jit(solution)/shard_map/ppermute | solution.py:220
  6.6 0.0 copy-start.3
  6.6 3.2 %collective-permute-start.1 = (bf16[512,128]{1,0:T(8,128)(2,1)S(1)}, bf16[512,128]{1,0:T(8,128)(2,1)S(1)}, u32[]{:S(2)}, u32[]{:S(2)}) collective-permute-start(bf16[512,128]{1,0:T(8,128)(2,1)S(1)} %pad_maximum_fusion.oth_ref), channel_id=1, source_target_pairs={{0,8},{16,24},{32,40},{48,56},{64,72},{80,88},{96,104},{112,120},{... | collective-permute-start | bytes 393224 | tf_op jit(solution)/shard_map/ppermute | solution.py:220
  9.8 5.0 %collective-permute-done.one_ref = bf16[528,128]{1,0:T(8,128)(2,1)S(1)} collective-permute-done((bf16[528,128]{1,0:T(8,128)(2,1)S(1)}, bf16[528,128]{1,0:T(8,128)(2,1)S(1)}, u32[]{:S(2)}, u32[]{:S(2)}) %collective-permute-start) | collective-permute-done | bytes 135200 | tf_op jit(solution)/shard_map/ppermute | solution.py:220
  14.8 0.7 collective-permute-start.2
  15.5 1.9 %collective-permute-start.3 = (bf16[528,128]{1,0:T(8,128)(2,1)S(1)}, bf16[528,128]{1,0:T(8,128)(2,1)S(1)}, u32[]{:S(2)}, u32[]{:S(2)}) collective-permute-start(bf16[528,128]{1,0:T(8,128)(2,1)S(1)} %collective-permute-done.one_ref), channel_id=1, source_target_pairs={{0,8},{8,16},{16,24},{24,32},{32,40},{40,48},{48,56},{56,64},{64,7... | collective-permute-start | bytes 405512 | tf_op jit(solution)/shard_map/ppermute | solution.py:220
  17.4 0.0 collective-permute-done.1._.other_ref
  17.4 0.0 copy-start.1
  17.4 1.2 %copy-done.1 = bf16[1,128,4096]{2,1,0:T(8,128)(2,1)S(1)} copy-done((bf16[1,128,4096]{2,1,0:T(8,128)(2,1)S(1)}, bf16[1,128,4096]{2,1,0:T(8,128)(2,1)}, u32[]{:S(2)}) %copy-start.1) | copy-done | bytes 1048600
  18.6 1.3 %short.1 = (bf16[128,2048]{1,0:T(8,128)(2,1)S(1)}, bf16[288,128]{1,0:T(8,128)(2,1)S(1)}, bf16[512,128]{1,0:T(8,128)(2,1)S(1)}, bf16[512,128]{1,0:T(8,128)(2,1)S(1)}) custom-call(bf16[16,128]{1,0:T(8,128)(2,1)S(1)} %bitcast.21, bf16[528,128]{1,0:T(8,128)(2,1)S(1)} %constant_dynamic-update-slice_fusion.sel_ref, ...), custom_call_target="tpu_custom_call" | custom-call | flops 700000000 | bytes 3000000 | tf_op jit(solution)/shard_map/short/pallas_call | solution.py:247
  20.0 0.0 collective-permute-done.2.three_ref
  20.0 6.3 %collective-permute-done.3.two_ref = bf16[528,128]{1,0:T(8,128)(2,1)S(1)} collective-permute-done((bf16[528,128]{1,0:T(8,128)(2,1)S(1)}, bf16[528,128]{1,0:T(8,128)(2,1)S(1)}, u32[]{:S(2)}, u32[]{:S(2)}) %collective-permute-start.3) | collective-permute-done | bytes 135200 | tf_op jit(solution)/shard_map/ppermute | solution.py:220
  26.2 0.0 copy-done.2
  26.2 3.8 %long.1 = (bf16[128,2048]{1,0:T(8,128)(2,1)S(1)}, bf16[768,128]{1,0:T(8,128)(2,1)}, bf16[512,128]{1,0:T(8,128)(2,1)S(1)}, bf16[1024,128]{1,0:T(8,128)(2,1)S(1)}, bf16[1024,128]{1,0:T(8,128)(2,1)S(1)}) custom-call(bf16[16,128]{1,0:T(8,128)(2,1)S(1)} %bitcast.22, bf16[528,128]{1,0:T(8,128)(2,1)S(1)} %constant_dynamic-update-slice_fusion.sel_ref, ...), custom_call_target="tpu_custom_call" | custom-call | flops 1400000000 | bytes 4000000 | tf_op jit(solution)/shard_map/long/pallas_call | solution.py:264
  30.1 9.6 %all-to-all-start = ((bf16[32,24,128]{2,1,0:T(8,128)(2,1)}), bf16[32,24,128]{2,1,0:T(8,128)(2,1)S(1)}, u32[]{:S(2)}, u32[]{:S(2)}) async-start(bf16[32,24,128]{2,1,0:T(8,128)(2,1)} %bitcast.12), calls=%async_computation | async-start | bytes 393216 | tf_op jit(solution)/shard_map/all_to_all | solution.py:320
  39.7 5.6 %collective-permute-start.5 = (bf16[1024,128]{1,0:T(8,128)(2,1)S(1)}, bf16[1024,128]{1,0:T(8,128)(2,1)S(1)}, u32[]{:S(2)}, u32[]{:S(2)}) collective-permute-start(bf16[1024,128]{1,0:T(8,128)(2,1)S(1)} %get-tuple-element.26), channel_id=1, source_target_pairs={{0,496},{8,504},{16,0},{24,8},{32,16},{40,24},{48,32},{56,40},{64,... | collective-permute-start | bytes 786440 | tf_op jit(solution)/shard_map/ppermute | solution.py:220
  45.3 1.9 %collective-permute-start.4 = (bf16[1024,128]{1,0:T(8,128)(2,1)S(1)}, bf16[1024,128]{1,0:T(8,128)(2,1)S(1)}, u32[]{:S(2)}, u32[]{:S(2)}) collective-permute-start(bf16[1024,128]{1,0:T(8,128)(2,1)S(1)} %get-tuple-element.25), channel_id=1, source_target_pairs={{0,504},{8,0},{16,8},{24,16},{32,24},{40,32},{48,40},{56,48},{64,5... | collective-permute-start | bytes 786440 | tf_op jit(solution)/shard_map/ppermute | solution.py:220
  47.2 0.4 all-to-all-done
  47.7 0.7 broadcast_in_dim.24
  48.3 8.2 %all-to-all-start.1 = ((bf16[16,24,128]{2,1,0:T(8,128)(2,1)}), bf16[16,24,128]{2,1,0:T(8,128)(2,1)S(1)}, u32[]{:S(2)}, u32[]{:S(2)}) async-start(bf16[16,24,128]{2,1,0:T(8,128)(2,1)} %broadcast_in_dim.24), calls=%async_computation.1 | async-start | bytes 196608 | tf_op jit(solution)/shard_map/all_to_all | solution.py:311
  56.6 0.0 collective-permute-done.5.r2_ref
  56.6 1.3 %collective-permute-start.6 = (bf16[512,128]{1,0:T(8,128)(2,1)S(1)}, bf16[512,128]{1,0:T(8,128)(2,1)S(1)}, u32[]{:S(2)}, u32[]{:S(2)}) collective-permute-start(bf16[512,128]{1,0:T(8,128)(2,1)S(1)} %slice.68), channel_id=1, source_target_pairs={{8,0},{24,16},{40,32},{56,48},{72,64},{88,80},{104,96},{120,112},{... | collective-permute-start | bytes 393224 | tf_op jit(solution)/shard_map/ppermute | solution.py:220
  57.9 10.2 %all-to-all-done.1 = bf16[16,24,128]{2,1,0:T(8,128)(2,1)S(1)} async-done(((bf16[16,24,128]{2,1,0:T(8,128)(2,1)}), bf16[16,24,128]{2,1,0:T(8,128)(2,1)S(1)}, u32[]{:S(2)}, u32[]{:S(2)}) %all-to-all-start.1) | async-done | bytes 98336 | tf_op jit(solution)/shard_map/all_to_all | solution.py:311
  68.2 0.7 broadcast_in_dim.25
  68.9 7.9 %all-to-all-start.2 = ((bf16[32,24,128]{2,1,0:T(8,128)(2,1)}), bf16[32,24,128]{2,1,0:T(8,128)(2,1)S(1)}, u32[]{:S(2)}, u32[]{:S(2)}) async-start(bf16[32,24,128]{2,1,0:T(8,128)(2,1)} %broadcast_in_dim.25), calls=%async_computation.2 | async-start | bytes 393216 | tf_op jit(solution)/shard_map/all_to_all | solution.py:311
  76.7 0.0 collective-permute-done.4.r1_ref
  76.7 0.0 collective-permute-done.6.r3_ref
  76.8 1.7 %gradients_out.1 = (bf16[128,4096]{1,0:T(8,128)(2,1)}, bf16[128,512]{1,0:T(8,128)(2,1)}, bf16[128,512]{1,0:T(8,128)(2,1)}) custom-call(bf16[128,2048]{1,0:T(8,128)(2,1)S(1)} %get-tuple-element.19.dq_short_ref, bf16[128,2048]{1,0:T(8,128)(2,1)S(1)} %get-tuple-element.22.dq_long_ref, bf16[512,128]{1,0:T(8,128)(2,1)S(1)} %get-tuple-element.23.short_ref, ...), custom_call_target="tpu_custom_call" | custom-call | flops 20000000000 | bytes 2000000 | tf_op jit(solution)/shard_map/gradients_out/pallas_call | solution.py:283
  78.5 6.1 %all-to-all-done.2 = bf16[32,24,128]{2,1,0:T(8,128)(2,1)S(1)} async-done(((bf16[32,24,128]{2,1,0:T(8,128)(2,1)}), bf16[32,24,128]{2,1,0:T(8,128)(2,1)S(1)}, u32[]{:S(2)}, u32[]{:S(2)}) %all-to-all-start.2) | async-done | bytes 196640 | tf_op jit(solution)/shard_map/all_to_all | solution.py:311
  84.6 0.7 adapter_out.1
  (14 shorter events, 0.1 us)
Async XLA Ops:
  0.6 16.8 %copy-start = (bf16[1,128,4096]{2,1,0:T(8,128)(2,1)S(1)}, bf16[1,128,4096]{2,1,0:T(8,128)(2,1)}, u32[]{:S(2)}) copy-start(bf16[1,128,4096]{2,1,0:T(8,128)(2,1)} %param.6) | copy-start | bytes 3145732
  2.5 12.3 %collective-permute-start = (bf16[528,128]{1,0:T(8,128)(2,1)S(1)}, bf16[528,128]{1,0:T(8,128)(2,1)S(1)}, u32[]{:S(2)}, u32[]{:S(2)}) collective-permute-start(bf16[528,128]{1,0:T(8,128)(2,1)S(1)} %constant_dynamic-update-slice_fusion.sel_ref), channel_id=1, source_target_pairs={{0,8},{8,16},{16,24},{24,32},{32,40},{40,48},{48,56},{56,64},{64,7... | collective-permute-start | bytes 405512 | tf_op jit(solution)/shard_map/ppermute | solution.py:220
  6.6 10.8 %copy-start.3 = (bf16[1,128,16]{1,2,0:T(8,128)(2,1)S(1)}, bf16[1,128,16]{1,2,0:T(8,128)(2,1)}, u32[]{:S(2)}) copy-start(bf16[1,128,16]{1,2,0:T(8,128)(2,1)} %param.10) | copy-start | bytes 12292
  6.6 10.8 %collective-permute-start.1 = (bf16[512,128]{1,0:T(8,128)(2,1)S(1)}, bf16[512,128]{1,0:T(8,128)(2,1)S(1)}, u32[]{:S(2)}, u32[]{:S(2)}) collective-permute-start(bf16[512,128]{1,0:T(8,128)(2,1)S(1)} %pad_maximum_fusion.oth_ref), channel_id=1, source_target_pairs={{0,8},{16,24},{32,40},{48,56},{64,72},{80,88},{96,104},{112,120},{... | collective-permute-start | bytes 393224 | tf_op jit(solution)/shard_map/ppermute | solution.py:220
  14.8 5.2 %collective-permute-start.2 = (bf16[528,128]{1,0:T(8,128)(2,1)S(1)}, bf16[528,128]{1,0:T(8,128)(2,1)S(1)}, u32[]{:S(2)}, u32[]{:S(2)}) collective-permute-start(bf16[528,128]{1,0:T(8,128)(2,1)S(1)} %collective-permute-done.one_ref), channel_id=1, source_target_pairs={{8,24},{24,40},{40,56},{56,72},{72,88},{88,104},{104,120},{120,136... | collective-permute-start | bytes 405512 | tf_op jit(solution)/shard_map/ppermute | solution.py:220
  15.5 10.8 %collective-permute-start.3 = (bf16[528,128]{1,0:T(8,128)(2,1)S(1)}, bf16[528,128]{1,0:T(8,128)(2,1)S(1)}, u32[]{:S(2)}, u32[]{:S(2)}) collective-permute-start(bf16[528,128]{1,0:T(8,128)(2,1)S(1)} %collective-permute-done.one_ref), channel_id=1, source_target_pairs={{0,8},{8,16},{16,24},{24,32},{32,40},{40,48},{48,56},{56,64},{64,7... | collective-permute-start | bytes 405512 | tf_op jit(solution)/shard_map/ppermute | solution.py:220
  17.4 1.2 %copy-start.1 = (bf16[1,128,4096]{2,1,0:T(8,128)(2,1)S(1)}, bf16[1,128,4096]{2,1,0:T(8,128)(2,1)}, u32[]{:S(2)}) copy-start(bf16[1,128,4096]{2,1,0:T(8,128)(2,1)} %param.9) | copy-start | bytes 3145732
  18.6 7.6 %copy-start.2 = (bf16[1,128,4096]{2,1,0:T(8,128)(2,1)S(1)}, bf16[1,128,4096]{2,1,0:T(8,128)(2,1)}, u32[]{:S(2)}) copy-start(bf16[1,128,4096]{2,1,0:T(8,128)(2,1)} %param.9) | copy-start | bytes 3145732
  30.1 17.6 %all-to-all-start = ((bf16[32,24,128]{2,1,0:T(8,128)(2,1)}), bf16[32,24,128]{2,1,0:T(8,128)(2,1)S(1)}, u32[]{:S(2)}, u32[]{:S(2)}) async-start(bf16[32,24,128]{2,1,0:T(8,128)(2,1)} %bitcast.12), calls=%async_computation | async-start | bytes 393216 | tf_op jit(solution)/shard_map/all_to_all | solution.py:320
  39.7 16.9 %collective-permute-start.5 = (bf16[1024,128]{1,0:T(8,128)(2,1)S(1)}, bf16[1024,128]{1,0:T(8,128)(2,1)S(1)}, u32[]{:S(2)}, u32[]{:S(2)}) collective-permute-start(bf16[1024,128]{1,0:T(8,128)(2,1)S(1)} %get-tuple-element.26), channel_id=1, source_target_pairs={{0,496},{8,504},{16,0},{24,8},{32,16},{40,24},{48,32},{56,40},{64,... | collective-permute-start | bytes 786440 | tf_op jit(solution)/shard_map/ppermute | solution.py:220
  45.3 31.4 %collective-permute-start.4 = (bf16[1024,128]{1,0:T(8,128)(2,1)S(1)}, bf16[1024,128]{1,0:T(8,128)(2,1)S(1)}, u32[]{:S(2)}, u32[]{:S(2)}) collective-permute-start(bf16[1024,128]{1,0:T(8,128)(2,1)S(1)} %get-tuple-element.25), channel_id=1, source_target_pairs={{0,504},{8,0},{16,8},{24,16},{32,24},{40,32},{48,40},{56,48},{64,5... | collective-permute-start | bytes 786440 | tf_op jit(solution)/shard_map/ppermute | solution.py:220
  48.3 19.8 %all-to-all-start.1 = ((bf16[16,24,128]{2,1,0:T(8,128)(2,1)}), bf16[16,24,128]{2,1,0:T(8,128)(2,1)S(1)}, u32[]{:S(2)}, u32[]{:S(2)}) async-start(bf16[16,24,128]{2,1,0:T(8,128)(2,1)} %broadcast_in_dim.24), calls=%async_computation.1 | async-start | bytes 196608 | tf_op jit(solution)/shard_map/all_to_all | solution.py:311
  56.6 20.1 %collective-permute-start.6 = (bf16[512,128]{1,0:T(8,128)(2,1)S(1)}, bf16[512,128]{1,0:T(8,128)(2,1)S(1)}, u32[]{:S(2)}, u32[]{:S(2)}) collective-permute-start(bf16[512,128]{1,0:T(8,128)(2,1)S(1)} %slice.68), channel_id=1, source_target_pairs={{8,0},{24,16},{40,32},{56,48},{72,64},{88,80},{104,96},{120,112},{... | collective-permute-start | bytes 393224 | tf_op jit(solution)/shard_map/ppermute | solution.py:220
  68.9 15.7 %all-to-all-start.2 = ((bf16[32,24,128]{2,1,0:T(8,128)(2,1)}), bf16[32,24,128]{2,1,0:T(8,128)(2,1)S(1)}, u32[]{:S(2)}, u32[]{:S(2)}) async-start(bf16[32,24,128]{2,1,0:T(8,128)(2,1)} %broadcast_in_dim.25), calls=%async_computation.2 | async-start | bytes 393216 | tf_op jit(solution)/shard_map/all_to_all | solution.py:311

commit v10 on v8

--- a/solution.py
+++ b/solution.py
@@ -174,8 +174,12 @@
         r1_ref[:UNIT, :] = backs_ref[...]
 
 
+def add_kernel(own_ref, r2_ref, out_ref):
+    out_ref[...] = own_ref[...].astype(f32) + r2_ref[...].astype(f32)
+
+
 def gradients_kernel(
-    dq_short_ref, dq_long_ref, short_ref, long_ref, r1_ref, r2_ref, r3_ref, dq_hbm, dk_ref, dv_ref, sems
+    dq_short_ref, dq_long_ref, short_ref, long_ref, r1_ref, r3_ref, dq_hbm, dk_ref, dv_ref, sems
 ):
     short, odd = group_place()
     even = odd == 0
@@ -191,8 +195,7 @@
         for h in range(2):
             base = (part * 2 + h) * ROWS
             rows = slice(base, base + ROWS)
-            total = short_ref[rows, :].astype(f32) + r1_ref[rows, :].astype(f32)
-            total = total + r2_ref[rows, :].astype(f32)
+            total = short_ref[rows, :] + r1_ref[rows, :].astype(f32)
             total = total + jnp.where(even, r3_ref[rows, :].astype(f32), 0.0)
             ref[:, head_columns(short * 2 + h)] = total.astype(bf16)
             other = r1_ref[UNIT + base : UNIT + base + ROWS, :].astype(f32)
@@ -279,11 +282,23 @@
     )(*operands)
 
 
+def add_second(*operands):
+    return pl.pallas_call(
+        add_kernel,
+        in_specs=[VMEM] * 2,
+        out_specs=VMEM,
+        out_shape=shape((UNIT, WIDTH), f32),
+        compiler_params=PARAMS,
+        cost_estimate=pl.CostEstimate(flops=SUM_FLOPS, bytes_accessed=500_000, transcendentals=0),
+        name="add_second",
+    )(*operands)
+
+
 def gradients_out(*operands):
     out = shape((ROWS, KEY_VALUE_HEADS * WIDTH))
     return pl.pallas_call(
         gradients_kernel,
-        in_specs=[VMEM] * 7,
+        in_specs=[VMEM] * 6,
         out_specs=[HBM, VMEM, VMEM],
         out_shape=[shape((ROWS, 2 * HALF_COLUMNS)), out, out],
         scratch_shapes=[pltpu.SemaphoreType.DMA((2,))],
@@ -316,11 +331,13 @@
     return jnp.sum(pieces.astype(f32), axis=0).astype(bf16)
 
 
-def sum_over_all(part):
+def sum_near(part):
     size = lax.axis_size(NEAR)
-    mine = summed(lax.all_to_all(part.reshape(size, part.shape[0] // size, WIDTH), NEAR, 0, 0))
-    mine = summed(copies_to_all(mine, FAR))
-    return copies_to_all(mine, NEAR).reshape(part.shape)
+    return summed(lax.all_to_all(part.reshape(size, part.shape[0] // size, WIDTH), NEAR, 0, 0))
+
+
+def sum_far(mine):
+    return summed(copies_to_all(mine, FAR))
 
 
 def body(queries, keys, values, output_gradient, adapter_query_down, adapter_value_down):
@@ -336,9 +353,11 @@
     )
     r1 = passed_along(r1, -1)
     r2 = passed_along(r2, -2)
+    mine, r3 = lax.optimization_barrier((sum_near(part), r3))
     r3 = passed_along(r3, -3, range(1, CTX_SIZE, 2))
-    dq, dk, dv = gradients_out(dq_short, dq_long, own_short, own_long, r1, r2, r3)
-    total = sum_over_all(part)
+    mine, sums_short = lax.optimization_barrier((sum_far(mine), add_second(own_short, r2)))
+    total = copies_to_all(mine, NEAR).reshape(part.shape)
+    dq, dk, dv = gradients_out(dq_short, dq_long, sums_short, own_long, r1, r3)
     adapter_q, adapter_v = adapter_out(total)
     return dq[None], dk[None], dv[None], adapter_q, adapter_v
 

time: 83.4 us -> 84.8 us (1.017)
  waiting for transfers between devices: 24.1 us -> 28 us
  starting transfers between devices: 45.7 us -> 43.3 us
    all_to_all x2, waiting for transfers between devices: 8.15 us -> 16.3 us  [copies_to_all(): lax.all_to_all(jnp.broadcast_to(block[None], (size,) + block.shape), axes...]
    ppermute x7, starting transfers between devices: 22.6 us -> 18.6 us  [passed_along(): lax.ppermute(block, CTX, [(i, (i + distance) % CTX_SIZE) for i in senders])]
    ppermute x7, waiting for transfers between devices: 13.7 us -> 11.3 us  [passed_along(): lax.ppermute(block, CTX, [(i, (i + distance) % CTX_SIZE) for i in senders])]
    all_to_all x1, waiting for transfers between devices: 2.33 us -> 0.4 us  [sum_near(): lax.all_to_all(part.reshape(size, part.shape[0] // size, WIDTH), NEAR, 0, 0)]
    all_to_all x2, starting transfers between devices: 13.5 us -> 15.1 us  [copies_to_all(): lax.all_to_all(jnp.broadcast_to(block[None], (size,) + block.shape), axes...]
    pallas_call x1 -> x2, Pallas kernels: 1.71 us -> 1.75 us  [the longest x1 1.72 us: gradients_out(): pl.pallas_call(gradients_kernel, in_specs=[VMEM] * 6, out_specs=[HBM, VME...]
  transfers between devices with their start and end apart: 10 -> 10, of which waited for: 6 -> 5; matrix products, arithmetic and copies ran while one was open for 2% -> 2% of each run, Pallas kernels for 4% -> 4%
where the time goes in v10:
time: 84.8 us; the launch traced here: 84.3 us
  starting transfers between devices  43.3 us (51%)
  waiting for transfers between devices  28 us (33%)
  Pallas kernels  7.61 us (9%)
  local copies, waits for them, and re-layouts  3.34 us (4%)
  other arithmetic  1.11 us (1%)
  between operations  0.9 us (1%)
    ppermute x7, starting transfers between devices, passed_along(): lax.ppermute(block, CTX, [(i, (i + distance) % CTX_SIZE) for i in senders])  18.6 us
    all_to_all x2, waiting for transfers between devices, copies_to_all(): lax.all_to_all(jnp.broadcast_to(block[None], (size,) + block.shape), axes...  16.3 us
    all_to_all x2, starting transfers between devices, copies_to_all(): lax.all_to_all(jnp.broadcast_to(block[None], (size,) + block.shape), axes...  15.1 us
    ppermute x7, waiting for transfers between devices, passed_along(): lax.ppermute(block, CTX, [(i, (i + distance) % CTX_SIZE) for i in senders])  11.3 us
    all_to_all x1, starting transfers between devices, sum_near(): lax.all_to_all(part.reshape(size, part.shape[0] // size, WIDTH), NEAR, 0, 0)  9.61 us
    pallas_call x1, Pallas kernels, attend_long(): pl.pallas_call(long_kernel, in_specs=[VMEM] * 11, out_specs=[VMEM] * 6, o...  3.82 us
    pallas_call x1, Pallas kernels, gradients_out(): pl.pallas_call(gradients_kernel, in_specs=[VMEM] * 6, out_specs=[HBM, VME...  1.72 us
  transfers between devices with their start and end apart: 10, of which 5 were waited for; matrix products, arithmetic and copies ran while one was open for 2% of the time, Pallas kernels for 4%

profile of v10, /device:TPU:1, one launch (start us, length us, event | category | flops | bytes accessed | tf_op | source)
XLA Modules:
  0.0 84.3 jit_solution(5578250632961180920)
XLA Ops:
  0.7 1.0 %broadcast_select_fusion = (bf16[128,256]{1,0:T(8,128)(2,1)S(1)}, bf16[128,256]{1,0:T(8,128)(2,1)S(1)}, bf16[128,256]{1,0:T(8,128)(2,1)S(1)}, bf16[128,256]{1,0:T(8,128)(2,1)S(1)}) fusion(pred[]{:T(512)S(6)} %eq.9, bf16[128,512]{1,0:T(8,128)(2,1)} %bitcast.23, pred[]{:T(512)S(6)} %eq.8, bf16[128,512]{1,0:T(8,128)(2,1)} %bitcast.24), kind=kLoop, calls=%fused_computation.1 | loop fusion | flops 131072 | bytes 524290 | tf_op jit(solution)/shard_map/jit(_where)/select_n | solution.py:238
  1.8 0.7 constant_dynamic-update-slice_fusion.sel_ref
  2.5 4.0 %collective-permute-start = (bf16[528,128]{1,0:T(8,128)(2,1)S(1)}, bf16[528,128]{1,0:T(8,128)(2,1)S(1)}, u32[]{:S(2)}, u32[]{:S(2)}) collective-permute-start(bf16[528,128]{1,0:T(8,128)(2,1)S(1)} %constant_dynamic-update-slice_fusion.sel_ref), channel_id=1, source_target_pairs={{0,8},{8,16},{16,24},{24,32},{32,40},{40,48},{48,56},{56,64},{64,7... | collective-permute-start | bytes 405512 | tf_op jit(solution)/shard_map/ppermute | solution.py:223
  6.6 0.0 copy-start.3
  6.6 3.2 %collective-permute-start.1 = (bf16[512,128]{1,0:T(8,128)(2,1)S(1)}, bf16[512,128]{1,0:T(8,128)(2,1)S(1)}, u32[]{:S(2)}, u32[]{:S(2)}) collective-permute-start(bf16[512,128]{1,0:T(8,128)(2,1)S(1)} %pad_maximum_fusion.oth_ref), channel_id=1, source_target_pairs={{0,8},{16,24},{32,40},{48,56},{64,72},{80,88},{96,104},{112,120},{... | collective-permute-start | bytes 393224 | tf_op jit(solution)/shard_map/ppermute | solution.py:223
  9.8 5.0 %collective-permute-done.one_ref = bf16[528,128]{1,0:T(8,128)(2,1)S(1)} collective-permute-done((bf16[528,128]{1,0:T(8,128)(2,1)S(1)}, bf16[528,128]{1,0:T(8,128)(2,1)S(1)}, u32[]{:S(2)}, u32[]{:S(2)}) %collective-permute-start) | collective-permute-done | bytes 135200 | tf_op jit(solution)/shard_map/ppermute | solution.py:223
  14.8 0.7 collective-permute-start.2
  15.5 1.9 %collective-permute-start.3 = (bf16[528,128]{1,0:T(8,128)(2,1)S(1)}, bf16[528,128]{1,0:T(8,128)(2,1)S(1)}, u32[]{:S(2)}, u32[]{:S(2)}) collective-permute-start(bf16[528,128]{1,0:T(8,128)(2,1)S(1)} %collective-permute-done.one_ref), channel_id=1, source_target_pairs={{0,8},{8,16},{16,24},{24,32},{32,40},{40,48},{48,56},{56,64},{64,7... | collective-permute-start | bytes 405512 | tf_op jit(solution)/shard_map/ppermute | solution.py:223
  17.4 0.0 collective-permute-done.1._.other_ref
  17.4 0.0 copy-start.1
  17.4 1.2 %copy-done.1 = bf16[1,128,4096]{2,1,0:T(8,128)(2,1)S(1)} copy-done((bf16[1,128,4096]{2,1,0:T(8,128)(2,1)S(1)}, bf16[1,128,4096]{2,1,0:T(8,128)(2,1)}, u32[]{:S(2)}) %copy-start.1) | copy-done | bytes 1048600
  18.6 1.3 %short.1 = (bf16[128,2048]{1,0:T(8,128)(2,1)S(1)}, bf16[288,128]{1,0:T(8,128)(2,1)S(1)}, bf16[512,128]{1,0:T(8,128)(2,1)S(1)}, bf16[512,128]{1,0:T(8,128)(2,1)S(1)}) custom-call(bf16[16,128]{1,0:T(8,128)(2,1)S(1)} %bitcast.21, bf16[528,128]{1,0:T(8,128)(2,1)S(1)} %constant_dynamic-update-slice_fusion.sel_ref, ...), custom_call_target="tpu_custom_call" | custom-call | flops 700000000 | bytes 3000000 | tf_op jit(solution)/shard_map/short/pallas_call | solution.py:250
  20.0 0.0 collective-permute-done.2.three_ref
  20.0 6.3 %collective-permute-done.3.two_ref = bf16[528,128]{1,0:T(8,128)(2,1)S(1)} collective-permute-done((bf16[528,128]{1,0:T(8,128)(2,1)S(1)}, bf16[528,128]{1,0:T(8,128)(2,1)S(1)}, u32[]{:S(2)}, u32[]{:S(2)}) %collective-permute-start.3) | collective-permute-done | bytes 135200 | tf_op jit(solution)/shard_map/ppermute | solution.py:223
  26.2 0.0 copy-done.2
  26.2 3.8 %long.1 = (bf16[128,2048]{1,0:T(8,128)(2,1)S(1)}, bf16[768,128]{1,0:T(8,128)(2,1)}, bf16[512,128]{1,0:T(8,128)(2,1)S(1)}, bf16[1024,128]{1,0:T(8,128)(2,1)S(1)},...) custom-call(bf16[16,128]{1,0:T(8,128)(2,1)S(1)} %bitcast.22, ...), custom_call_target="tpu_custom_call" | custom-call | flops 1400000000 | bytes 4000000 | tf_op jit(solution)/shard_map/long/pallas_call | solution.py:267
  30.1 9.6 %all-to-all-start = ((bf16[32,24,128]{2,1,0:T(8,128)(2,1)}), bf16[32,24,128]{2,1,0:T(8,128)(2,1)S(1)}, u32[]{:S(2)}, u32[]{:S(2)}) async-start(bf16[32,24,128]{2,1,0:T(8,128)(2,1)} %bitcast.9), calls=%async_computation | async-start | bytes 393216 | tf_op jit(solution)/shard_map/all_to_all | solution.py:336
  39.7 5.6 %collective-permute-start.4 = (bf16[512,128]{1,0:T(8,128)(2,1)S(1)}, bf16[512,128]{1,0:T(8,128)(2,1)S(1)}, u32[]{:S(2)}, u32[]{:S(2)}) collective-permute-start(bf16[512,128]{1,0:T(8,128)(2,1)S(1)} %get-tuple-element.32), channel_id=1, source_target_pairs={{0,496},{8,504},{16,0},{24,8},{32,16},{40,24},{48,32},{56,40},{64,... | collective-permute-start | bytes 393224 | tf_op jit(solution)/shard_map/ppermute | solution.py:223
  45.3 1.9 %collective-permute-start.5 = (bf16[1024,128]{1,0:T(8,128)(2,1)S(1)}, bf16[1024,128]{1,0:T(8,128)(2,1)S(1)}, u32[]{:S(2)}, u32[]{:S(2)}) collective-permute-start(bf16[1024,128]{1,0:T(8,128)(2,1)S(1)} %get-tuple-element.35), channel_id=1, source_target_pairs={{0,504},{8,0},{16,8},{24,16},{32,24},{40,32},{48,40},{56,48},{64,5... | collective-permute-start | bytes 786440 | tf_op jit(solution)/shard_map/ppermute | solution.py:223
  47.2 0.4 all-to-all-done
  47.7 0.7 broadcast_in_dim.10
  48.3 8.2 %all-to-all-start.1 = ((bf16[16,24,128]{2,1,0:T(8,128)(2,1)}), bf16[16,24,128]{2,1,0:T(8,128)(2,1)S(1)}, u32[]{:S(2)}, u32[]{:S(2)}) async-start(bf16[16,24,128]{2,1,0:T(8,128)(2,1)} %broadcast_in_dim.10), calls=%async_computation.1 | async-start | bytes 196608 | tf_op jit(solution)/shard_map/all_to_all | solution.py:327
  56.6 1.3 %collective-permute-start.6 = (bf16[512,128]{1,0:T(8,128)(2,1)S(1)}, bf16[512,128]{1,0:T(8,128)(2,1)S(1)}, u32[]{:S(2)}, u32[]{:S(2)}) collective-permute-start(bf16[512,128]{1,0:T(8,128)(2,1)S(1)} %get-tuple-element.36), channel_id=1, source_target_pairs={{8,496},{24,0},{40,16},{56,32},{72,48},{88,64},{104,80},{120,96},{... | collective-permute-start | bytes 393224 | tf_op jit(solution)/shard_map/ppermute | solution.py:223
  57.9 0.0 collective-permute-done.4.r2_ref
  57.9 10.2 %all-to-all-done.1 = bf16[16,24,128]{2,1,0:T(8,128)(2,1)S(1)} async-done(((bf16[16,24,128]{2,1,0:T(8,128)(2,1)}), bf16[16,24,128]{2,1,0:T(8,128)(2,1)S(1)}, u32[]{:S(2)}, u32[]{:S(2)}) %all-to-all-start.1) | async-done | bytes 98336 | tf_op jit(solution)/shard_map/all_to_all | solution.py:327
  68.2 0.7 broadcast_in_dim.25
  68.9 6.8 %all-to-all-start.2 = ((bf16[32,24,128]{2,1,0:T(8,128)(2,1)}), bf16[32,24,128]{2,1,0:T(8,128)(2,1)S(1)}, u32[]{:S(2)}, u32[]{:S(2)}) async-start(bf16[32,24,128]{2,1,0:T(8,128)(2,1)} %broadcast_in_dim.25), calls=%async_computation.2 | async-start | bytes 393216 | tf_op jit(solution)/shard_map/all_to_all | solution.py:327
  75.7 0.0 collective-permute-done.5.r1_ref
  75.7 0.0 collective-permute-done.6.r3_ref
  75.7 1.7 %gradients_out.1 = (bf16[128,4096]{1,0:T(8,128)(2,1)}, bf16[128,512]{1,0:T(8,128)(2,1)}, bf16[128,512]{1,0:T(8,128)(2,1)}) custom-call(bf16[128,2048]{1,0:T(8,128)(2,1)S(1)} %get-tuple-element.24.dq_short_ref, bf16[128,2048]{1,0:T(8,128)(2,1)S(1)} %get-tuple-element.27.dq_long_ref, f32[512,128]{1,0:T(8,128)S(1)} %add_second.1.short_ref, ...), custom_call_target="tpu_custom_call" | custom-call | flops 20000000000 | bytes 2000000 | tf_op jit(solution)/shard_map/gradients_out/pallas_call | solution.py:299
  77.4 6.1 %all-to-all-done.2 = bf16[32,24,128]{2,1,0:T(8,128)(2,1)S(1)} async-done(((bf16[32,24,128]{2,1,0:T(8,128)(2,1)}), bf16[32,24,128]{2,1,0:T(8,128)(2,1)S(1)}, u32[]{:S(2)}, u32[]{:S(2)}) %all-to-all-start.2) | async-done | bytes 196640 | tf_op jit(solution)/shard_map/all_to_all | solution.py:327
  83.5 0.7 adapter_out.1
  (14 shorter events, 0.2 us)
Async XLA Ops:
  0.6 16.8 %copy-start = (bf16[1,128,4096]{2,1,0:T(8,128)(2,1)S(1)}, bf16[1,128,4096]{2,1,0:T(8,128)(2,1)}, u32[]{:S(2)}) copy-start(bf16[1,128,4096]{2,1,0:T(8,128)(2,1)} %param.6) | copy-start | bytes 3145732
  2.5 12.3 %collective-permute-start = (bf16[528,128]{1,0:T(8,128)(2,1)S(1)}, bf16[528,128]{1,0:T(8,128)(2,1)S(1)}, u32[]{:S(2)}, u32[]{:S(2)}) collective-permute-start(bf16[528,128]{1,0:T(8,128)(2,1)S(1)} %constant_dynamic-update-slice_fusion.sel_ref), channel_id=1, source_target_pairs={{0,8},{8,16},{16,24},{24,32},{32,40},{40,48},{48,56},{56,64},{64,7... | collective-permute-start | bytes 405512 | tf_op jit(solution)/shard_map/ppermute | solution.py:223
  6.6 10.8 %copy-start.3 = (bf16[1,128,16]{1,2,0:T(8,128)(2,1)S(1)}, bf16[1,128,16]{1,2,0:T(8,128)(2,1)}, u32[]{:S(2)}) copy-start(bf16[1,128,16]{1,2,0:T(8,128)(2,1)} %param.10) | copy-start | bytes 12292
  6.6 10.8 %collective-permute-start.1 = (bf16[512,128]{1,0:T(8,128)(2,1)S(1)}, bf16[512,128]{1,0:T(8,128)(2,1)S(1)}, u32[]{:S(2)}, u32[]{:S(2)}) collective-permute-start(bf16[512,128]{1,0:T(8,128)(2,1)S(1)} %pad_maximum_fusion.oth_ref), channel_id=1, source_target_pairs={{0,8},{16,24},{32,40},{48,56},{64,72},{80,88},{96,104},{112,120},{... | collective-permute-start | bytes 393224 | tf_op jit(solution)/shard_map/ppermute | solution.py:223
  14.8 5.2 %collective-permute-start.2 = (bf16[528,128]{1,0:T(8,128)(2,1)S(1)}, bf16[528,128]{1,0:T(8,128)(2,1)S(1)}, u32[]{:S(2)}, u32[]{:S(2)}) collective-permute-start(bf16[528,128]{1,0:T(8,128)(2,1)S(1)} %collective-permute-done.one_ref), channel_id=1, source_target_pairs={{8,24},{24,40},{40,56},{56,72},{72,88},{88,104},{104,120},{120,136... | collective-permute-start | bytes 405512 | tf_op jit(solution)/shard_map/ppermute | solution.py:223
  15.5 10.8 %collective-permute-start.3 = (bf16[528,128]{1,0:T(8,128)(2,1)S(1)}, bf16[528,128]{1,0:T(8,128)(2,1)S(1)}, u32[]{:S(2)}, u32[]{:S(2)}) collective-permute-start(bf16[528,128]{1,0:T(8,128)(2,1)S(1)} %collective-permute-done.one_ref), channel_id=1, source_target_pairs={{0,8},{8,16},{16,24},{24,32},{32,40},{40,48},{48,56},{56,64},{64,7... | collective-permute-start | bytes 405512 | tf_op jit(solution)/shard_map/ppermute | solution.py:223
  17.4 1.2 %copy-start.1 = (bf16[1,128,4096]{2,1,0:T(8,128)(2,1)S(1)}, bf16[1,128,4096]{2,1,0:T(8,128)(2,1)}, u32[]{:S(2)}) copy-start(bf16[1,128,4096]{2,1,0:T(8,128)(2,1)} %param.9) | copy-start | bytes 3145732
  18.6 7.6 %copy-start.2 = (bf16[1,128,4096]{2,1,0:T(8,128)(2,1)S(1)}, bf16[1,128,4096]{2,1,0:T(8,128)(2,1)}, u32[]{:S(2)}) copy-start(bf16[1,128,4096]{2,1,0:T(8,128)(2,1)} %param.9) | copy-start | bytes 3145732
  30.1 17.6 %all-to-all-start = ((bf16[32,24,128]{2,1,0:T(8,128)(2,1)}), bf16[32,24,128]{2,1,0:T(8,128)(2,1)S(1)}, u32[]{:S(2)}, u32[]{:S(2)}) async-start(bf16[32,24,128]{2,1,0:T(8,128)(2,1)} %bitcast.9), calls=%async_computation | async-start | bytes 393216 | tf_op jit(solution)/shard_map/all_to_all | solution.py:336
  39.7 18.2 %collective-permute-start.4 = (bf16[512,128]{1,0:T(8,128)(2,1)S(1)}, bf16[512,128]{1,0:T(8,128)(2,1)S(1)}, u32[]{:S(2)}, u32[]{:S(2)}) collective-permute-start(bf16[512,128]{1,0:T(8,128)(2,1)S(1)} %get-tuple-element.32), channel_id=1, source_target_pairs={{0,496},{8,504},{16,0},{24,8},{32,16},{40,24},{48,32},{56,40},{64,... | collective-permute-start | bytes 393224 | tf_op jit(solution)/shard_map/ppermute | solution.py:223
  45.3 30.4 %collective-permute-start.5 = (bf16[1024,128]{1,0:T(8,128)(2,1)S(1)}, bf16[1024,128]{1,0:T(8,128)(2,1)S(1)}, u32[]{:S(2)}, u32[]{:S(2)}) collective-permute-start(bf16[1024,128]{1,0:T(8,128)(2,1)S(1)} %get-tuple-element.35), channel_id=1, source_target_pairs={{0,504},{8,0},{16,8},{24,16},{32,24},{40,32},{48,40},{56,48},{64,5... | collective-permute-start | bytes 786440 | tf_op jit(solution)/shard_map/ppermute | solution.py:223
  48.3 19.8 %all-to-all-start.1 = ((bf16[16,24,128]{2,1,0:T(8,128)(2,1)}), bf16[16,24,128]{2,1,0:T(8,128)(2,1)S(1)}, u32[]{:S(2)}, u32[]{:S(2)}) async-start(bf16[16,24,128]{2,1,0:T(8,128)(2,1)} %broadcast_in_dim.10), calls=%async_computation.1 | async-start | bytes 196608 | tf_op jit(solution)/shard_map/all_to_all | solution.py:327
  56.6 19.1 %collective-permute-start.6 = (bf16[512,128]{1,0:T(8,128)(2,1)S(1)}, bf16[512,128]{1,0:T(8,128)(2,1)S(1)}, u32[]{:S(2)}, u32[]{:S(2)}) collective-permute-start(bf16[512,128]{1,0:T(8,128)(2,1)S(1)} %get-tuple-element.36), channel_id=1, source_target_pairs={{8,496},{24,0},{40,16},{56,32},{72,48},{88,64},{104,80},{120,96},{... | collective-permute-start | bytes 393224 | tf_op jit(solution)/shard_map/ppermute | solution.py:223
  68.9 14.7 %all-to-all-start.2 = ((bf16[32,24,128]{2,1,0:T(8,128)(2,1)}), bf16[32,24,128]{2,1,0:T(8,128)(2,1)S(1)}, u32[]{:S(2)}, u32[]{:S(2)}) async-start(bf16[32,24,128]{2,1,0:T(8,128)(2,1)} %broadcast_in_dim.25), calls=%async_computation.2 | async-start | bytes 393216 | tf_op jit(solution)/shard_map/all_to_all | solution.py:327

commit v11 on v8

--- a/solution.py
+++ b/solution.py
@@ -328,8 +328,9 @@
     sel, oth = pack(group_place()[0], keys[0], values[0], adapter_value_down[0].T)
     one = passed_along(sel, 1)
     other = passed_along(oth, 1, range(0, CTX_SIZE, 2))
+    later, _ = lax.optimization_barrier((sel, oth))
+    two = passed_along(later, 2)
     three = passed_along(one, 2, range(1, CTX_SIZE, 2))
-    two = passed_along(one, 1)
     dq_short, ads, own_short, backs = attend_short(aq_t, sel, one, other, q, grad)
     dq_long, part, own_long, r1, r2, r3 = attend_long(
         aq_t, sel, oth, one, other, three, two, ads, backs, q, grad

time: 83.4 us -> 84.2 us (level)
  starting transfers between devices: 45.7 us -> 55.4 us
  waiting for transfers between devices: 24.1 us -> 15.2 us
    ppermute x7, waiting for transfers between devices: 13.7 us -> 5.66 us  [passed_along(): lax.ppermute(block, CTX, [(i, (i + distance) % CTX_SIZE) for i in senders])]
    ppermute x7, starting transfers between devices: 22.6 us -> 26.9 us  [passed_along(): lax.ppermute(block, CTX, [(i, (i + distance) % CTX_SIZE) for i in senders])]
    all_to_all x1, starting transfers between devices: 9.61 us -> 12.3 us  [sum_over_all(): lax.all_to_all(part.reshape(size, part.shape[0] // size, WIDTH), NEAR, 0, 0)]
    all_to_all x2, starting transfers between devices: 13.5 us -> 16.2 us  [copies_to_all(): lax.all_to_all(jnp.broadcast_to(block[None], (size,) + block.shape), axes...]
    all_to_all x1, waiting for transfers between devices: 2.33 us -> 1.42 us  [sum_over_all(): lax.all_to_all(part.reshape(size, part.shape[0] // size, WIDTH), NEAR, 0, 0)]
  transfers between devices with their start and end apart: 10 -> 10, of which waited for: 6 -> 5; matrix products, arithmetic and copies ran while one was open for 2% -> 2% of each run, Pallas kernels for 4% -> 4%
where the time goes in v11:
time: 84.2 us; the launch traced here: 83.6 us
  starting transfers between devices  55.4 us (66%)
  waiting for transfers between devices  15.2 us (18%)
  Pallas kernels  7.59 us (9%)
  local copies, waits for them, and re-layouts  3.34 us (4%)
  other arithmetic  1.11 us (1%)
  between operations  0.89 us (1%)
    ppermute x7, starting transfers between devices, passed_along(): lax.ppermute(block, CTX, [(i, (i + distance) % CTX_SIZE) for i in senders])  26.9 us
    all_to_all x2, starting transfers between devices, copies_to_all(): lax.all_to_all(jnp.broadcast_to(block[None], (size,) + block.shape), axes...  16.2 us
    all_to_all x1, starting transfers between devices, sum_over_all(): lax.all_to_all(part.reshape(size, part.shape[0] // size, WIDTH), NEAR, 0, 0)  12.3 us
    all_to_all x2, waiting for transfers between devices, copies_to_all(): lax.all_to_all(jnp.broadcast_to(block[None], (size,) + block.shape), axes...  8.15 us
    ppermute x7, waiting for transfers between devices, passed_along(): lax.ppermute(block, CTX, [(i, (i + distance) % CTX_SIZE) for i in senders])  5.66 us
    pallas_call x1, Pallas kernels, attend_long(): pl.pallas_call(long_kernel, in_specs=[VMEM] * 11, out_specs=[VMEM] * 6, o...  3.84 us
    pallas_call x1, Pallas kernels, gradients_out(): pl.pallas_call(gradients_kernel, in_specs=[VMEM] * 7, out_specs=[HBM, VME...  1.71 us
  transfers between devices with their start and end apart: 10, of which 5 were waited for; matrix products, arithmetic and copies ran while one was open for 2% of the time, Pallas kernels for 4%

profile of v11, /device:TPU:1, one launch (start us, length us, event | category | flops | bytes accessed | tf_op | source)
XLA Modules:
  0.0 83.6 jit_solution(1235497180202305178)
XLA Ops:
  0.7 1.0 %broadcast_select_fusion = (bf16[128,256]{1,0:T(8,128)(2,1)S(1)}, bf16[128,256]{1,0:T(8,128)(2,1)S(1)}, bf16[128,256]{1,0:T(8,128)(2,1)S(1)}, bf16[128,256]{1,0:T(8,128)(2,1)S(1)}) fusion(pred[]{:T(512)S(6)} %eq.9, bf16[128,512]{1,0:T(8,128)(2,1)} %bitcast.23, pred[]{:T(512)S(6)} %eq.8, bf16[128,512]{1,0:T(8,128)(2,1)} %bitcast.24), kind=kLoop, calls=%fused_computation.1 | loop fusion | flops 131072 | bytes 524290 | tf_op jit(solution)/shard_map/jit(_where)/select_n | solution.py:235
  1.8 0.7 constant_dynamic-update-slice_fusion.sel_ref
  2.5 4.0 %collective-permute-start = (bf16[528,128]{1,0:T(8,128)(2,1)S(1)}, bf16[528,128]{1,0:T(8,128)(2,1)S(1)}, u32[]{:S(2)}, u32[]{:S(2)}) collective-permute-start(bf16[528,128]{1,0:T(8,128)(2,1)S(1)} %constant_dynamic-update-slice_fusion.sel_ref), channel_id=1, source_target_pairs={{0,8},{8,16},{16,24},{24,32},{32,40},{40,48},{48,56},{56,64},{64,7... | collective-permute-start | bytes 405512 | tf_op jit(solution)/shard_map/ppermute | solution.py:220
  6.6 0.0 copy-start.3
  6.6 3.2 %collective-permute-start.1 = (bf16[512,128]{1,0:T(8,128)(2,1)S(1)}, bf16[512,128]{1,0:T(8,128)(2,1)S(1)}, u32[]{:S(2)}, u32[]{:S(2)}) collective-permute-start(bf16[512,128]{1,0:T(8,128)(2,1)S(1)} %pad_maximum_fusion.oth_ref), channel_id=1, source_target_pairs={{0,8},{16,24},{32,40},{48,56},{64,72},{80,88},{96,104},{112,120},{... | collective-permute-start | bytes 393224 | tf_op jit(solution)/shard_map/ppermute | solution.py:220
  9.8 5.4 %collective-permute-start.3 = (bf16[528,128]{1,0:T(8,128)(2,1)S(1)}, bf16[528,128]{1,0:T(8,128)(2,1)S(1)}, u32[]{:S(2)}, u32[]{:S(2)}) collective-permute-start(bf16[528,128]{1,0:T(8,128)(2,1)S(1)} %constant_dynamic-update-slice_fusion.sel_ref), channel_id=1, source_target_pairs={{0,16},{8,24},{16,32},{24,40},{32,48},{40,56},{48,64},{56,72},{64,... | collective-permute-start | bytes 405512 | tf_op jit(solution)/shard_map/ppermute | solution.py:220
  15.2 0.0 collective-permute-done.one_ref
  15.2 0.7 collective-permute-start.2
  15.9 0.0 collective-permute-done.1._.other_ref
  15.9 0.0 copy-start.1
  16.0 1.2 %copy-done.1 = bf16[1,128,4096]{2,1,0:T(8,128)(2,1)S(1)} copy-done((bf16[1,128,4096]{2,1,0:T(8,128)(2,1)S(1)}, bf16[1,128,4096]{2,1,0:T(8,128)(2,1)}, u32[]{:S(2)}) %copy-start.1) | copy-done | bytes 1048600
  17.2 1.3 %short.1 = (bf16[128,2048]{1,0:T(8,128)(2,1)S(1)}, bf16[288,128]{1,0:T(8,128)(2,1)S(1)}, bf16[512,128]{1,0:T(8,128)(2,1)S(1)}, bf16[512,128]{1,0:T(8,128)(2,1)S(1)}) custom-call(bf16[16,128]{1,0:T(8,128)(2,1)S(1)} %bitcast.21, bf16[528,128]{1,0:T(8,128)(2,1)S(1)} %constant_dynamic-update-slice_fusion.sel_ref, ...), custom_call_target="tpu_custom_call" | custom-call | flops 700000000 | bytes 3000000 | tf_op jit(solution)/shard_map/short/pallas_call | solution.py:247
  18.5 3.3 %collective-permute-done.3.two_ref = bf16[528,128]{1,0:T(8,128)(2,1)S(1)} collective-permute-done((bf16[528,128]{1,0:T(8,128)(2,1)S(1)}, bf16[528,128]{1,0:T(8,128)(2,1)S(1)}, u32[]{:S(2)}, u32[]{:S(2)}) %collective-permute-start.3) | collective-permute-done | bytes 135200 | tf_op jit(solution)/shard_map/ppermute | solution.py:220
  21.8 0.0 collective-permute-done.2.three_ref
  21.8 0.0 copy-done.2
  21.8 3.8 %long.1 = (bf16[128,2048]{1,0:T(8,128)(2,1)S(1)}, bf16[768,128]{1,0:T(8,128)(2,1)}, bf16[512,128]{1,0:T(8,128)(2,1)S(1)}, bf16[1024,128]{1,0:T(8,128)(2,1)S(1)},...) custom-call(bf16[16,128]{1,0:T(8,128)(2,1)S(1)} %bitcast.22, ...), custom_call_target="tpu_custom_call" | custom-call | flops 1400000000 | bytes 4000000 | tf_op jit(solution)/shard_map/long/pallas_call | solution.py:264
  25.6 12.3 %all-to-all-start = ((bf16[32,24,128]{2,1,0:T(8,128)(2,1)}), bf16[32,24,128]{2,1,0:T(8,128)(2,1)S(1)}, u32[]{:S(2)}, u32[]{:S(2)}) async-start(bf16[32,24,128]{2,1,0:T(8,128)(2,1)} %bitcast.12), calls=%async_computation | async-start | bytes 393216 | tf_op jit(solution)/shard_map/all_to_all | solution.py:321
  38.0 6.4 %collective-permute-start.4 = (bf16[1024,128]{1,0:T(8,128)(2,1)S(1)}, bf16[1024,128]{1,0:T(8,128)(2,1)S(1)}, u32[]{:S(2)}, u32[]{:S(2)}) collective-permute-start(bf16[1024,128]{1,0:T(8,128)(2,1)S(1)} %get-tuple-element.28), channel_id=1, source_target_pairs={{0,504},{8,0},{16,8},{24,16},{32,24},{40,32},{48,40},{56,48},{64,5... | collective-permute-start | bytes 786440 | tf_op jit(solution)/shard_map/ppermute | solution.py:220
  44.4 1.4 %all-to-all-done = bf16[32,24,128]{2,1,0:T(8,128)(2,1)S(1)} async-done(((bf16[32,24,128]{2,1,0:T(8,128)(2,1)}), bf16[32,24,128]{2,1,0:T(8,128)(2,1)S(1)}, u32[]{:S(2)}, u32[]{:S(2)}) %all-to-all-start) | async-done | bytes 196640 | tf_op jit(solution)/shard_map/all_to_all | solution.py:321
  45.8 0.7 broadcast_in_dim.24
  46.5 10.9 %all-to-all-start.1 = ((bf16[16,24,128]{2,1,0:T(8,128)(2,1)}), bf16[16,24,128]{2,1,0:T(8,128)(2,1)S(1)}, u32[]{:S(2)}, u32[]{:S(2)}) async-start(bf16[16,24,128]{2,1,0:T(8,128)(2,1)} %broadcast_in_dim.24), calls=%async_computation.1 | async-start | bytes 196608 | tf_op jit(solution)/shard_map/all_to_all | solution.py:312
  57.4 5.9 %collective-permute-start.5 = (bf16[512,128]{1,0:T(8,128)(2,1)S(1)}, bf16[512,128]{1,0:T(8,128)(2,1)S(1)}, u32[]{:S(2)}, u32[]{:S(2)}) collective-permute-start(bf16[512,128]{1,0:T(8,128)(2,1)S(1)} %get-tuple-element.29), channel_id=1, source_target_pairs={{0,496},{8,504},{16,0},{24,8},{32,16},{40,24},{48,32},{56,40},{64,... | collective-permute-start | bytes 393224 | tf_op jit(solution)/shard_map/ppermute | solution.py:220
  63.3 1.3 %collective-permute-start.6 = (bf16[512,128]{1,0:T(8,128)(2,1)S(1)}, bf16[512,128]{1,0:T(8,128)(2,1)S(1)}, u32[]{:S(2)}, u32[]{:S(2)}) collective-permute-start(bf16[512,128]{1,0:T(8,128)(2,1)S(1)} %get-tuple-element.30), channel_id=1, source_target_pairs={{8,496},{24,0},{40,16},{56,32},{72,48},{88,64},{104,80},{120,96},{... | collective-permute-start | bytes 393224 | tf_op jit(solution)/shard_map/ppermute | solution.py:220
  64.6 4.3 %all-to-all-done.1 = bf16[16,24,128]{2,1,0:T(8,128)(2,1)S(1)} async-done(((bf16[16,24,128]{2,1,0:T(8,128)(2,1)}), bf16[16,24,128]{2,1,0:T(8,128)(2,1)S(1)}, u32[]{:S(2)}, u32[]{:S(2)}) %all-to-all-start.1) | async-done | bytes 98336 | tf_op jit(solution)/shard_map/all_to_all | solution.py:312
  68.9 0.7 broadcast_in_dim.25
  69.6 5.3 %all-to-all-start.2 = ((bf16[32,24,128]{2,1,0:T(8,128)(2,1)}), bf16[32,24,128]{2,1,0:T(8,128)(2,1)S(1)}, u32[]{:S(2)}, u32[]{:S(2)}) async-start(bf16[32,24,128]{2,1,0:T(8,128)(2,1)} %broadcast_in_dim.25), calls=%async_computation.2 | async-start | bytes 393216 | tf_op jit(solution)/shard_map/all_to_all | solution.py:312
  74.9 0.0 collective-permute-done.5.r2_ref
  74.9 2.4 %collective-permute-done.6.r3_ref = bf16[512,128]{1,0:T(8,128)(2,1)S(1)} collective-permute-done((bf16[512,128]{1,0:T(8,128)(2,1)S(1)}, bf16[512,128]{1,0:T(8,128)(2,1)S(1)}, u32[]{:S(2)}, u32[]{:S(2)}) %collective-permute-start.6) | collective-permute-done | bytes 131104 | tf_op jit(solution)/shard_map/ppermute | solution.py:220
  77.3 0.0 collective-permute-done.4.r1_ref
  77.3 1.7 %gradients_out.1 = (bf16[128,4096]{1,0:T(8,128)(2,1)}, bf16[128,512]{1,0:T(8,128)(2,1)}, bf16[128,512]{1,0:T(8,128)(2,1)}) custom-call(bf16[128,2048]{1,0:T(8,128)(2,1)S(1)} %get-tuple-element.21.dq_short_ref, bf16[128,2048]{1,0:T(8,128)(2,1)S(1)} %get-tuple-element.25.dq_long_ref, bf16[512,128]{1,0:T(8,128)(2,1)S(1)} %get-tuple-element.26.short_ref, ...), custom_call_target="tpu_custom_call" | custom-call | flops 20000000000 | bytes 2000000 | tf_op jit(solution)/shard_map/gradients_out/pallas_call | solution.py:284
  79.0 3.8 %all-to-all-done.2 = bf16[32,24,128]{2,1,0:T(8,128)(2,1)S(1)} async-done(((bf16[32,24,128]{2,1,0:T(8,128)(2,1)}), bf16[32,24,128]{2,1,0:T(8,128)(2,1)S(1)}, u32[]{:S(2)}, u32[]{:S(2)}) %all-to-all-start.2) | async-done | bytes 196640 | tf_op jit(solution)/shard_map/all_to_all | solution.py:312
  82.9 0.7 adapter_out.1
  (13 shorter events, 0.1 us)
Async XLA Ops:
  0.6 15.3 %copy-start = (bf16[1,128,4096]{2,1,0:T(8,128)(2,1)S(1)}, bf16[1,128,4096]{2,1,0:T(8,128)(2,1)}, u32[]{:S(2)}) copy-start(bf16[1,128,4096]{2,1,0:T(8,128)(2,1)} %param.6) | copy-start | bytes 3145732
  2.5 12.7 %collective-permute-start = (bf16[528,128]{1,0:T(8,128)(2,1)S(1)}, bf16[528,128]{1,0:T(8,128)(2,1)S(1)}, u32[]{:S(2)}, u32[]{:S(2)}) collective-permute-start(bf16[528,128]{1,0:T(8,128)(2,1)S(1)} %constant_dynamic-update-slice_fusion.sel_ref), channel_id=1, source_target_pairs={{0,8},{8,16},{16,24},{24,32},{32,40},{40,48},{48,56},{56,64},{64,7... | collective-permute-start | bytes 405512 | tf_op jit(solution)/shard_map/ppermute | solution.py:220
  6.6 9.4 %copy-start.3 = (bf16[1,128,16]{1,2,0:T(8,128)(2,1)S(1)}, bf16[1,128,16]{1,2,0:T(8,128)(2,1)}, u32[]{:S(2)}) copy-start(bf16[1,128,16]{1,2,0:T(8,128)(2,1)} %param.10) | copy-start | bytes 12292
  6.6 9.3 %collective-permute-start.1 = (bf16[512,128]{1,0:T(8,128)(2,1)S(1)}, bf16[512,128]{1,0:T(8,128)(2,1)S(1)}, u32[]{:S(2)}, u32[]{:S(2)}) collective-permute-start(bf16[512,128]{1,0:T(8,128)(2,1)S(1)} %pad_maximum_fusion.oth_ref), channel_id=1, source_target_pairs={{0,8},{16,24},{32,40},{48,56},{64,72},{80,88},{96,104},{112,120},{... | collective-permute-start | bytes 393224 | tf_op jit(solution)/shard_map/ppermute | solution.py:220
  9.8 12.0 %collective-permute-start.3 = (bf16[528,128]{1,0:T(8,128)(2,1)S(1)}, bf16[528,128]{1,0:T(8,128)(2,1)S(1)}, u32[]{:S(2)}, u32[]{:S(2)}) collective-permute-start(bf16[528,128]{1,0:T(8,128)(2,1)S(1)} %constant_dynamic-update-slice_fusion.sel_ref), channel_id=1, source_target_pairs={{0,16},{8,24},{16,32},{24,40},{32,48},{40,56},{48,64},{56,72},{64,... | collective-permute-start | bytes 405512 | tf_op jit(solution)/shard_map/ppermute | solution.py:220
  15.2 6.5 %collective-permute-start.2 = (bf16[528,128]{1,0:T(8,128)(2,1)S(1)}, bf16[528,128]{1,0:T(8,128)(2,1)S(1)}, u32[]{:S(2)}, u32[]{:S(2)}) collective-permute-start(bf16[528,128]{1,0:T(8,128)(2,1)S(1)} %collective-permute-done.one_ref), channel_id=1, source_target_pairs={{8,24},{24,40},{40,56},{56,72},{72,88},{88,104},{104,120},{120,136... | collective-permute-start | bytes 405512 | tf_op jit(solution)/shard_map/ppermute | solution.py:220
  15.9 1.2 %copy-start.1 = (bf16[1,128,4096]{2,1,0:T(8,128)(2,1)S(1)}, bf16[1,128,4096]{2,1,0:T(8,128)(2,1)}, u32[]{:S(2)}) copy-start(bf16[1,128,4096]{2,1,0:T(8,128)(2,1)} %param.9) | copy-start | bytes 3145732
  17.2 4.6 %copy-start.2 = (bf16[1,128,4096]{2,1,0:T(8,128)(2,1)S(1)}, bf16[1,128,4096]{2,1,0:T(8,128)(2,1)}, u32[]{:S(2)}) copy-start(bf16[1,128,4096]{2,1,0:T(8,128)(2,1)} %param.9) | copy-start | bytes 3145732
  25.6 20.2 %all-to-all-start = ((bf16[32,24,128]{2,1,0:T(8,128)(2,1)}), bf16[32,24,128]{2,1,0:T(8,128)(2,1)S(1)}, u32[]{:S(2)}, u32[]{:S(2)}) async-start(bf16[32,24,128]{2,1,0:T(8,128)(2,1)} %bitcast.12), calls=%async_computation | async-start | bytes 393216 | tf_op jit(solution)/shard_map/all_to_all | solution.py:321
  38.0 39.4 %collective-permute-start.4 = (bf16[1024,128]{1,0:T(8,128)(2,1)S(1)}, bf16[1024,128]{1,0:T(8,128)(2,1)S(1)}, u32[]{:S(2)}, u32[]{:S(2)}) collective-permute-start(bf16[1024,128]{1,0:T(8,128)(2,1)S(1)} %get-tuple-element.28), channel_id=1, source_target_pairs={{0,504},{8,0},{16,8},{24,16},{32,24},{40,32},{48,40},{56,48},{64,5... | collective-permute-start | bytes 786440 | tf_op jit(solution)/shard_map/ppermute | solution.py:220
  46.5 22.4 %all-to-all-start.1 = ((bf16[16,24,128]{2,1,0:T(8,128)(2,1)}), bf16[16,24,128]{2,1,0:T(8,128)(2,1)S(1)}, u32[]{:S(2)}, u32[]{:S(2)}) async-start(bf16[16,24,128]{2,1,0:T(8,128)(2,1)} %broadcast_in_dim.24), calls=%async_computation.1 | async-start | bytes 196608 | tf_op jit(solution)/shard_map/all_to_all | solution.py:312
  57.4 17.5 %collective-permute-start.5 = (bf16[512,128]{1,0:T(8,128)(2,1)S(1)}, bf16[512,128]{1,0:T(8,128)(2,1)S(1)}, u32[]{:S(2)}, u32[]{:S(2)}) collective-permute-start(bf16[512,128]{1,0:T(8,128)(2,1)S(1)} %get-tuple-element.29), channel_id=1, source_target_pairs={{0,496},{8,504},{16,0},{24,8},{32,16},{40,24},{48,32},{56,40},{64,... | collective-permute-start | bytes 393224 | tf_op jit(solution)/shard_map/ppermute | solution.py:220
  63.3 14.0 %collective-permute-start.6 = (bf16[512,128]{1,0:T(8,128)(2,1)S(1)}, bf16[512,128]{1,0:T(8,128)(2,1)S(1)}, u32[]{:S(2)}, u32[]{:S(2)}) collective-permute-start(bf16[512,128]{1,0:T(8,128)(2,1)S(1)} %get-tuple-element.30), channel_id=1, source_target_pairs={{8,496},{24,0},{40,16},{56,32},{72,48},{88,64},{104,80},{120,96},{... | collective-permute-start | bytes 393224 | tf_op jit(solution)/shard_map/ppermute | solution.py:220
  69.6 13.2 %all-to-all-start.2 = ((bf16[32,24,128]{2,1,0:T(8,128)(2,1)}), bf16[32,24,128]{2,1,0:T(8,128)(2,1)S(1)}, u32[]{:S(2)}, u32[]{:S(2)}) async-start(bf16[32,24,128]{2,1,0:T(8,128)(2,1)} %broadcast_in_dim.25), calls=%async_computation.2 | async-start | bytes 393216 | tf_op jit(solution)/shard_map/all_to_all | solution.py:312

commit v12 on v11

--- a/solution.py
+++ b/solution.py
@@ -116,7 +116,7 @@
         pl.when(condition)(lambda rest=rest: go(*rest))
 
 
-def short_kernel(aq_ref, sel_ref, one_ref, _, q_ref, g_ref, dq_ref, ad_ref, own_ref, back_ref):
+def short_kernel(aq_ref, sel_ref, one_ref, q_ref, g_ref, dq_ref, ad_ref, own_ref, back_ref):
     short, odd = group_place()
 
     def put_adapter(h, value):
@@ -239,14 +239,14 @@
         return [piece[:, h * WIDTH : (h + 1) * WIDTH] for piece in pieces for h in range(2)]
 
     sel = jnp.concatenate(stacked(short == 0) + [av_t], axis=0)
-    oth = jnp.concatenate(stacked(short == 1), axis=0)
+    oth = jnp.concatenate(stacked(short == 1) + [av_t, av_t], axis=0)
     return sel, oth
 
 
 def attend_short(*operands):
     return pl.pallas_call(
         short_kernel,
-        in_specs=[VMEM] * 6,
+        in_specs=[VMEM] * 5,
         out_specs=[VMEM] * 4,
         out_shape=[
             shape((ROWS, HALF_COLUMNS)),
@@ -331,7 +331,7 @@
     later, _ = lax.optimization_barrier((sel, oth))
     two = passed_along(later, 2)
     three = passed_along(one, 2, range(1, CTX_SIZE, 2))
-    dq_short, ads, own_short, backs = attend_short(aq_t, sel, one, other, q, grad)
+    dq_short, ads, own_short, backs = attend_short(aq_t, sel, one, q, grad)
     dq_long, part, own_long, r1, r2, r3 = attend_long(
         aq_t, sel, oth, one, other, three, two, ads, backs, q, grad
     )

time: 84.2 us -> 84.5 us (level)
  waiting for transfers between devices: 15.2 us -> 16.6 us
  starting transfers between devices: 55.4 us -> 54.4 us
    all_to_all x1, waiting for transfers between devices: 1.42 us -> 2.62 us  [sum_over_all(): lax.all_to_all(part.reshape(size, part.shape[0] // size, WIDTH), NEAR, 0, 0)]
    ppermute x7, starting transfers between devices: 26.9 us -> 25.9 us  [passed_along(): lax.ppermute(block, CTX, [(i, (i + distance) % CTX_SIZE) for i in senders])]
    unnamed x12 -> x19, local copies, waits for them, and re-layouts: 1.27 us -> 1.98 us
where the time goes in v12:
time: 84.5 us; the launch traced here: 83.9 us
  starting transfers between devices  54.4 us (64%)
  waiting for transfers between devices  16.6 us (20%)
  Pallas kernels  7.61 us (9%)
  local copies, waits for them, and re-layouts  3.35 us (4%)
  other arithmetic  1.1 us (1%)
  between operations  0.88 us (1%)
    ppermute x7, starting transfers between devices, passed_along(): lax.ppermute(block, CTX, [(i, (i + distance) % CTX_SIZE) for i in senders])  25.9 us
    all_to_all x2, starting transfers between devices, copies_to_all(): lax.all_to_all(jnp.broadcast_to(block[None], (size,) + block.shape), axes...  16.1 us
    all_to_all x1, starting transfers between devices, sum_over_all(): lax.all_to_all(part.reshape(size, part.shape[0] // size, WIDTH), NEAR, 0, 0)  12.4 us
    all_to_all x2, waiting for transfers between devices, copies_to_all(): lax.all_to_all(jnp.broadcast_to(block[None], (size,) + block.shape), axes...  8.15 us
    ppermute x7, waiting for transfers between devices, passed_along(): lax.ppermute(block, CTX, [(i, (i + distance) % CTX_SIZE) for i in senders])  5.84 us
    pallas_call x1, Pallas kernels, attend_long(): pl.pallas_call(long_kernel, in_specs=[VMEM] * 11, out_specs=[VMEM] * 6, o...  3.86 us
    all_to_all x1, waiting for transfers between devices, sum_over_all(): lax.all_to_all(part.reshape(size, part.shape[0] // size, WIDTH), NEAR, 0, 0)  2.62 us
    unnamed x19, local copies, waits for them, and re-layouts  1.98 us
  transfers between devices with their start and end apart: 10, of which 5 were waited for; matrix products, arithmetic and copies ran while one was open for 2% of the time, Pallas kernels for 4%

profile of v12, /device:TPU:1, one launch (start us, length us, event | category | flops | bytes accessed | tf_op | source)
XLA Modules:
  0.0 83.9 jit_solution(3582394054950788723)
XLA Ops:
  0.6 0.0 copy-start
  0.7 1.0 %broadcast_select_fusion = (bf16[128,256]{1,0:T(8,128)(2,1)S(1)}, bf16[128,256]{1,0:T(8,128)(2,1)S(1)}, bf16[128,256]{1,0:T(8,128)(2,1)S(1)}, bf16[128,256]{1,0:T(8,128)(2,1)S(1)}) fusion(pred[]{:T(512)S(6)} %eq.9, bf16[128,512]{1,0:T(8,128)(2,1)} %bitcast.25, pred[]{:T(512)S(6)} %eq.8, bf16[128,512]{1,0:T(8,128)(2,1)} %bitcast.26), kind=kLoop, calls=%fused_computation | loop fusion | flops 131072 | bytes 524290 | tf_op jit(solution)/shard_map/jit(_where)/select_n | solution.py:235
  1.8 0.0 copy-start.4
  1.9 0.7 copy-done.4
  2.5 4.2 %collective-permute-start = (bf16[528,128]{1,0:T(8,128)(2,1)S(1)}, bf16[528,128]{1,0:T(8,128)(2,1)S(1)}, u32[]{:S(2)}, u32[]{:S(2)}) collective-permute-start(bf16[528,128]{1,0:T(8,128)(2,1)S(1)} %get-tuple-element.22.sel_ref), channel_id=1, source_target_pairs={{0,8},{8,16},{16,24},{24,32},{32,40},{40,48},{48,56},{56,64},{64,7... | collective-permute-start | bytes 405512 | tf_op jit(solution)/shard_map/ppermute | solution.py:220
  6.7 3.2 %collective-permute-start.1 = (bf16[544,128]{1,0:T(8,128)(2,1)S(1)}, bf16[544,128]{1,0:T(8,128)(2,1)S(1)}, u32[]{:S(2)}, u32[]{:S(2)}) collective-permute-start(bf16[544,128]{1,0:T(8,128)(2,1)S(1)} %get-tuple-element.41.oth_ref), channel_id=1, source_target_pairs={{0,8},{16,24},{32,40},{48,56},{64,72},{80,88},{96,104},{112,120},{... | collective-permute-start | bytes 417800 | tf_op jit(solution)/shard_map/ppermute | solution.py:220
  9.9 5.4 %collective-permute-start.3 = (bf16[528,128]{1,0:T(8,128)(2,1)S(1)}, bf16[528,128]{1,0:T(8,128)(2,1)S(1)}, u32[]{:S(2)}, u32[]{:S(2)}) collective-permute-start(bf16[528,128]{1,0:T(8,128)(2,1)S(1)} %get-tuple-element.22.sel_ref), channel_id=1, source_target_pairs={{0,16},{8,24},{16,32},{24,40},{32,48},{40,56},{48,64},{56,72},{64,... | collective-permute-start | bytes 405512 | tf_op jit(solution)/shard_map/ppermute | solution.py:220
  15.4 0.0 collective-permute-done.one_ref
  15.4 0.7 collective-permute-start.2
  16.1 0.0 copy-start.1
  16.1 1.2 %copy-done.1 = bf16[1,128,4096]{2,1,0:T(8,128)(2,1)S(1)} copy-done((bf16[1,128,4096]{2,1,0:T(8,128)(2,1)S(1)}, bf16[1,128,4096]{2,1,0:T(8,128)(2,1)}, u32[]{:S(2)}) %copy-start.1) | copy-done | bytes 1048600
  17.3 1.3 %short.1 = (bf16[128,2048]{1,0:T(8,128)(2,1)S(1)}, bf16[288,128]{1,0:T(8,128)(2,1)S(1)}, bf16[512,128]{1,0:T(8,128)(2,1)S(1)}, bf16[512,128]{1,0:T(8,128)(2,1)S(1)}) custom-call(bf16[16,128]{1,0:T(8,128)(2,1)S(1)} %bitcast.23, bf16[528,128]{1,0:T(8,128)(2,1)S(1)} %get-tuple-element.22.sel_ref, bf16[528,128]{1,0:T(8,128)(2,1)S(1)} %collective-permute-done.one_ref, ...), custom_call_target="tpu_custom_call" | custom-call | flops 700000000 | bytes 3000000 | tf_op jit(solution)/shard_map/short/pallas_call | solution.py:247
  18.6 3.4 %collective-permute-done.3.two_ref = bf16[528,128]{1,0:T(8,128)(2,1)S(1)} collective-permute-done((bf16[528,128]{1,0:T(8,128)(2,1)S(1)}, bf16[528,128]{1,0:T(8,128)(2,1)S(1)}, u32[]{:S(2)}, u32[]{:S(2)}) %collective-permute-start.3) | collective-permute-done | bytes 135200 | tf_op jit(solution)/shard_map/ppermute | solution.py:220
  22.1 0.0 collective-permute-done.1.other_ref
  22.1 0.0 collective-permute-done.2.three_ref
  22.1 3.9 %long.1 = (bf16[128,2048]{1,0:T(8,128)(2,1)S(1)}, bf16[768,128]{1,0:T(8,128)(2,1)}, bf16[512,128]{1,0:T(8,128)(2,1)S(1)}, bf16[1024,128]{1,0:T(8,128)(2,1)S(1)},...) custom-call(bf16[16,128]{1,0:T(8,128)(2,1)S(1)} %bitcast.24, bf16[528,128]{1,0:T(8,128)(2,1)S(1)} %get-tuple-element.22.sel_ref, ...), custom_call_target="tpu_custom_call" | custom-call | flops 1400000000 | bytes 4000000 | tf_op jit(solution)/shard_map/long/pallas_call | solution.py:264
  25.9 12.4 %all-to-all-start = ((bf16[32,24,128]{2,1,0:T(8,128)(2,1)}), bf16[32,24,128]{2,1,0:T(8,128)(2,1)S(1)}, u32[]{:S(2)}, u32[]{:S(2)}) async-start(bf16[32,24,128]{2,1,0:T(8,128)(2,1)} %bitcast.13), calls=%async_computation | async-start | bytes 393216 | tf_op jit(solution)/shard_map/all_to_all | solution.py:321
  38.3 5.2 %collective-permute-start.4 = (bf16[1024,128]{1,0:T(8,128)(2,1)S(1)}, bf16[1024,128]{1,0:T(8,128)(2,1)S(1)}, u32[]{:S(2)}, u32[]{:S(2)}) collective-permute-start(bf16[1024,128]{1,0:T(8,128)(2,1)S(1)} %get-tuple-element.28), channel_id=1, source_target_pairs={{0,504},{8,0},{16,8},{24,16},{32,24},{40,32},{48,40},{56,48},{64,5... | collective-permute-start | bytes 786440 | tf_op jit(solution)/shard_map/ppermute | solution.py:220
  43.6 2.6 %all-to-all-done = bf16[32,24,128]{2,1,0:T(8,128)(2,1)S(1)} async-done(((bf16[32,24,128]{2,1,0:T(8,128)(2,1)}), bf16[32,24,128]{2,1,0:T(8,128)(2,1)S(1)}, u32[]{:S(2)}, u32[]{:S(2)}) %all-to-all-start) | async-done | bytes 196640 | tf_op jit(solution)/shard_map/all_to_all | solution.py:321
  46.2 0.7 broadcast_in_dim.24
  46.9 10.8 %all-to-all-start.1 = ((bf16[16,24,128]{2,1,0:T(8,128)(2,1)}), bf16[16,24,128]{2,1,0:T(8,128)(2,1)S(1)}, u32[]{:S(2)}, u32[]{:S(2)}) async-start(bf16[16,24,128]{2,1,0:T(8,128)(2,1)} %broadcast_in_dim.24), calls=%async_computation.1 | async-start | bytes 196608 | tf_op jit(solution)/shard_map/all_to_all | solution.py:312
  57.7 5.9 %collective-permute-start.5 = (bf16[512,128]{1,0:T(8,128)(2,1)S(1)}, bf16[512,128]{1,0:T(8,128)(2,1)S(1)}, u32[]{:S(2)}, u32[]{:S(2)}) collective-permute-start(bf16[512,128]{1,0:T(8,128)(2,1)S(1)} %get-tuple-element.29), channel_id=1, source_target_pairs={{0,496},{8,504},{16,0},{24,8},{32,16},{40,24},{48,32},{56,40},{64,... | collective-permute-start | bytes 393224 | tf_op jit(solution)/shard_map/ppermute | solution.py:220
  63.6 1.3 %collective-permute-start.6 = (bf16[512,128]{1,0:T(8,128)(2,1)S(1)}, bf16[512,128]{1,0:T(8,128)(2,1)S(1)}, u32[]{:S(2)}, u32[]{:S(2)}) collective-permute-start(bf16[512,128]{1,0:T(8,128)(2,1)S(1)} %get-tuple-element.30), channel_id=1, source_target_pairs={{8,496},{24,0},{40,16},{56,32},{72,48},{88,64},{104,80},{120,96},{... | collective-permute-start | bytes 393224 | tf_op jit(solution)/shard_map/ppermute | solution.py:220
  64.9 4.3 %all-to-all-done.1 = bf16[16,24,128]{2,1,0:T(8,128)(2,1)S(1)} async-done(((bf16[16,24,128]{2,1,0:T(8,128)(2,1)}), bf16[16,24,128]{2,1,0:T(8,128)(2,1)S(1)}, u32[]{:S(2)}, u32[]{:S(2)}) %all-to-all-start.1) | async-done | bytes 98336 | tf_op jit(solution)/shard_map/all_to_all | solution.py:312
  69.2 0.7 broadcast_in_dim.25
  69.9 5.3 %all-to-all-start.2 = ((bf16[32,24,128]{2,1,0:T(8,128)(2,1)}), bf16[32,24,128]{2,1,0:T(8,128)(2,1)S(1)}, u32[]{:S(2)}, u32[]{:S(2)}) async-start(bf16[32,24,128]{2,1,0:T(8,128)(2,1)} %broadcast_in_dim.25), calls=%async_computation.2 | async-start | bytes 393216 | tf_op jit(solution)/shard_map/all_to_all | solution.py:312
  75.2 0.0 collective-permute-done.5.r2_ref
  75.2 2.4 %collective-permute-done.6.r3_ref = bf16[512,128]{1,0:T(8,128)(2,1)S(1)} collective-permute-done((bf16[512,128]{1,0:T(8,128)(2,1)S(1)}, bf16[512,128]{1,0:T(8,128)(2,1)S(1)}, u32[]{:S(2)}, u32[]{:S(2)}) %collective-permute-start.6) | collective-permute-done | bytes 131104 | tf_op jit(solution)/shard_map/ppermute | solution.py:220
  77.6 0.0 collective-permute-done.4.r1_ref
  77.6 1.7 %gradients_out.1 = (bf16[128,4096]{1,0:T(8,128)(2,1)}, bf16[128,512]{1,0:T(8,128)(2,1)}, bf16[128,512]{1,0:T(8,128)(2,1)}) custom-call(bf16[128,2048]{1,0:T(8,128)(2,1)S(1)} %get-tuple-element.21.dq_short_ref, bf16[128,2048]{1,0:T(8,128)(2,1)S(1)} %get-tuple-element.25.dq_long_ref, bf16[512,128]{1,0:T(8,128)(2,1)S(1)} %get-tuple-element.26.short_ref, ...), custom_call_target="tpu_custom_call" | custom-call | flops 20000000000 | bytes 2000000 | tf_op jit(solution)/shard_map/gradients_out/pallas_call | solution.py:284
  79.4 3.8 %all-to-all-done.2 = bf16[32,24,128]{2,1,0:T(8,128)(2,1)S(1)} async-done(((bf16[32,24,128]{2,1,0:T(8,128)(2,1)}), bf16[32,24,128]{2,1,0:T(8,128)(2,1)S(1)}, u32[]{:S(2)}, u32[]{:S(2)}) %all-to-all-start.2) | async-done | bytes 196640 | tf_op jit(solution)/shard_map/all_to_all | solution.py:312
  83.2 0.7 adapter_out.1
  (17 shorter events, 0.2 us)
Async XLA Ops:
  0.6 15.4 %copy-start = (bf16[1,128,4096]{2,1,0:T(8,128)(2,1)S(1)}, bf16[1,128,4096]{2,1,0:T(8,128)(2,1)}, u32[]{:S(2)}) copy-start(bf16[1,128,4096]{2,1,0:T(8,128)(2,1)} %param.6) | copy-start | bytes 3145732
  1.8 0.7 copy-start.4
  2.5 13.5 %copy-start.3 = (bf16[1,128,16]{1,2,0:T(8,128)(2,1)S(1)}, bf16[1,128,16]{1,2,0:T(8,128)(2,1)}, u32[]{:S(2)}) copy-start(bf16[1,128,16]{1,2,0:T(8,128)(2,1)} %param.10) | copy-start | bytes 12292
  2.5 12.8 %collective-permute-start = (bf16[528,128]{1,0:T(8,128)(2,1)S(1)}, bf16[528,128]{1,0:T(8,128)(2,1)S(1)}, u32[]{:S(2)}, u32[]{:S(2)}) collective-permute-start(bf16[528,128]{1,0:T(8,128)(2,1)S(1)} %get-tuple-element.22.sel_ref), channel_id=1, source_target_pairs={{0,8},{8,16},{16,24},{24,32},{32,40},{40,48},{48,56},{56,64},{64,7... | collective-permute-start | bytes 405512 | tf_op jit(solution)/shard_map/ppermute | solution.py:220
  6.7 15.4 %collective-permute-start.1 = (bf16[544,128]{1,0:T(8,128)(2,1)S(1)}, bf16[544,128]{1,0:T(8,128)(2,1)S(1)}, u32[]{:S(2)}, u32[]{:S(2)}) collective-permute-start(bf16[544,128]{1,0:T(8,128)(2,1)S(1)} %get-tuple-element.41.oth_ref), channel_id=1, source_target_pairs={{0,8},{16,24},{32,40},{48,56},{64,72},{80,88},{96,104},{112,120},{... | collective-permute-start | bytes 417800 | tf_op jit(solution)/shard_map/ppermute | solution.py:220
  9.9 12.1 %collective-permute-start.3 = (bf16[528,128]{1,0:T(8,128)(2,1)S(1)}, bf16[528,128]{1,0:T(8,128)(2,1)S(1)}, u32[]{:S(2)}, u32[]{:S(2)}) collective-permute-start(bf16[528,128]{1,0:T(8,128)(2,1)S(1)} %get-tuple-element.22.sel_ref), channel_id=1, source_target_pairs={{0,16},{8,24},{16,32},{24,40},{32,48},{40,56},{48,64},{56,72},{64,... | collective-permute-start | bytes 405512 | tf_op jit(solution)/shard_map/ppermute | solution.py:220
  15.4 6.7 %collective-permute-start.2 = (bf16[528,128]{1,0:T(8,128)(2,1)S(1)}, bf16[528,128]{1,0:T(8,128)(2,1)S(1)}, u32[]{:S(2)}, u32[]{:S(2)}) collective-permute-start(bf16[528,128]{1,0:T(8,128)(2,1)S(1)} %collective-permute-done.one_ref), channel_id=1, source_target_pairs={{8,24},{24,40},{40,56},{56,72},{72,88},{88,104},{104,120},{120,136... | collective-permute-start | bytes 405512 | tf_op jit(solution)/shard_map/ppermute | solution.py:220
  16.1 1.2 %copy-start.1 = (bf16[1,128,4096]{2,1,0:T(8,128)(2,1)S(1)}, bf16[1,128,4096]{2,1,0:T(8,128)(2,1)}, u32[]{:S(2)}) copy-start(bf16[1,128,4096]{2,1,0:T(8,128)(2,1)} %param.9) | copy-start | bytes 3145732
  17.3 4.8 %copy-start.2 = (bf16[1,128,4096]{2,1,0:T(8,128)(2,1)S(1)}, bf16[1,128,4096]{2,1,0:T(8,128)(2,1)}, u32[]{:S(2)}) copy-start(bf16[1,128,4096]{2,1,0:T(8,128)(2,1)} %param.9) | copy-start | bytes 3145732
  25.9 20.3 %all-to-all-start = ((bf16[32,24,128]{2,1,0:T(8,128)(2,1)}), bf16[32,24,128]{2,1,0:T(8,128)(2,1)S(1)}, u32[]{:S(2)}, u32[]{:S(2)}) async-start(bf16[32,24,128]{2,1,0:T(8,128)(2,1)} %bitcast.13), calls=%async_computation | async-start | bytes 393216 | tf_op jit(solution)/shard_map/all_to_all | solution.py:321
  38.3 39.3 %collective-permute-start.4 = (bf16[1024,128]{1,0:T(8,128)(2,1)S(1)}, bf16[1024,128]{1,0:T(8,128)(2,1)S(1)}, u32[]{:S(2)}, u32[]{:S(2)}) collective-permute-start(bf16[1024,128]{1,0:T(8,128)(2,1)S(1)} %get-tuple-element.28), channel_id=1, source_target_pairs={{0,504},{8,0},{16,8},{24,16},{32,24},{40,32},{48,40},{56,48},{64,5... | collective-permute-start | bytes 786440 | tf_op jit(solution)/shard_map/ppermute | solution.py:220
  46.9 22.3 %all-to-all-start.1 = ((bf16[16,24,128]{2,1,0:T(8,128)(2,1)}), bf16[16,24,128]{2,1,0:T(8,128)(2,1)S(1)}, u32[]{:S(2)}, u32[]{:S(2)}) async-start(bf16[16,24,128]{2,1,0:T(8,128)(2,1)} %broadcast_in_dim.24), calls=%async_computation.1 | async-start | bytes 196608 | tf_op jit(solution)/shard_map/all_to_all | solution.py:312
  57.7 17.5 %collective-permute-start.5 = (bf16[512,128]{1,0:T(8,128)(2,1)S(1)}, bf16[512,128]{1,0:T(8,128)(2,1)S(1)}, u32[]{:S(2)}, u32[]{:S(2)}) collective-permute-start(bf16[512,128]{1,0:T(8,128)(2,1)S(1)} %get-tuple-element.29), channel_id=1, source_target_pairs={{0,496},{8,504},{16,0},{24,8},{32,16},{40,24},{48,32},{56,40},{64,... | collective-permute-start | bytes 393224 | tf_op jit(solution)/shard_map/ppermute | solution.py:220
  63.6 14.0 %collective-permute-start.6 = (bf16[512,128]{1,0:T(8,128)(2,1)S(1)}, bf16[512,128]{1,0:T(8,128)(2,1)S(1)}, u32[]{:S(2)}, u32[]{:S(2)}) collective-permute-start(bf16[512,128]{1,0:T(8,128)(2,1)S(1)} %get-tuple-element.30), channel_id=1, source_target_pairs={{8,496},{24,0},{40,16},{56,32},{72,48},{88,64},{104,80},{120,96},{... | collective-permute-start | bytes 393224 | tf_op jit(solution)/shard_map/ppermute | solution.py:220
  69.9 13.2 %all-to-all-start.2 = ((bf16[32,24,128]{2,1,0:T(8,128)(2,1)}), bf16[32,24,128]{2,1,0:T(8,128)(2,1)S(1)}, u32[]{:S(2)}, u32[]{:S(2)}) async-start(bf16[32,24,128]{2,1,0:T(8,128)(2,1)} %broadcast_in_dim.25), calls=%async_computation.2 | async-start | bytes 393216 | tf_op jit(solution)/shard_map/all_to_all | solution.py:312
